TPU v7x, 32 devices: a whole 2x2x4 slice. The times are simulated.
32 devices in a mesh: session: 2 (over y), seq: 4 (over z), tensor: 4 (over x, core).
Axes of the slice: x: 2, y: 2, z: 4, core: 2. Of those that a mesh axis runs over, the one named last changes fastest.
Arguments:
- queries: bfloat16 [1536, 3072], P(('session', 'seq'), 'tensor'), parts along dimension 0, may hold values from -210 to 210
- new_keys: bfloat16 [1536, 3072], P(('session', 'seq'), 'tensor'), parts along dimension 0, may hold values from -5 to 5
- new_values: bfloat16 [1536, 3072], P(('session', 'seq'), 'tensor'), parts along dimension 0, may hold values from -6 to 6
- context_queries: bfloat16 [1024, 3072], P(('session', 'seq'), 'tensor'), parts along dimension 0, may hold values from -6 to 6
- context_keys: bfloat16 [1024, 3072], P(('session', 'seq'), 'tensor'), parts along dimension 0, may hold values from -6 to 6
- context_values: bfloat16 [1024, 3072], P(('session', 'seq'), 'tensor'), parts along dimension 0, may hold values from -6 to 6
- levels: int32 [16], P('session'), parts along dimension 0, may hold values from 0 to 1
- frame_mask: int32 [4, 8], P('session'), parts along dimension 0, may hold values 0 or 1
- owners: int32 [256], P('session'), parts along dimension 0, may hold values from 0 to 3, as said below
- out_weight: bfloat16 [3072, 3072], P('tensor'), may hold values from -0.15625 to 0.15625
Outputs:
- block_out: bfloat16 [1536, 3072], P(('session', 'seq'), 'tensor'), parts along dimension 0
- context_out: bfloat16 [1024, 3072], P(('session', 'seq'), 'tensor'), parts along dimension 0
- cache_keys: bfloat16 [1024, 3072], P(('session', 'seq'), 'tensor'), parts along dimension 0
- cache_values: bfloat16 [1024, 3072], P(('session', 'seq'), 'tensor'), parts along dimension 0
There are 2 independent parts, one for each index of `session`. A program takes and returns all parts, laid end to end along the dimension named above; an argument that names none is the same for every part. Nothing has to cross between parts.
Inputs may be any that keep to these rules, and one draw needn't show every extreme that they name: `owners`: every seq index owns exactly 32 blocks; a seq index gives either none or exactly 16 of its own blocks to each owner, and the owner minus the giver, modulo the number of seq indices, takes the same 32 // 16 values for every giver.
All inputs are finite; a program needn't handle non-finite values.
Results may differ from a plain program's by a relative error of at most 0.014.
Values may be sent and summed in bfloat16 or wider, within the bound.
No kernel may reach another device: no remote copies, remote signals or barrier semaphores. Data moves between devices by JAX's collectives and lax.ppermute only.
A program may use at most 64 MiB of HBM per device.

v0:
```python
import math

import jax
import jax.numpy as jnp
from jax import lax
from jax.sharding import PartitionSpec as P

HEAD_DIM = 128


NEGATIVE = -1e30


def lookup(table, index):
    hits = index[..., None] == jnp.arange(table.shape[0], dtype=jnp.int32)
    return jnp.sum(jnp.where(hits, table, 0), axis=-1)


def pool_blocks(rows, coarse):
    blocks = rows.reshape(-1, 4, rows.shape[-1])
    mean = jnp.mean(blocks.astype(jnp.float32), axis=1).astype(jnp.bfloat16)
    first = (jnp.arange(4) == 0)[None, :, None]
    pooled = jnp.where(first, mean[:, None, :], jnp.zeros_like(blocks))
    return jnp.where(coarse[:, None, None], pooled, blocks)


def group_plan(total_rows, shard_rows):
    shards = total_rows // shard_rows
    group = math.gcd(shards, max(1, 1024 // shard_rows))
    return (shards // group, group)


def attend(state, heads_q, keys, values, allowed, scale):
    best, total, accum = state
    count = keys.shape[0]
    heads = heads_q.shape[0]
    hdim = heads_q.shape[2]
    keys_h = keys.reshape(count, heads, hdim)
    values_h = values.reshape(count, heads, hdim)
    scores = jnp.einsum("hqd,khd->hqk", heads_q, keys_h, preferred_element_type=jnp.float32) * scale
    if allowed is not None:
        scores = jnp.where(allowed[None], scores, NEGATIVE)
    fresh = jnp.maximum(best, jnp.max(scores, axis=2))
    weights = jnp.exp(scores - fresh[..., None])
    if allowed is not None:
        weights = jnp.where(allowed[None], weights, 0.0)
    decay = jnp.exp(best - fresh)
    total = total * decay + jnp.sum(weights, axis=2)
    accum = accum * decay[..., None] + jnp.einsum(
        "hqk,khd->hqd", weights.astype(jnp.bfloat16), values_h, preferred_element_type=jnp.float32
    )
    return (fresh, total, accum)


def per_device(
    queries,
    new_keys,
    new_values,
    context_queries,
    context_keys,
    context_values,
    levels,
    frame_mask,
    owners,
    out_weight,
):
    width = queries.shape[1]
    new_rows = queries.shape[0]
    ctx_rows = context_keys.shape[0]
    blocks_dev = ctx_rows // 4
    devices = lax.axis_size("seq")
    place = lax.axis_index("seq")
    blocks_all = blocks_dev * devices
    frames_ctx = levels.shape[0]
    frames_new = frame_mask.shape[0]
    new_all = new_rows * devices
    hdim = HEAD_DIM
    heads = width // hdim
    scale = 1.0 / math.sqrt(hdim)
    pair = max(2, 2 * blocks_dev // devices)
    block_ids = jnp.arange(blocks_all, dtype=jnp.int32)
    block_frame = block_ids * frames_ctx // blocks_all
    coarse_all = lookup(levels, block_frame) == 1
    mine = owners == place
    rank = jnp.cumsum(mine.astype(jnp.int32)) - 1
    own_coarse = lax.dynamic_slice_in_dim(coarse_all, place * blocks_dev, blocks_dev)
    pooled_q = pool_blocks(context_queries, own_coarse)
    pooled_k = pool_blocks(context_keys, own_coarse)
    pooled_v = pool_blocks(context_values, own_coarse)
    slots = jnp.arange(blocks_dev, dtype=jnp.int32)[:, None] == rank[None, :]
    held_coarse = jnp.any(slots & mine[None, :] & coarse_all[None, :], axis=1)
    held_live = jnp.logical_or(
        jnp.logical_not(held_coarse)[:, None], (jnp.arange(4) == 0)[None, :]
    ).reshape(ctx_rows)
    my_owners = lax.dynamic_slice_in_dim(owners, place * blocks_dev, blocks_dev)
    hits = my_owners[:, None] == jnp.arange(devices, dtype=jnp.int32)[None, :]
    within = jnp.sum(jnp.where(hits, jnp.cumsum(hits.astype(jnp.int32), axis=0) - 1, 0), axis=1)
    send_slot = my_owners * pair + within

    def pack(blocks):
        buffer = jnp.zeros((devices * pair, 4, width), blocks.dtype).at[send_slot].set(blocks)
        return buffer.reshape(devices, pair * 4, width)

    counts = jnp.sum((owners.reshape(devices, blocks_dev) == place).astype(jnp.int32), axis=1)
    before = jnp.cumsum(counts) - counts
    order_in = jnp.arange(pair, dtype=jnp.int32)[None, :]
    target = jnp.where(order_in < counts[:, None], before[:, None] + order_in, blocks_dev).reshape(
        -1
    )

    def unpack(arrived):
        blocks = arrived.reshape(devices * pair, 4, width)
        return jnp.zeros((blocks_dev, 4, width), arrived.dtype).at[target].set(blocks, mode="drop")

    arrived = (
        lax.all_to_all(pack(pooled_q), "seq", split_axis=0, concat_axis=0, tiled=True),
        lax.all_to_all(pack(pooled_k), "seq", split_axis=0, concat_axis=0, tiled=True),
        lax.all_to_all(pack(pooled_v), "seq", split_axis=0, concat_axis=0, tiled=True),
    )
    held_q = unpack(arrived[0])
    held_k = unpack(arrived[1])
    held_v = unpack(arrived[2])
    all_q = jnp.concatenate([queries, held_q.reshape(ctx_rows, width)], axis=0)
    rows_q = all_q.shape[0]
    heads_q = all_q.reshape(rows_q, heads, hdim).transpose(1, 0, 2)
    q_global = place * new_rows + jnp.arange(new_rows, dtype=jnp.int32)
    q_frame = q_global * frames_new // new_all
    frame_hits = (q_frame[:, None] == jnp.arange(frames_new, dtype=jnp.int32)[None, :])[:, :, None]
    new_mask = jnp.sum(jnp.where(frame_hits, frame_mask[None], 0), axis=1)
    query_mask = jnp.concatenate(
        [new_mask, jnp.ones((ctx_rows, frames_ctx), jnp.int32)], axis=0
    ).astype(jnp.float32)

    def context_allowed(first_shard, count_rows):
        index = first_shard * ctx_rows + jnp.arange(count_rows, dtype=jnp.int32)
        frame = index // 4 * frames_ctx // blocks_all
        coarse = lookup(levels, frame) == 1
        live = jnp.logical_or(jnp.logical_not(coarse), index % 4 == 0)
        onehot = (frame[:, None] == jnp.arange(frames_ctx, dtype=jnp.int32)[None, :]).astype(
            jnp.float32
        )
        reach = jnp.dot(query_mask, onehot.T) > 0.5
        return jnp.logical_and(reach, live[None, :])

    def take_new(state, keys, values):
        return attend(state, heads_q, keys, values, None, scale)

    def take_context(state, keys, values, first_shard):
        allowed = context_allowed(first_shard, keys.shape[0])
        return attend(state, heads_q, keys, values, allowed, scale)

    start_state = (
        jnp.full((heads, rows_q), NEGATIVE, jnp.float32),
        jnp.zeros((heads, rows_q), jnp.float32),
        jnp.zeros((heads, rows_q, hdim), jnp.float32),
    )
    empty_cache = (
        jnp.zeros((blocks_dev, 4, width), jnp.bfloat16),
        jnp.zeros((blocks_dev, 4, width), jnp.bfloat16),
    )
    flat_k = pooled_k.reshape(ctx_rows, width)
    flat_v = pooled_v.reshape(ctx_rows, width)
    piece = (
        lax.all_gather(new_keys, "seq", axis=0, tiled=True),
        lax.all_gather(new_values, "seq", axis=0, tiled=True),
    )
    steps, group = group_plan(piece[0].shape[0], new_rows)
    size = group * new_rows
    stacked = (piece[0].reshape(steps, size, width), piece[1].reshape(steps, size, width))

    def one(carry, item):
        return (take_new(carry, item[0], item[1]), None)

    state = lax.scan(one, start_state, stacked)[0]
    piece = (
        lax.all_gather(flat_k, "seq", axis=0, tiled=True),
        lax.all_gather(flat_v, "seq", axis=0, tiled=True),
    )
    steps, group = group_plan(piece[0].shape[0], ctx_rows)
    size = group * ctx_rows
    firsts = jnp.arange(steps, dtype=jnp.int32) * group
    stacked = (piece[0].reshape(steps, size, width), piece[1].reshape(steps, size, width), firsts)

    def one(inner, item):
        keys, values, first = item
        attended = take_context(inner[0], keys, values, first)
        cache = inner[1]
        return ((attended, cache), None)

    state, cache = lax.scan(one, (state, empty_cache), stacked)[0]
    best, total, accum = state
    mixed = (accum / total[..., None]).transpose(1, 0, 2).reshape(rows_q, width)
    live_rows = jnp.concatenate([jnp.ones((new_rows,), dtype=bool), held_live], axis=0)
    mixed = jnp.where(live_rows[:, None], mixed, 0.0).astype(jnp.bfloat16)
    summed = lax.psum_scatter(
        lax.dot_general(
            out_weight, mixed, (((0,), (1,)), ((), ())), preferred_element_type=jnp.float32
        ).astype(jnp.bfloat16),
        "tensor",
        scatter_dimension=0,
        tiled=True,
    ).astype(jnp.float32)
    result = summed.T.astype(jnp.bfloat16)
    return (
        result[:new_rows],
        result[new_rows:],
        held_k.reshape(ctx_rows, width),
        held_v.reshape(ctx_rows, width),
    )


def solution(mesh):
    in_specs = (
        P(("session", "seq"), "tensor"),
        P(("session", "seq"), "tensor"),
        P(("session", "seq"), "tensor"),
        P(("session", "seq"), "tensor"),
        P(("session", "seq"), "tensor"),
        P(("session", "seq"), "tensor"),
        P("session"),
        P("session", None),
        P("session"),
        P("tensor", None),
    )
    out_specs = (
        P(("session", "seq"), "tensor"),
        P(("session", "seq"), "tensor"),
        P(("session", "seq"), "tensor"),
        P(("session", "seq"), "tensor"),
    )
    return jax.shard_map(
        per_device, mesh=mesh, in_specs=in_specs, out_specs=out_specs, check_vma=False
    )
```

profile of v0, /device:TPU:0, one launch (start us, length us, event | category | flops | bytes accessed | tf_op | source)
XLA Modules:
  0.0 170.4 jit_solution(9977035083352543394)
XLA Ops:
  7.2 0.7 all-gather.3.cloned.1.call-update
  8.0 0.7 dynamic_slice.21
  8.7 0.7 select_reduce_fusion.3
  9.4 0.7 convert_bitcast_fusion
  10.3 1.0 reshape.342
  11.3 1.0 reshape.346
  12.3 1.0 reshape.348
  13.5 0.3 convert_reduce_fusion.2
  14.3 0.7 compare_select_fusion
  15.1 1.1 select_select_fusion
  16.3 1.5 scatter_fusion
  17.9 0.8 reshape.343
  18.7 6.3 %all-to-all-start = ((bf16[4,64,768]{2,1,0:T(8,128)(2,1)}), bf16[4,64,768]{2,1,0:T(8,128)(2,1)S(1)}, u32[]{:S(2)}, u32[]{:S(2)}) async-start(bf16[4,64,768]{2,1,0:T(8,128)(2,1)} %reshape.343), calls=%async_computation | async-start | bytes 786432 | tf_op jit(solution)/shard_map/all_to_all | solution.py:116
  25.0 0.7 all-gather.5.cloned.1.call-update
  27.6 36.2 %all_gather.14 = bf16[512,768]{1,0:T(8,128)(2,1)S(1)} all-gather(bf16[128,768]{1,0:T(8,128)(2,1)S(1)} %get-tuple-element.124), channel_id=1, replica_groups=mesh['session'=2,'seq'=4,'tensor'=4] {'seq'}, dimensions={0}, use_global_device_ids=true | all-gather | bytes 983040 | tf_op jit(solution)/shard_map/all_gather | solution.py:176
  63.8 28.0 %all_gather.15 = bf16[512,768]{1,0:T(8,128)(2,1)S(1)} all-gather(bf16[128,768]{1,0:T(8,128)(2,1)S(1)} %get-tuple-element.125), channel_id=1, replica_groups=mesh['session'=2,'seq'=4,'tensor'=4] {'seq'}, dimensions={0}, use_global_device_ids=true | all-gather | bytes 983040 | tf_op jit(solution)/shard_map/all_gather | solution.py:177
  92.2 1.2 copy.42
  93.3 1.2 copy.44
  94.7 1.0 fusion.22
  95.9 2.6 %scatter_fusion.1 = bf16[32,4,768]{2,1,0:T(4,128)(2,1)S(1)} fusion(bf16[32,4,768]{2,1,0:T(4,128)(2,1)S(1)} %broadcast.324.clone, s32[64]{0:T(128)S(1)} %fusion.44, bf16[64,4,768]{2,1,0:T(4,128)(2,1)S(1)} %reshape.371), kind=kCustom, calls=%fused_computation.1 | custom fusion | bytes 1179904 | tf_op jit(solution)/shard_map/scatter | solution.py:113
  98.7 3.6 %fusion.12 = (f32[6,320]{1,0:T(8,128)S(1)}, f32[6,320,512]{2,1,0:T(8,128)}) fusion(pred[320,512]{1,0:T(8,128)(4,1)} %fusion.22, bf16[512,6,128]{0,2,1:T(8,128)(2,1)S(1)} %bitcast.62, bf16[128,6,128]{2,0,1:T(8,128)(2,1)S(1)} %copy.41, bf16[192,6,128]{2,0,1:T(8,128)(2,1)S(1)} %copy_bitcast_fusion), kind=kOutput, calls=%fused_computation.29 | convolution fusion | flops 255588480 | bytes 5381632 | tf_op jit(solution)/shard_map/while/body/eval_jaxpr/hqd,khd->hqk/dot_general | solution.py:40
  102.3 14.3 %while.3 = (s32[]{:T(128)}, f32[6,320]{1,0:T(8,128)S(1)}, f32[6,320]{1,0:T(8,128)S(1)}, f32[6,320,128]{2,1,0:T(8,128)S(1)}, bf16[4,192,768]{2,1,0:T(8,128)(2,1)}...) while((s32[]{:T(128)}, f32[6,320]{1,0:T(8,128)S(1)}, ...), condition=%wide.region_13.14_spmd.clone, body=%wide.region_10.13_spmd.clone.sunk | while | flops 192439680 | bytes 9953397 | solution.py:174
  102.3 1.1 constant_dynamic-slice_fusion.3
  103.4 0.3 reshape.415
  103.8 0.3 reshape.416
  104.1 0.4 bitcast_reduce_fusion.2
  104.6 0.3 fusion.64
  104.9 0.9 convolution_add_fusion.2
  105.9 1.1 constant_dynamic-slice_fusion.3
  107.0 0.3 reshape.415
  107.4 0.3 reshape.416
  107.7 0.4 bitcast_reduce_fusion.2
  108.2 0.3 fusion.64
  108.5 0.9 convolution_add_fusion.2
  109.5 1.1 constant_dynamic-slice_fusion.3
  110.6 0.3 reshape.415
  110.9 0.3 reshape.416
  111.3 0.4 bitcast_reduce_fusion.2
  111.7 0.3 fusion.64
  112.1 0.9 convolution_add_fusion.2
  113.0 1.1 constant_dynamic-slice_fusion.3
  114.1 0.3 reshape.415
  114.5 0.3 reshape.416
  114.9 0.4 bitcast_reduce_fusion.2
  115.3 0.3 fusion.64
  115.6 0.9 convolution_add_fusion.2
  116.6 3.6 %fusion.13 = f32[6,320]{1,0:T(8,128)S(1)} fusion(f32[6,320,512]{2,1,0:T(8,128)} %get-tuple-element.127, f32[6,320]{1,0:T(8,128)S(1)} %max.7, pred[320,512]{1,0:T(8,128)(4,1)S(1)} %copy-done.6), kind=kLoop, calls=%fused_computation.30 | loop fusion | flops 4913280 | bytes 4111360 | tf_op jit(solution)/shard_map/while/body/eval_jaxpr/reduce_sum | solution.py:48
  120.3 3.1 %divide_bitcast_fusion = bf16[320,6,128]{2,0,1:T(8,128)(2,1)S(1)} fusion(bf16[512,6,128]{0,2,1:T(8,128)(2,1)} %bitcast.61, f32[6,320,512]{2,1,0:T(8,128)S(1)} %copy-done.1, f32[6,320]{1,0:T(8,128)S(1)} %max.7, pred[320,512]{1,0:T(8,128)(4,1)S(1)} %copy-done.6, f32[6,320,128]{2,1,0:T(8,128)S(1)} %get-tuple-element.70, f32[6,320]{1,0:T(8,128)S(1)} %get-tuple-element.115, ...), kind=kOutput, calls=%fused_computation.39 | convolution fusion | flops 257556480 | bytes 6380032 | tf_op jit(solution)/shard_map/while/body/eval_jaxpr/hqk,khd->hqd/dot_general | solution.py:49
  123.3 0.3 copy.46
  123.8 5.4 %fusion.11 = bf16[3072,320]{0,1:T(8,128)(2,1)} fusion(bf16[320,768]{0,1:T(8,128)(2,1)S(1)} %fusion.21, bf16[768,3072]{1,0:T(8,128)(2,1)} %param.21), kind=kOutput, calls=%fused_computation.28 | convolution fusion | flops 1510932480 | bytes 7176192 | tf_op jit(solution)/shard_map/dot_general | solution.py:196
  129.4 1.5 scatter_fusion.2
  130.9 0.8 reshape.351
  131.7 4.1 %all-to-all-start.1 = ((bf16[4,64,768]{2,1,0:T(8,128)(2,1)}), bf16[4,64,768]{2,1,0:T(8,128)(2,1)S(1)}, u32[]{:S(2)}, u32[]{:S(2)}) async-start(bf16[4,64,768]{2,1,0:T(8,128)(2,1)} %reshape.351), calls=%async_computation.2 | async-start | bytes 786432 | tf_op jit(solution)/shard_map/all_to_all | solution.py:117
  136.0 1.5 scatter_fusion.4
  137.5 0.9 reshape.354
  138.4 6.4 %all-to-all-done.1 = bf16[4,64,768]{2,1,0:T(8,128)(2,1)S(1)} async-done(((bf16[4,64,768]{2,1,0:T(8,128)(2,1)}), bf16[4,64,768]{2,1,0:T(8,128)(2,1)S(1)}, u32[]{:S(2)}, u32[]{:S(2)}) %all-to-all-start.1) | async-done | bytes 393248 | tf_op jit(solution)/shard_map/all_to_all | solution.py:117
  144.7 3.5 %all-to-all-start.2 = ((bf16[4,64,768]{2,1,0:T(8,128)(2,1)}), bf16[4,64,768]{2,1,0:T(8,128)(2,1)S(1)}, u32[]{:S(2)}, u32[]{:S(2)}) async-start(bf16[4,64,768]{2,1,0:T(8,128)(2,1)} %reshape.354), calls=%async_computation.3 | async-start | bytes 786432 | tf_op jit(solution)/shard_map/all_to_all | solution.py:118
  148.4 2.6 %scatter_fusion.3 = bf16[32,4,768]{2,1,0:T(4,128)(2,1)S(1)} fusion(bf16[32,4,768]{2,1,0:T(4,128)(2,1)S(1)} %broadcast.324.clone.1, s32[64]{0:T(128)S(1)} %fusion.44, bf16[64,4,768]{2,1,0:T(4,128)(2,1)S(1)} %reshape.387), kind=kCustom, calls=%fused_computation.3 | custom fusion | bytes 1179904 | tf_op jit(solution)/shard_map/scatter | solution.py:113
  151.0 0.7 reshape.353
  151.8 5.3 %all-to-all-done.2 = bf16[4,64,768]{2,1,0:T(8,128)(2,1)S(1)} async-done(((bf16[4,64,768]{2,1,0:T(8,128)(2,1)}), bf16[4,64,768]{2,1,0:T(8,128)(2,1)S(1)}, u32[]{:S(2)}, u32[]{:S(2)}) %all-to-all-start.2) | async-done | bytes 393248 | tf_op jit(solution)/shard_map/all_to_all | solution.py:118
  157.2 2.6 %scatter_fusion.5 = bf16[32,4,768]{2,1,0:T(4,128)(2,1)S(1)} fusion(bf16[32,4,768]{2,1,0:T(4,128)(2,1)S(1)} %broadcast.324.clone.2, s32[64]{0:T(128)S(1)} %fusion.44, bf16[64,4,768]{2,1,0:T(4,128)(2,1)S(1)} %reshape.403), kind=kCustom, calls=%fused_computation.5 | custom fusion | bytes 1179904 | tf_op jit(solution)/shard_map/scatter | solution.py:113
  159.9 0.7 reshape.356
  160.6 1.6 slice.9
  162.2 1.7 slice.8
  (99 shorter events, 4.5 us)
Async XLA Ops:
  7.2 88.5 %copy-start = (bf16[192,768]{1,0:T(8,128)(2,1)S(1)}, bf16[192,768]{1,0:T(8,128)(2,1)}, u32[]{:S(2)}) copy-start(bf16[192,768]{1,0:T(8,128)(2,1)} %param.12) | copy-start | bytes 884740
  7.2 19.2 %copy-start.8 = (s32[8]{0:T(128)S(1)}, s32[8]{0:T(128)}, u32[]{:S(2)}) copy-start(s32[8]{0:T(128)} %param.18) | copy-start | bytes 100
  7.2 95.1 %all-gather.3.cloned.1.call-start = ((), (), s32[]{:S(2)}) async-start(), calls=%async_computation.4 | async-start | bytes 1474560 | tf_op jit(solution)/shard_map/all_gather | solution.py:164
  11.3 16.1 %copy-start.3 = (bf16[128,768]{1,0:T(8,128)(2,1)S(1)}, bf16[128,768]{1,0:T(8,128)(2,1)}, u32[]{:S(2)}) copy-start(bf16[128,768]{1,0:T(8,128)(2,1)} %param.16) | copy-start | bytes 589828
  11.3 16.1 %copy-start.4 = (bf16[128,768]{1,0:T(8,128)(2,1)S(1)}, bf16[128,768]{1,0:T(8,128)(2,1)}, u32[]{:S(2)}) copy-start(bf16[128,768]{1,0:T(8,128)(2,1)} %param.17) | copy-start | bytes 589828
  18.7 77.0 %all-to-all-start = ((bf16[4,64,768]{2,1,0:T(8,128)(2,1)}), bf16[4,64,768]{2,1,0:T(8,128)(2,1)S(1)}, u32[]{:S(2)}, u32[]{:S(2)}) async-start(bf16[4,64,768]{2,1,0:T(8,128)(2,1)} %reshape.343), calls=%async_computation | async-start | bytes 786432 | tf_op jit(solution)/shard_map/all_to_all | solution.py:116
  25.0 77.3 %all-gather.5.cloned.1.call-start = ((), (), s32[]{:S(2)}) async-start(), calls=%async_computation.5 | async-start | bytes 1474560 | tf_op jit(solution)/shard_map/all_gather | solution.py:165
  25.7 134.9 %reduce-scatter.2.cloned.1.call-start = ((), (), s32[]{:S(2)}) async-start(), calls=%async_computation.6 | async-start | bytes 2457600 | tf_op jit(solution)/shard_map/reduce_scatter | solution.py:195
  26.8 67.8 %copy-start.7 = (s32[2,8]{1,0:T(2,128)S(1)}, s32[2,8]{1,0:T(2,128)}, u32[]{:S(2)}) copy-start(s32[2,8]{1,0:T(2,128)} %param.19) | copy-start | bytes 196
  94.5 4.2 %copy-start.2 = (bf16[512,768]{0,1:T(8,128)(2,1)S(1)}, bf16[512,768]{0,1:T(8,128)(2,1)}, u32[]{:S(2)}) copy-start(bf16[512,768]{0,1:T(8,128)(2,1)} %copy.42) | copy-start | bytes 2359300
  102.3 14.3 %copy-start.6 = (pred[320,512]{1,0:T(8,128)(4,1)S(1)}, pred[320,512]{1,0:T(8,128)(4,1)}, u32[]{:S(2)}) copy-start(pred[320,512]{1,0:T(8,128)(4,1)} %fusion.22) | copy-start | bytes 491524
  116.6 3.6 %copy-start.1 = (f32[6,320,512]{2,1,0:T(8,128)S(1)}, f32[6,320,512]{2,1,0:T(8,128)}, u32[]{:S(2)}) copy-start(f32[6,320,512]{2,1,0:T(8,128)} %get-tuple-element.127) | copy-start | bytes 11796484
  123.8 5.5 %copy-start.5 = (bf16[32,4,768]{2,1,0:T(4,128)(2,1)S(1)}, bf16[32,4,768]{2,1,0:T(4,128)(2,1)}, u32[]{:S(2)}) copy-start(bf16[32,4,768]{2,1,0:T(4,128)(2,1)} %get-tuple-element.122) | copy-start | bytes 589828
  131.7 13.0 %all-to-all-start.1 = ((bf16[4,64,768]{2,1,0:T(8,128)(2,1)}), bf16[4,64,768]{2,1,0:T(8,128)(2,1)S(1)}, u32[]{:S(2)}, u32[]{:S(2)}) async-start(bf16[4,64,768]{2,1,0:T(8,128)(2,1)} %reshape.351), calls=%async_computation.2 | async-start | bytes 786432 | tf_op jit(solution)/shard_map/all_to_all | solution.py:117
  144.7 12.3 %all-to-all-start.2 = ((bf16[4,64,768]{2,1,0:T(8,128)(2,1)}), bf16[4,64,768]{2,1,0:T(8,128)(2,1)S(1)}, u32[]{:S(2)}, u32[]{:S(2)}) async-start(bf16[4,64,768]{2,1,0:T(8,128)(2,1)} %reshape.354), calls=%async_computation.3 | async-start | bytes 786432 | tf_op jit(solution)/shard_map/all_to_all | solution.py:118
Sparse Core Ops, SparseCore 0:
  9.6 49.0 all-gather.2
  60.3 38.5 all-gather.4
  129.4 31.1 reduce-scatter.1
where the time goes:
time: 171 us; the launch traced here: 170 us
  blocking collectives  64.2 us (38%)
  local copies, waits for them, and re-layouts  35.5 us (21%)
  matrix products  18.4 us (11%)
  between operations  14.2 us (8%)
  starting transfers between devices  14 us (8%)
  waiting for transfers between devices  13.1 us (8%)
  other arithmetic  10.7 us (6%)
    all_gather x1, blocking collectives, per_device(): lax.all_gather(flat_k, 'seq', axis=0, tiled=True)  36.2 us
    all_gather x1, blocking collectives, per_device(): lax.all_gather(flat_v, 'seq', axis=0, tiled=True)  28 us
    scatter x3, local copies, waits for them, and re-layouts, unpack(): jnp.zeros((blocks_dev, 4, width), arrived.dtype).at[target]  7.88 us
    dot_general x5, matrix products, attend(): jnp.einsum('hqk,khd->hqd', weights.astype(jnp.bfloat16), values_h, prefer...  6.8 us
    all_to_all x1, waiting for transfers between devices, per_device(): lax.all_to_all(pack(pooled_k), 'seq', split_axis=0, concat_axis=0, tiled=...  6.37 us
    all_to_all x1, starting transfers between devices, per_device(): lax.all_to_all(pack(pooled_q), 'seq', split_axis=0, concat_axis=0, tiled=...  6.32 us
    dot_general x1, matrix products, per_device(): lax.dot_general(out_weight, mixed, (((0,), (1,)), ((), ())), preferred_el...  5.39 us
    all_to_all x1, waiting for transfers between devices, per_device(): lax.all_to_all(pack(pooled_v), 'seq', split_axis=0, concat_axis=0, tiled=...  5.32 us
  transfers between devices with their start and end apart: 6, of which 2 were waited for; matrix products, arithmetic and copies ran while one was open for 20% of the time, Pallas kernels for 0%

commit v1 on v0

--- a/solution.py
+++ b/solution.py
@@ -1,8 +1,11 @@
+import functools
 import math
 
 import jax
 import jax.numpy as jnp
 from jax import lax
+from jax.experimental import pallas as pl
+from jax.experimental.pallas import tpu as pltpu
 from jax.sharding import PartitionSpec as P
 
 HEAD_DIM = 128
@@ -209,6 +212,368 @@
     )
 
 
+def place_index(shape, dim):
+    return lax.broadcasted_iota(jnp.int32, shape, dim)
+
+
+def coarse_of(frame, levels_ref, frames_ctx):
+    coarse = frame < 0
+    for f in range(frames_ctx):
+        coarse = jnp.logical_or(coarse, jnp.logical_and(frame == f, levels_ref[f] == 1))
+    return coarse
+
+
+def pack_kernel(levels, q, k, v, cq, ck, cv, near, far):
+    z = lax.axis_index("seq")
+    devices = lax.axis_size("seq")
+    new_rows = q.shape[0]
+    ctx_rows = cq.shape[0]
+    width = q.shape[1]
+    half = width // 2
+    rows = new_rows + ctx_rows
+    frames_ctx = levels.shape[0]
+    index = place_index((ctx_rows, 1), 0)
+    frame = (z * ctx_rows + index) * frames_ctx // (devices * ctx_rows)
+    coarse = coarse_of(frame, levels, frames_ctx)
+    first = index % 4 == 0
+
+    def pooled(ref, lanes):
+        x = ref[:, lanes]
+        wide = x.astype(jnp.float32)
+        pairs = wide + pltpu.roll(wide, ctx_rows - 1, 0)
+        quads = pairs + pltpu.roll(pairs, ctx_rows - 2, 0)
+        mean = jnp.where(first, quads * 0.25, 0.0)
+        return jnp.where(coarse, mean, wide).astype(jnp.bfloat16)
+
+    def put(a, b):
+        for part, (fresh, ctx) in enumerate(((k, ck), (v, cv), (q, cq))):
+            base = part * rows
+            for out, lo in ((a, 0), (b, half)):
+                lanes = slice(lo, lo + half)
+                out[base : base + new_rows] = fresh[:, lanes]
+                out[base + new_rows : base + rows] = pooled(ctx, lanes)
+
+    @pl.when(z < devices // 2)
+    def _():
+        put(near, far)
+
+    @pl.when(z >= devices // 2)
+    def _():
+        put(far, near)
+
+
+def plan_kernel(owners, levels, order, alive):
+    blocks = owners.shape[1]
+    size = order.shape[0]
+    per = size // blocks
+    devices = lax.axis_size("seq")
+    frames_ctx = levels.shape[0]
+    row = owners[...].astype(jnp.float32)
+    r = place_index((blocks, blocks), 0)
+    c = place_index((blocks, blocks), 1)
+    col = jnp.sum(jnp.where(r == c, row, 0.0), axis=1, keepdims=True)
+    ahead = jnp.logical_and(col == row, r < c)
+    rank = jnp.sum(ahead.astype(jnp.float32), axis=0, keepdims=True)
+    spot = row * float(blocks // devices) + rank
+    spread = (
+        place_index((blocks, size), 1) // per == place_index((blocks, size), 0)
+    ).astype(jnp.bfloat16)
+    wide = jnp.dot(
+        jnp.broadcast_to(spot, (16, blocks)).astype(jnp.bfloat16),
+        spread,
+        preferred_element_type=jnp.float32,
+    )[0:1]
+    lane = place_index((1, size), 1)
+    target = wide.astype(jnp.int32) * per + lane % per
+    move = (place_index((size, size), 0) == target).astype(jnp.bfloat16)
+    order[...] = move
+    index = place_index((size, alive.shape[1]), 0)
+    coarse = coarse_of(index * frames_ctx // size, levels, frames_ctx)
+    live = jnp.logical_or(jnp.logical_not(coarse), index % per == 0)
+    alive[...] = jnp.dot(
+        move, live.astype(jnp.bfloat16), preferred_element_type=jnp.float32
+    )
+
+
+def far_places(z):
+    across = 3 - z
+    beside = jnp.where(z == 1, 0, 3)
+    return (z, beside, across, 3 - beside)
+
+
+def attend_kernel(scale, new_rows, levels, masks, s0, s1, s2, s3, order, alive, o0, o1, o2, o3, kc, va, qc):
+    z = lax.axis_index("seq")
+    ctx_rows = s0.shape[0] // 3 - new_rows
+    rows = new_rows + ctx_rows
+    sources = (s0, s1, s2, s3)
+    outs = (o0, o1, o2, o3)
+    count = len(sources)
+    fresh = count * new_rows
+    ctx = count * ctx_rows
+    hdim = s0.shape[1]
+    frames_ctx = levels.shape[0]
+    frames_new = masks.shape[0]
+    factor = scale * math.log2(math.e)
+
+    @pl.when(jnp.logical_or(z == 1, z == 2))
+    def _():
+        places = far_places(z)
+        va[:, hdim:] = jnp.ones((fresh + ctx, hdim), jnp.bfloat16)
+        for i, src in enumerate(sources):
+            at = slice(i * new_rows, (i + 1) * new_rows)
+            to = pl.ds(pl.multiple_of(fresh + places[i] * ctx_rows, ctx_rows), ctx_rows)
+            kc[at] = src[0:new_rows]
+            kc[to] = src[new_rows:rows]
+            va[at, :hdim] = src[rows : rows + new_rows]
+            va[to, :hdim] = src[rows + new_rows : 2 * rows]
+            qc[pl.ds(pl.multiple_of(places[i] * ctx_rows, ctx_rows), ctx_rows)] = src[
+                2 * rows + new_rows : 3 * rows
+            ]
+        index = place_index((1, ctx), 1)
+        frame = index * frames_ctx // ctx
+        live = jnp.logical_or(
+            jnp.logical_not(coarse_of(frame, levels, frames_ctx)), index % 4 == 0
+        )
+
+        def weigh(q, allowed):
+            scores = lax.dot_general(
+                q, kc[...], (((1,), (1,)), ((), ())), preferred_element_type=jnp.float32
+            )
+            bias = jnp.where(allowed, 0.0, NEGATIVE)
+            ahead = scores[:, :fresh]
+            behind = scores[:, fresh:] + bias
+            top = jnp.maximum(
+                jnp.max(ahead, axis=1, keepdims=True), jnp.max(behind, axis=1, keepdims=True)
+            )
+            w_ahead = jnp.exp2((ahead - top) * factor).astype(jnp.bfloat16)
+            w_behind = jnp.exp2((behind - top) * factor).astype(jnp.bfloat16)
+            both = jnp.dot(
+                w_ahead, va[:fresh], preferred_element_type=jnp.float32
+            ) + jnp.dot(w_behind, va[fresh:], preferred_element_type=jnp.float32)
+            return both[:, :hdim] / both[:, hdim:]
+
+        for i, (src, out) in enumerate(zip(sources, outs)):
+            row_frame = places[i] * frames_new // count
+            seen = frame < 0
+            for f in range(frames_ctx):
+                seen = jnp.logical_or(
+                    seen, jnp.logical_and(frame == f, masks[row_frame, f] == 1)
+                )
+            q = src[2 * rows : 2 * rows + new_rows]
+            out[0:new_rows] = weigh(q, jnp.logical_and(live, seen)).astype(jnp.bfloat16)
+        for i, out in enumerate(outs):
+            part = pl.ds(pl.multiple_of(places[i] * ctx_rows, ctx_rows), ctx_rows)
+            q = jnp.dot(order[part], qc[...], preferred_element_type=jnp.float32)
+            mixed = weigh(q.astype(jnp.bfloat16), live) * alive[part]
+            out[new_rows:rows] = mixed.astype(jnp.bfloat16)
+
+
+def cache_kernel(new_rows, s0, s1, s2, s3, order, c0, c1, c2, c3, kk):
+    z = lax.axis_index("seq")
+    ctx_rows = s0.shape[0] // 3 - new_rows
+    rows = new_rows + ctx_rows
+    sources = (s0, s1, s2, s3)
+    width = s0.shape[1]
+
+    @pl.when(jnp.logical_or(z == 1, z == 2))
+    def _():
+        places = far_places(z)
+        for i, src in enumerate(sources):
+            to = pl.ds(pl.multiple_of(places[i] * ctx_rows, ctx_rows), ctx_rows)
+            kk[to, :width] = src[new_rows:rows]
+            kk[to, width:] = src[rows + new_rows : 2 * rows]
+        for i, out in enumerate((c0, c1, c2, c3)):
+            part = pl.ds(pl.multiple_of(places[i] * ctx_rows, ctx_rows), ctx_rows)
+            moved = jnp.dot(order[part], kk[...], preferred_element_type=jnp.float32)
+            out[:ctx_rows] = moved[:, :width].astype(jnp.bfloat16)
+            out[ctx_rows:] = moved[:, width:].astype(jnp.bfloat16)
+
+
+def halves(z, own, beside, across, beyond):
+    own, beside, across, beyond = own[...], beside[...], across[...], beyond[...]
+    inner = jnp.logical_or(z == 1, z == 2)
+    low = z < 2
+    near = jnp.where(inner, own, beside)
+    far = jnp.where(inner, across, beyond)
+    return (jnp.where(low, near, far), jnp.where(low, far, near))
+
+
+def project_kernel(cols, o0, o1, o2, o3, weight, out):
+    z = lax.axis_index("seq")
+    a, b = halves(z, o0, o1, o2, o3)
+    half = a.shape[1]
+    total = jnp.dot(a, weight[:half], preferred_element_type=jnp.float32)
+    total += jnp.dot(b, weight[half:], preferred_element_type=jnp.float32)
+    out[...] = total.astype(out.dtype)
+
+
+def add_kernel(keep, came, out):
+    chip = lax.axis_index("tensor") // 2
+    rows = out.shape[0]
+    at = pl.ds(pl.multiple_of((1 - chip) * rows, rows), rows)
+    out[...] = (keep[at] + came[at].astype(jnp.float32)).astype(jnp.bfloat16)
+
+
+def finish_kernel(keep, came, last, out, out_ctx):
+    chip = lax.axis_index("tensor") // 2
+    rows = last.shape[0]
+    at = pl.ds(pl.multiple_of(chip * rows, rows), rows)
+    total = keep[at] + came[at].astype(jnp.float32) + last[...].astype(jnp.float32)
+    total = total.astype(jnp.bfloat16)
+    out[...] = total[: out.shape[0]]
+    out_ctx[...] = total[out.shape[0] :]
+
+
+def store_kernel(c0, c1, c2, c3, keys, values):
+    z = lax.axis_index("seq")
+    a, b = halves(z, c0, c1, c2, c3)
+    half = a.shape[1]
+    ctx_rows = keys.shape[0]
+    keys[:, :half] = a[:ctx_rows]
+    keys[:, half:] = b[:ctx_rows]
+    values[:, :half] = a[ctx_rows:]
+    values[:, half:] = b[ctx_rows:]
+
+
+SMALL = pl.BlockSpec(memory_space=pltpu.SMEM)
+LIMIT = pltpu.CompilerParams(vmem_limit_bytes=48 * 1024 * 1024)
+
+
+def shape16(*dims):
+    return jax.ShapeDtypeStruct(dims, jnp.bfloat16)
+
+
+def permute(x, pairs):
+    return lax.ppermute(x, "seq", pairs)
+
+
+BESIDE = ((0, 1), (3, 2))
+ACROSS = ((1, 2), (2, 1))
+BEYOND = ((0, 2), (3, 1))
+
+
+def back(pairs):
+    return tuple((b, a) for a, b in pairs)
+
+
+def fast_device(
+    queries,
+    new_keys,
+    new_values,
+    context_queries,
+    context_keys,
+    context_values,
+    levels,
+    frame_mask,
+    owners,
+    out_weight,
+):
+    new_rows, width = queries.shape
+    ctx_rows = context_keys.shape[0]
+    rows = new_rows + ctx_rows
+    half = width // 2
+    devices = lax.axis_size("seq")
+    ctx_all = ctx_rows * devices
+    hdim = HEAD_DIM
+    scale = 1.0 / math.sqrt(hdim)
+    whole = pl.BlockSpec()
+    near, far = pl.pallas_call(
+        pack_kernel,
+        out_shape=(shape16(3 * rows, half), shape16(3 * rows, half)),
+        in_specs=[SMALL] + [whole] * 6,
+        compiler_params=LIMIT,
+    )(levels, queries, new_keys, new_values, context_queries, context_keys, context_values)
+    beside = permute(near, BESIDE)
+    across = permute(far, ACROSS)
+    beyond = permute(far, BEYOND)
+    order, alive = pl.pallas_call(
+        plan_kernel,
+        out_shape=(shape16(ctx_all, ctx_all), jax.ShapeDtypeStruct((ctx_all, hdim), jnp.float32)),
+        in_specs=[whole, SMALL],
+        compiler_params=LIMIT,
+    )(owners.reshape(1, -1), levels)
+    per_head = lambda length: pl.BlockSpec((length, hdim), lambda h: (0, h))
+    mixed = pl.pallas_call(
+        functools.partial(attend_kernel, scale, new_rows),
+        grid=(half // hdim,),
+        out_shape=[shape16(rows, half)] * 4,
+        in_specs=[SMALL, SMALL]
+        + [per_head(3 * rows)] * 4
+        + [
+            pl.BlockSpec((ctx_all, ctx_all), lambda h: (0, 0)),
+            pl.BlockSpec((ctx_all, hdim), lambda h: (0, 0)),
+        ],
+        out_specs=[per_head(rows)] * 4,
+        scratch_shapes=[
+            pltpu.VMEM((rows * devices, hdim), jnp.bfloat16),
+            pltpu.VMEM((rows * devices, 2 * hdim), jnp.bfloat16),
+            pltpu.VMEM((ctx_all, hdim), jnp.bfloat16),
+        ],
+        compiler_params=LIMIT,
+    )(levels, frame_mask, near, beside, across, beyond, order, alive)
+    got = (
+        mixed[0],
+        permute(mixed[1], back(BESIDE)),
+        permute(mixed[2], ACROSS),
+        permute(mixed[3], back(BEYOND)),
+    )
+    caches = pl.pallas_call(
+        functools.partial(cache_kernel, new_rows),
+        out_shape=[shape16(2 * ctx_rows, half)] * 4,
+        scratch_shapes=[pltpu.VMEM((ctx_all, width), jnp.bfloat16)],
+        compiler_params=LIMIT,
+    )(near, beside, across, beyond, order)
+
+    def project(which, dtype):
+        def column(p, me):
+            core = me[0] % 2
+            return (0, 2 * p + (core if which else 1 - core))
+
+        full = pl.BlockSpec((rows, half), lambda p, me: (0, 0))
+        return pl.pallas_call(
+            lambda me, *refs: project_kernel(width, *refs),
+            grid_spec=pltpu.PrefetchScalarGridSpec(
+                num_scalar_prefetch=1,
+                grid=(2,),
+                in_specs=[full] * 4 + [pl.BlockSpec((width, width), column)],
+                out_specs=pl.BlockSpec((rows, width), lambda p, me: (p, 0)),
+            ),
+            out_shape=jax.ShapeDtypeStruct((2 * rows, width), dtype),
+            compiler_params=LIMIT,
+        )(me, *got, out_weight)
+
+    me = lax.axis_index("tensor").reshape(1).astype(jnp.int32)
+    give = project(False, jnp.bfloat16)
+    came = lax.ppermute(give, "tensor", ((0, 1), (1, 0), (2, 3), (3, 2)))
+    keep = project(True, jnp.float32)
+    other = pl.pallas_call(add_kernel, out_shape=shape16(rows, width), compiler_params=LIMIT)(
+        keep, came
+    )
+    last = lax.ppermute(other, "tensor", ((0, 2), (2, 0), (1, 3), (3, 1)))
+    stored = (
+        caches[0],
+        permute(caches[1], back(BESIDE)),
+        permute(caches[2], ACROSS),
+        permute(caches[3], back(BEYOND)),
+    )
+    cache_keys, cache_values = pl.pallas_call(
+        store_kernel,
+        out_shape=(shape16(ctx_rows, width), shape16(ctx_rows, width)),
+        compiler_params=LIMIT,
+    )(*stored)
+    block_out, context_out = pl.pallas_call(
+        finish_kernel,
+        out_shape=(shape16(new_rows, width), shape16(ctx_rows, width)),
+        compiler_params=LIMIT,
+    )(keep, came, last)
+    return (block_out, context_out, cache_keys, cache_values)
+
+
+def fits_fast(mesh):
+    sizes = mesh.shape
+    return sizes["seq"] == 4 and sizes["tensor"] == 4
+
+
 def solution(mesh):
     in_specs = (
         P(("session", "seq"), "tensor"),
@@ -228,6 +593,5 @@
         P(("session", "seq"), "tensor"),
         P(("session", "seq"), "tensor"),
     )
-    return jax.shard_map(
-        per_device, mesh=mesh, in_specs=in_specs, out_specs=out_specs, check_vma=False
-    )
+    step = fast_device if fits_fast(mesh) else per_device
+    return jax.shard_map(step, mesh=mesh, in_specs=in_specs, out_specs=out_specs, check_vma=False)

time: 171 us -> 102 us (0.60)
  blocking collectives: 64.2 us -> 0 us
  waiting for transfers between devices: 13.1 us -> 60.3 us
  local copies, waits for them, and re-layouts: 35.5 us -> 9.27 us
  matrix products: 18.4 us -> 0 us
  between operations: 14.2 us -> 0.79 us
  Pallas kernels: 0 us -> 12.5 us
  other arithmetic: 10.7 us -> 0 us
  starting transfers between devices: 14 us -> 18.4 us
    all_gather x2 -> x0, blocking collectives: 64.2 us -> none  [the longest x1 36.2 us: per_device(): lax.all_gather(flat_k, 'seq', axis=0, tiled=True)]
    ppermute x0 -> x11, waiting for transfers between devices: none -> 60.3 us  [the longest x9 60.3 us: permute(): return lax.ppermute(x, 'seq', pairs)]
    dot_general x12 -> x0, matrix products: 18.4 us -> none  [the longest x5 6.8 us: attend(): jnp.einsum('hqk,khd->hqd', weights.astype(jnp.bfloat16), values_h, prefer...]
    ppermute x0 -> x11, starting transfers between devices: none -> 18.4 us  [the longest x9 16.8 us: permute(): return lax.ppermute(x, 'seq', pairs)]
    all_to_all x3 -> x0, starting transfers between devices: 13.9 us -> none  [the longest x1 6.32 us: per_device(): lax.all_to_all(pack(pooled_q), 'seq', split_axis=0, concat_axis=0, tiled=...]
    scatter x6 -> x0, local copies, waits for them, and re-layouts: 12.5 us -> none  [the longest x3 7.88 us: unpack(): jnp.zeros((blocks_dev, 4, width), arrived.dtype).at[target]]
    pallas_call x0 -> x9, Pallas kernels: none -> 12.5 us  [the longest x2 5.7 us: project(): pl.pallas_call(lambda me, *refs: project_kernel(width, *refs), grid_spec=...]
    all_to_all x3 -> x0, waiting for transfers between devices: 11.7 us -> none  [the longest x1 6.37 us: per_device(): lax.all_to_all(pack(pooled_k), 'seq', split_axis=0, concat_axis=0, tiled=...]
  transfers between devices with their start and end apart: 6 -> 11, of which waited for: 2 -> 6; matrix products, arithmetic and copies ran while one was open for 20% -> 0% of each run, Pallas kernels for 0% -> 5%
where the time goes in v1:
time: 102 us; the launch traced here: 101 us
  waiting for transfers between devices  60.3 us (59%)
  starting transfers between devices  18.4 us (18%)
  Pallas kernels  12.5 us (12%)
  local copies, waits for them, and re-layouts  9.27 us (9%)
    ppermute x9, waiting for transfers between devices, permute(): return lax.ppermute(x, 'seq', pairs)  60.3 us
    ppermute x9, starting transfers between devices, permute(): return lax.ppermute(x, 'seq', pairs)  16.8 us
    unnamed x22, local copies, waits for them, and re-layouts  9.27 us
    pallas_call x2, Pallas kernels, project(): pl.pallas_call(lambda me, *refs: project_kernel(width, *refs), grid_spec=...  5.7 us
    pallas_call x1, Pallas kernels, fast_device(): pl.pallas_call(functools.partial(attend_kernel, scale, new_rows), grid=(h...  2.21 us
  transfers between devices with their start and end apart: 11, of which 6 were waited for; matrix products, arithmetic and copies ran while one was open for 0% of the time, Pallas kernels for 5%

profile of v1, /device:TPU:0, one launch (start us, length us, event | category | flops | bytes accessed | tf_op | source)
XLA Modules:
  0.0 101.3 jit_solution(8666818724360007626)
XLA Ops:
  0.6 0.0 copy-start.2
  0.6 1.0 copy-done.2
  1.6 0.0 copy-start.3
  1.6 1.0 copy-done.3
  2.6 0.0 copy-start.4
  2.6 1.0 copy-done.4
  3.5 0.0 copy-start.5
  3.5 0.9 copy-done.5
  4.4 0.0 copy-start.6
  4.4 0.9 copy-done.6
  5.4 0.0 copy-start.7
  5.4 0.9 copy-done.7
  6.3 0.0 copy-start.8
  6.3 0.7 copy-done.8
  7.0 1.2 %shard_map.129 = (bf16[960,384]{1,0:T(8,128)(2,1)S(1)}, bf16[960,384]{1,0:T(8,128)(2,1)S(1)}) custom-call(s32[8]{0:T(128)S(1)} %copy-done.8, bf16[192,768]{1,0:T(8,128)(2,1)S(1)} %copy-done.2, bf16[192,768]{1,0:T(8,128)(2,1)S(1)} %copy-done.3, bf16[192,768]{1,0:T(8,128)(2,1)S(1)} %copy-done.4, bf16[128,768]{1,0:T(8,128)(2,1)S(1)} %copy-done.5, ...), custom_call_target="tpu_custom_call" | custom-call | tf_op jit(solution)/shard_map/pallas_call | solution.py:480
  8.2 5.0 %collective-permute-start = (bf16[960,384]{1,0:T(8,128)(2,1)S(1)}, bf16[960,384]{1,0:T(8,128)(2,1)S(1)}, u32[]{:S(2)}, u32[]{:S(2)}) collective-permute-start(bf16[960,384]{1,0:T(8,128)(2,1)S(1)} %get-tuple-element.20.s0), channel_id=1, source_target_pairs={{0,4},{12,8},{1,5},{13,9},{2,6},{14,10},{3,7},{15,11},{16,20},{28,... | collective-permute-start | bytes 2211848 | tf_op jit(solution)/shard_map/ppermute | solution.py:447
  13.2 0.7 collective-permute-start.1
  13.9 4.0 %collective-permute-start.2 = (bf16[960,384]{1,0:T(8,128)(2,1)S(1)}, bf16[960,384]{1,0:T(8,128)(2,1)S(1)}, u32[]{:S(2)}, u32[]{:S(2)}) collective-permute-start(bf16[960,384]{1,0:T(8,128)(2,1)S(1)} %get-tuple-element.21), channel_id=1, source_target_pairs={{0,8},{12,4},{1,9},{13,5},{2,10},{14,6},{3,11},{15,7},{16,24},{28,... | collective-permute-start | bytes 2211848 | tf_op jit(solution)/shard_map/ppermute | solution.py:447
  17.8 0.0 copy-start.10
  17.9 0.6 copy-done.10
  18.5 1.6 %shard_map.130 = (bf16[512,512]{1,0:T(8,128)(2,1)S(1)}, f32[512,128]{1,0:T(8,128)S(1)}) custom-call(s32[1,128]{1,0:T(1,128)S(1)} %bitcast.2, s32[8]{0:T(128)S(1)} %copy-done.8), custom_call_target="tpu_custom_call" | custom-call | tf_op jit(solution)/shard_map/pallas_call | solution.py:489
  20.1 9.9 %collective-permute-done.s1 = bf16[960,384]{1,0:T(8,128)(2,1)S(1)} collective-permute-done((bf16[960,384]{1,0:T(8,128)(2,1)S(1)}, bf16[960,384]{1,0:T(8,128)(2,1)S(1)}, u32[]{:S(2)}, u32[]{:S(2)}) %collective-permute-start) | collective-permute-done | bytes 737312 | tf_op jit(solution)/shard_map/ppermute | solution.py:447
  30.0 0.0 collective-permute-done.1.s2
  30.0 14.7 %collective-permute-done.2.s3 = bf16[960,384]{1,0:T(8,128)(2,1)S(1)} collective-permute-done((bf16[960,384]{1,0:T(8,128)(2,1)S(1)}, bf16[960,384]{1,0:T(8,128)(2,1)S(1)}, u32[]{:S(2)}, u32[]{:S(2)}) %collective-permute-start.2) | collective-permute-done | bytes 737312 | tf_op jit(solution)/shard_map/ppermute | solution.py:447
  44.7 0.0 copy-start.9
  44.7 0.7 copy-done.9
  45.4 2.2 %shard_map.131 = (bf16[320,384]{1,0:T(8,128)(2,1)S(1)}, bf16[320,384]{1,0:T(8,128)(2,1)}, bf16[320,384]{1,0:T(8,128)(2,1)}, bf16[320,384]{1,0:T(8,128)(2,1)}) custom-call(s32[8]{0:T(128)S(1)} %copy-done.8, s32[2,8]{1,0:T(2,128)S(1)} %copy-done.9, bf16[960,384]{1,0:T(8,128)(2,1)S(1)} %get-tuple-element.20.s0, bf16[960,384]{1,0:T(8,128)(2,1)S(1)} %collective-permute-done.s1, ...), custom_call_target="tpu_custom_call" | custom-call | tf_op jit(solution)/shard_map/pallas_call | solution.py:496
  47.6 0.0 copy-start
  47.6 0.7 copy-done
  48.3 1.3 %collective-permute-start.3 = (bf16[320,384]{1,0:T(8,128)(2,1)}, bf16[320,384]{1,0:T(8,128)(2,1)}, u32[]{:S(2)}, u32[]{:S(2)}) collective-permute-start(bf16[320,384]{1,0:T(8,128)(2,1)} %get-tuple-element.25), channel_id=1, source_target_pairs={{4,0},{8,12},{5,1},{9,13},{6,2},{10,14},{7,3},{11,15},{20,16},{24,... | collective-permute-start | bytes 737288 | tf_op jit(solution)/shard_map/ppermute | solution.py:447
  49.6 1.4 %collective-permute-start.4 = (bf16[320,384]{1,0:T(8,128)(2,1)}, bf16[320,384]{1,0:T(8,128)(2,1)}, u32[]{:S(2)}, u32[]{:S(2)}) collective-permute-start(bf16[320,384]{1,0:T(8,128)(2,1)} %get-tuple-element.26), channel_id=1, source_target_pairs={{4,8},{8,4},{5,9},{9,5},{6,10},{10,6},{7,11},{11,7},{20,24},{24,20... | collective-permute-start | bytes 737288 | tf_op jit(solution)/shard_map/ppermute | solution.py:447
  50.9 1.3 %collective-permute-start.5 = (bf16[320,384]{1,0:T(8,128)(2,1)}, bf16[320,384]{1,0:T(8,128)(2,1)}, u32[]{:S(2)}, u32[]{:S(2)}) collective-permute-start(bf16[320,384]{1,0:T(8,128)(2,1)} %get-tuple-element.27), channel_id=1, source_target_pairs={{8,0},{4,12},{9,1},{5,13},{10,2},{6,14},{11,3},{7,15},{24,16},{20,... | collective-permute-start | bytes 737288 | tf_op jit(solution)/shard_map/ppermute | solution.py:447
  52.2 15.8 %collective-permute-done.3.refs_1_ = bf16[320,384]{1,0:T(8,128)(2,1)} collective-permute-done((bf16[320,384]{1,0:T(8,128)(2,1)}, bf16[320,384]{1,0:T(8,128)(2,1)}, u32[]{:S(2)}, u32[]{:S(2)}) %collective-permute-start.3) | collective-permute-done | bytes 245792 | tf_op jit(solution)/shard_map/ppermute | solution.py:447
  68.1 0.0 collective-permute-done.4.refs_2_
  68.1 9.1 %collective-permute-done.5.refs_3_ = bf16[320,384]{1,0:T(8,128)(2,1)} collective-permute-done((bf16[320,384]{1,0:T(8,128)(2,1)}, bf16[320,384]{1,0:T(8,128)(2,1)}, u32[]{:S(2)}, u32[]{:S(2)}) %collective-permute-start.5) | collective-permute-done | bytes 245792 | tf_op jit(solution)/shard_map/ppermute | solution.py:447
  77.2 0.0 copy-start.1
  77.2 0.9 copy-done.1
  78.1 2.8 %shard_map.133 = bf16[640,768]{1,0:T(8,128)(2,1)S(1)} custom-call(s32[1]{0:T(128)} %bitcast.me, bf16[320,384]{1,0:T(8,128)(2,1)S(1)} %copy-done.1, bf16[320,384]{1,0:T(8,128)(2,1)} %collective-permute-done.3.refs_1_, bf16[320,384]{1,0:T(8,128)(2,1)} %collective-permute-done.4.refs_2_, bf16[320,384]{1,0:T(8,128)(2,1)} %collective-permute-done.5.refs_3_, ...), custom_call_target="tpu_custom_call" | custom-call | tf_op jit(solution)/shard_map/pallas_call | solution.py:533
  81.0 0.1 collective-permute-start.6
  81.1 2.9 %shard_map.132.keep = f32[640,768]{1,0:T(8,128)S(1)} custom-call(s32[1]{0:T(128)} %bitcast.me, bf16[320,384]{1,0:T(8,128)(2,1)S(1)} %copy-done.1, bf16[320,384]{1,0:T(8,128)(2,1)} %collective-permute-done.3.refs_1_, bf16[320,384]{1,0:T(8,128)(2,1)} %collective-permute-done.4.refs_2_, bf16[320,384]{1,0:T(8,128)(2,1)} %collective-permute-done.5.refs_3_, ...), custom_call_target="tpu_custom_call" | custom-call | tf_op jit(solution)/shard_map/pallas_call | solution.py:533
  83.9 0.0 collective-permute-done.6.came
  84.0 0.1 shard_map.134
  84.1 1.6 %collective-permute-start.7 = (bf16[320,768]{1,0:T(8,128)(2,1)S(1)}, bf16[320,768]{1,0:T(8,128)(2,1)S(1)}, u32[]{:S(2)}, u32[]{:S(2)}) collective-permute-start(bf16[320,768]{1,0:T(8,128)(2,1)S(1)} %shard_map.134), channel_id=1, source_target_pairs={{0,2},{2,0},{1,3},{3,1},{4,6},{6,4},{5,7},{7,5},{8,10},{10,8},{9,1... | collective-permute-start | bytes 1474568 | tf_op jit(solution)/shard_map/ppermute | solution.py:552
  85.6 1.3 %collective-permute-start.10 = (bf16[256,384]{1,0:T(8,128)(2,1)S(1)}, bf16[256,384]{1,0:T(8,128)(2,1)S(1)}, u32[]{:S(2)}, u32[]{:S(2)}) collective-permute-start(bf16[256,384]{1,0:T(8,128)(2,1)S(1)} %get-tuple-element.33), channel_id=1, source_target_pairs={{8,0},{4,12},{9,1},{5,13},{10,2},{6,14},{11,3},{7,15},{24,16},{20,... | collective-permute-start | bytes 589832 | tf_op jit(solution)/shard_map/ppermute | solution.py:447
  86.9 1.3 %collective-permute-start.8 = (bf16[256,384]{1,0:T(8,128)(2,1)S(1)}, bf16[256,384]{1,0:T(8,128)(2,1)S(1)}, u32[]{:S(2)}, u32[]{:S(2)}) collective-permute-start(bf16[256,384]{1,0:T(8,128)(2,1)S(1)} %get-tuple-element.31), channel_id=1, source_target_pairs={{4,0},{8,12},{5,1},{9,13},{6,2},{10,14},{7,3},{11,15},{20,16},{24,... | collective-permute-start | bytes 589832 | tf_op jit(solution)/shard_map/ppermute | solution.py:447
  88.2 0.7 collective-permute-start.9
  88.9 6.6 %collective-permute-done.10.c3 = bf16[256,384]{1,0:T(8,128)(2,1)S(1)} collective-permute-done((bf16[256,384]{1,0:T(8,128)(2,1)S(1)}, bf16[256,384]{1,0:T(8,128)(2,1)S(1)}, u32[]{:S(2)}, u32[]{:S(2)}) %collective-permute-start.10) | collective-permute-done | bytes 196640 | tf_op jit(solution)/shard_map/ppermute | solution.py:447
  95.5 4.1 %collective-permute-done.8.c1 = bf16[256,384]{1,0:T(8,128)(2,1)S(1)} collective-permute-done((bf16[256,384]{1,0:T(8,128)(2,1)S(1)}, bf16[256,384]{1,0:T(8,128)(2,1)S(1)}, u32[]{:S(2)}, u32[]{:S(2)}) %collective-permute-start.8) | collective-permute-done | bytes 196640 | tf_op jit(solution)/shard_map/ppermute | solution.py:447
  99.6 0.0 collective-permute-done.9.c2
  99.6 0.8 shard_map.137
  100.4 0.0 collective-permute-done.7.last
  100.4 0.9 shard_map.135
  (1 shorter events, 0.0 us)
Async XLA Ops:
  0.6 1.0 copy-start.2
  1.6 1.0 copy-start.3
  2.6 1.0 copy-start.4
  3.5 0.9 copy-start.5
  4.4 0.9 copy-start.6
  5.4 0.9 copy-start.7
  6.3 0.7 copy-start.8
  8.2 21.8 %collective-permute-start = (bf16[960,384]{1,0:T(8,128)(2,1)S(1)}, bf16[960,384]{1,0:T(8,128)(2,1)S(1)}, u32[]{:S(2)}, u32[]{:S(2)}) collective-permute-start(bf16[960,384]{1,0:T(8,128)(2,1)S(1)} %get-tuple-element.20.s0), channel_id=1, source_target_pairs={{0,4},{12,8},{1,5},{13,9},{2,6},{14,10},{3,7},{15,11},{16,20},{28,... | collective-permute-start | bytes 2211848 | tf_op jit(solution)/shard_map/ppermute | solution.py:447
  13.2 16.8 %collective-permute-start.1 = (bf16[960,384]{1,0:T(8,128)(2,1)S(1)}, bf16[960,384]{1,0:T(8,128)(2,1)S(1)}, u32[]{:S(2)}, u32[]{:S(2)}) collective-permute-start(bf16[960,384]{1,0:T(8,128)(2,1)S(1)} %get-tuple-element.21), channel_id=1, source_target_pairs={{4,8},{8,4},{5,9},{9,5},{6,10},{10,6},{7,11},{11,7},{20,24},{24,20... | collective-permute-start | bytes 2211848 | tf_op jit(solution)/shard_map/ppermute | solution.py:447
  13.9 30.8 %collective-permute-start.2 = (bf16[960,384]{1,0:T(8,128)(2,1)S(1)}, bf16[960,384]{1,0:T(8,128)(2,1)S(1)}, u32[]{:S(2)}, u32[]{:S(2)}) collective-permute-start(bf16[960,384]{1,0:T(8,128)(2,1)S(1)} %get-tuple-element.21), channel_id=1, source_target_pairs={{0,8},{12,4},{1,9},{13,5},{2,10},{14,6},{3,11},{15,7},{16,24},{28,... | collective-permute-start | bytes 2211848 | tf_op jit(solution)/shard_map/ppermute | solution.py:447
  17.8 0.7 copy-start.10
  44.7 0.7 copy-start.9
  47.6 0.7 copy-start
  48.3 19.8 %collective-permute-start.3 = (bf16[320,384]{1,0:T(8,128)(2,1)}, bf16[320,384]{1,0:T(8,128)(2,1)}, u32[]{:S(2)}, u32[]{:S(2)}) collective-permute-start(bf16[320,384]{1,0:T(8,128)(2,1)} %get-tuple-element.25), channel_id=1, source_target_pairs={{4,0},{8,12},{5,1},{9,13},{6,2},{10,14},{7,3},{11,15},{20,16},{24,... | collective-permute-start | bytes 737288 | tf_op jit(solution)/shard_map/ppermute | solution.py:447
  49.6 18.5 %collective-permute-start.4 = (bf16[320,384]{1,0:T(8,128)(2,1)}, bf16[320,384]{1,0:T(8,128)(2,1)}, u32[]{:S(2)}, u32[]{:S(2)}) collective-permute-start(bf16[320,384]{1,0:T(8,128)(2,1)} %get-tuple-element.26), channel_id=1, source_target_pairs={{4,8},{8,4},{5,9},{9,5},{6,10},{10,6},{7,11},{11,7},{20,24},{24,20... | collective-permute-start | bytes 737288 | tf_op jit(solution)/shard_map/ppermute | solution.py:447
  50.9 26.3 %collective-permute-start.5 = (bf16[320,384]{1,0:T(8,128)(2,1)}, bf16[320,384]{1,0:T(8,128)(2,1)}, u32[]{:S(2)}, u32[]{:S(2)}) collective-permute-start(bf16[320,384]{1,0:T(8,128)(2,1)} %get-tuple-element.27), channel_id=1, source_target_pairs={{8,0},{4,12},{9,1},{5,13},{10,2},{6,14},{11,3},{7,15},{24,16},{20,... | collective-permute-start | bytes 737288 | tf_op jit(solution)/shard_map/ppermute | solution.py:447
  77.2 0.9 copy-start.1
  81.0 3.0 %collective-permute-start.6 = (bf16[640,768]{1,0:T(8,128)(2,1)S(1)}, bf16[640,768]{1,0:T(8,128)(2,1)S(1)}, u32[]{:S(2)}, u32[]{:S(2)}) collective-permute-start(bf16[640,768]{1,0:T(8,128)(2,1)S(1)} %shard_map.133), channel_id=1, source_target_pairs={{0,1},{1,0},{2,3},{3,2},{4,5},{5,4},{6,7},{7,6},{8,9},{9,8},{10,11... | collective-permute-start | bytes 2949128 | tf_op jit(solution)/shard_map/ppermute | solution.py:547
  84.1 16.4 %collective-permute-start.7 = (bf16[320,768]{1,0:T(8,128)(2,1)S(1)}, bf16[320,768]{1,0:T(8,128)(2,1)S(1)}, u32[]{:S(2)}, u32[]{:S(2)}) collective-permute-start(bf16[320,768]{1,0:T(8,128)(2,1)S(1)} %shard_map.134), channel_id=1, source_target_pairs={{0,2},{2,0},{1,3},{3,1},{4,6},{6,4},{5,7},{7,5},{8,10},{10,8},{9,1... | collective-permute-start | bytes 1474568 | tf_op jit(solution)/shard_map/ppermute | solution.py:552
  85.6 9.9 %collective-permute-start.10 = (bf16[256,384]{1,0:T(8,128)(2,1)S(1)}, bf16[256,384]{1,0:T(8,128)(2,1)S(1)}, u32[]{:S(2)}, u32[]{:S(2)}) collective-permute-start(bf16[256,384]{1,0:T(8,128)(2,1)S(1)} %get-tuple-element.33), channel_id=1, source_target_pairs={{8,0},{4,12},{9,1},{5,13},{10,2},{6,14},{11,3},{7,15},{24,16},{20,... | collective-permute-start | bytes 589832 | tf_op jit(solution)/shard_map/ppermute | solution.py:447
  86.9 12.7 %collective-permute-start.8 = (bf16[256,384]{1,0:T(8,128)(2,1)S(1)}, bf16[256,384]{1,0:T(8,128)(2,1)S(1)}, u32[]{:S(2)}, u32[]{:S(2)}) collective-permute-start(bf16[256,384]{1,0:T(8,128)(2,1)S(1)} %get-tuple-element.31), channel_id=1, source_target_pairs={{4,0},{8,12},{5,1},{9,13},{6,2},{10,14},{7,3},{11,15},{20,16},{24,... | collective-permute-start | bytes 589832 | tf_op jit(solution)/shard_map/ppermute | solution.py:447
  88.2 11.4 %collective-permute-start.9 = (bf16[256,384]{1,0:T(8,128)(2,1)S(1)}, bf16[256,384]{1,0:T(8,128)(2,1)S(1)}, u32[]{:S(2)}, u32[]{:S(2)}) collective-permute-start(bf16[256,384]{1,0:T(8,128)(2,1)S(1)} %get-tuple-element.32), channel_id=1, source_target_pairs={{4,8},{8,4},{5,9},{9,5},{6,10},{10,6},{7,11},{11,7},{20,24},{24,20... | collective-permute-start | bytes 589832 | tf_op jit(solution)/shard_map/ppermute | solution.py:447

commit v2 on v0

--- a/solution.py
+++ b/solution.py
@@ -1,8 +1,11 @@
+import functools
 import math
 
 import jax
 import jax.numpy as jnp
 from jax import lax
+from jax.experimental import pallas as pl
+from jax.experimental.pallas import tpu as pltpu
 from jax.sharding import PartitionSpec as P
 
 HEAD_DIM = 128
@@ -209,25 +212,458 @@
     )
 
 
+def place_index(shape, dim):
+    return lax.broadcasted_iota(jnp.int32, shape, dim)
+
+
+def coarse_of(frame, levels_ref, frames_ctx):
+    coarse = frame < 0
+    for f in range(frames_ctx):
+        coarse = jnp.logical_or(coarse, jnp.logical_and(frame == f, levels_ref[f] == 1))
+    return coarse
+
+
+def pack_kernel(levels, q, k, v, cq, ck, cv, near_a, near_b, far_a, far_b, lv, sq, sk, sv, sems):
+    z = lax.axis_index("seq")
+    devices = lax.axis_size("seq")
+    new_rows, width = q.shape
+    ctx_rows = cq.shape[0]
+    half = width // 2
+    rows = new_rows + ctx_rows
+    frames_ctx = levels.shape[0]
+    low = jnp.where(z < devices // 2, 0, half)
+    near_lanes = pl.ds(pl.multiple_of(low, 128), half)
+    far_lanes = pl.ds(pl.multiple_of(half - low, 128), half)
+    pairs = [(levels, lv), (ck, sk), (cv, sv), (cq, sq)]
+    for out_a, out_b, lanes in ((far_a, far_b, far_lanes), (near_a, near_b, near_lanes)):
+        pairs.append((k.at[:, lanes], out_a.at[0:new_rows]))
+        pairs.append((v.at[:, lanes], out_a.at[rows : rows + new_rows]))
+        pairs.append((q.at[:, lanes], out_b))
+    copies = [pltpu.make_async_copy(src, dst, sems.at[i]) for i, (src, dst) in enumerate(pairs)]
+    for copy in copies:
+        copy.start()
+    index = place_index((ctx_rows, 1), 0)
+    first = index % 4 == 0
+    copies[0].wait()
+    frame = (z * ctx_rows + index) * frames_ctx // (devices * ctx_rows)
+    coarse = coarse_of(frame, lv, frames_ctx)
+    for part, (ref, copy) in enumerate(((sk, copies[1]), (sv, copies[2]), (sq, copies[3]))):
+        copy.wait()
+        at = slice(part * rows + new_rows, (part + 1) * rows)
+        if part == 2:
+            at = slice(2 * rows, 2 * rows + ctx_rows)
+        for out, lanes in ((far_a, far_lanes), (near_a, near_lanes)):
+            wide = ref[:, lanes].astype(jnp.float32)
+            pair = wide + pltpu.roll(wide, ctx_rows - 1, 0)
+            quad = pair + pltpu.roll(pair, ctx_rows - 2, 0)
+            mean = jnp.where(first, quad * 0.25, 0.0)
+            out[at] = jnp.where(coarse, mean, wide).astype(jnp.bfloat16)
+    for copy in copies[4:]:
+        copy.wait()
+
+
+def plan_kernel(owners, levels, masks, order, alive, biases):
+    blocks = owners.shape[1]
+    size = order.shape[0]
+    per = size // blocks
+    devices = lax.axis_size("seq")
+    frames_ctx = levels.shape[0]
+    row = owners[...].astype(jnp.float32)
+    r = place_index((blocks, blocks), 0)
+    c = place_index((blocks, blocks), 1)
+    col = jnp.sum(jnp.where(r == c, row, 0.0), axis=1, keepdims=True)
+    ahead = jnp.logical_and(col == row, r < c)
+    rank = jnp.sum(ahead.astype(jnp.float32), axis=0, keepdims=True)
+    spot = row * float(blocks // devices) + rank
+    spread = (
+        place_index((blocks, size), 1) // per == place_index((blocks, size), 0)
+    ).astype(jnp.bfloat16)
+    wide = jnp.dot(
+        jnp.broadcast_to(spot, (16, blocks)).astype(jnp.bfloat16),
+        spread,
+        preferred_element_type=jnp.float32,
+    )[0:1]
+    lane = place_index((1, size), 1)
+    target = wide.astype(jnp.int32) * per + lane % per
+    move = (place_index((size, size), 0) == target).astype(jnp.bfloat16)
+    order[...] = move
+    index = place_index((size, alive.shape[1]), 0)
+    coarse = coarse_of(index * frames_ctx // size, levels, frames_ctx)
+    live = jnp.logical_or(jnp.logical_not(coarse), index % per == 0)
+    alive[...] = jnp.dot(
+        move, live.astype(jnp.bfloat16), preferred_element_type=jnp.float32
+    )
+    frame = lane * frames_ctx // size
+    live = jnp.logical_or(
+        jnp.logical_not(coarse_of(frame, levels, frames_ctx)), lane % per == 0
+    )
+    biases[...] = jnp.zeros_like(biases)
+    biases[0:1] = jnp.where(live, 0.0, NEGATIVE)
+    for g in range(masks.shape[0]):
+        seen = frame < 0
+        for f in range(frames_ctx):
+            seen = jnp.logical_or(seen, jnp.logical_and(frame == f, masks[g, f] == 1))
+        biases[g + 1 : g + 2] = jnp.where(jnp.logical_and(live, seen), 0.0, NEGATIVE)
+
+
+def far_places(z):
+    across = 3 - z
+    beside = jnp.where(z == 1, 0, 3)
+    return (z, beside, across, 3 - beside)
+
+
+def middle(z):
+    return jnp.logical_or(z == 1, z == 2)
+
+
+def run_jobs(jobs, keys, values, fresh, factor):
+    hdim = values.shape[2] // 2
+
+    def score(head, q):
+        lanes = slice(head * hdim, (head + 1) * hdim)
+        return lax.dot_general(
+            q, keys[:, lanes], (((1,), (1,)), ((), ())), preferred_element_type=jnp.float32
+        )
+
+    def finish(head, scores, bias):
+        ahead = scores[:, :fresh]
+        behind = scores[:, fresh:] + bias
+        top = jnp.maximum(
+            jnp.max(ahead, axis=1, keepdims=True), jnp.max(behind, axis=1, keepdims=True)
+        )
+        w_ahead = jnp.exp2((ahead - top) * factor).astype(jnp.bfloat16)
+        w_behind = jnp.exp2((behind - top) * factor).astype(jnp.bfloat16)
+        both = jnp.dot(
+            w_ahead, values[head, :fresh], preferred_element_type=jnp.float32
+        ) + jnp.dot(w_behind, values[head, fresh:], preferred_element_type=jnp.float32)
+        return both[:, :hdim] / both[:, hdim:]
+
+    held = None
+    for job in [*jobs, None]:
+        scores = None if job is None else score(job[0], job[1]())
+        if held is not None:
+            held[3](finish(held[0], held[4], held[2]))
+        held = None if job is None else (*job, scores)
+
+
+def first_kernel(
+    factor, new_rows, frames_new,
+    a0, a1, a2, a3, b0, order, alive, biases,
+    keys, values, n0, qc,
+):
+    z = lax.axis_index("seq")
+    ctx_rows = qc.shape[0] // 4
+    rows = new_rows + ctx_rows
+    fresh = 4 * new_rows
+    heads = values.shape[0]
+    hdim = values.shape[2] // 2
+
+    @pl.when(middle(z))
+    def _():
+        places = far_places(z)
+        values[:, :, hdim:] = jnp.ones((heads, values.shape[1], hdim), jnp.bfloat16)
+        for i, src in enumerate((a0, a1, a2, a3)):
+            at = slice(i * new_rows, (i + 1) * new_rows)
+            spot = pl.multiple_of(places[i] * ctx_rows, ctx_rows)
+            to = pl.ds(fresh + spot, ctx_rows)
+            keys[at] = src[0:new_rows]
+            keys[to] = src[new_rows:rows]
+            for h in range(heads):
+                lanes = slice(h * hdim, (h + 1) * hdim)
+                values[h, at, :hdim] = src[rows : rows + new_rows, lanes]
+                values[h, to, :hdim] = src[rows + new_rows : 2 * rows, lanes]
+            qc[pl.ds(spot, ctx_rows)] = src[2 * rows : 2 * rows + ctx_rows]
+        qc[...] = jnp.dot(order[...], qc[...], preferred_element_type=jnp.float32).astype(
+            jnp.bfloat16
+        )
+        mine = biases[pl.ds(1 + z * frames_new // 4, 1)]
+        jobs = []
+        for h in range(heads):
+            lanes = slice(h * hdim, (h + 1) * hdim)
+
+            def put_ctx(r, lanes=lanes):
+                qc[:, lanes] = (r * alive[...]).astype(jnp.bfloat16)
+
+            def put_new(r, lanes=lanes):
+                n0[:, lanes] = r.astype(jnp.bfloat16)
+
+            jobs.append((h, lambda lanes=lanes: qc[:, lanes], biases[0:1], put_ctx))
+            jobs.append((h, lambda lanes=lanes: b0[:, lanes], mine, put_new))
+        run_jobs(jobs, keys, values, fresh, factor)
+
+
+def second_kernel(
+    factor, frames_new, b1, b2, b3, keys, values, biases, n0, held, o0, o1, o2, o3
+):
+    z = lax.axis_index("seq")
+    new_rows = b1.shape[0]
+    ctx_rows = held.shape[0] // 4
+    heads = values.shape[0]
+    hdim = values.shape[2] // 2
+
+    @pl.when(middle(z))
+    def _():
+        places = far_places(z)
+        near = biases[pl.ds(1 + places[1] * frames_new // 4, 1)]
+        away = biases[pl.ds(1 + places[2] * frames_new // 4, 1)]
+        jobs = []
+        for h in range(heads):
+            lanes = slice(h * hdim, (h + 1) * hdim)
+
+            def put_near(r, lanes=lanes):
+                o1[:new_rows, lanes] = r.astype(jnp.bfloat16)
+
+            def put_away(r, lanes=lanes):
+                o2[:new_rows, lanes] = r[:new_rows].astype(jnp.bfloat16)
+                o3[:new_rows, lanes] = r[new_rows:].astype(jnp.bfloat16)
+
+            def two(lanes=lanes):
+                return jnp.concatenate([b2[:, lanes], b3[:, lanes]], axis=0)
+
+            jobs.append((h, two, away, put_away))
+            jobs.append((h, lambda lanes=lanes: b1[:, lanes], near, put_near))
+        run_jobs(jobs, keys, values, 4 * new_rows, factor)
+        o0[:new_rows] = n0[...]
+        for place, out in zip(places, (o0, o1, o2, o3)):
+            part = pl.ds(pl.multiple_of(place * ctx_rows, ctx_rows), ctx_rows)
+            out[new_rows:] = held[part]
+
+
+def cache_kernel(new_rows, a0, a1, a2, a3, order, c0, c1, c2, c3, kk):
+    z = lax.axis_index("seq")
+    ctx_rows = c0.shape[0] // 2
+    rows = new_rows + ctx_rows
+    width = a0.shape[1]
+
+    @pl.when(middle(z))
+    def _():
+        places = far_places(z)
+        for place, src in zip(places, (a0, a1, a2, a3)):
+            to = pl.ds(pl.multiple_of(place * ctx_rows, ctx_rows), ctx_rows)
+            kk[to, :width] = src[new_rows:rows]
+            kk[to, width:] = src[rows + new_rows : 2 * rows]
+        for place, out in zip(places, (c0, c1, c2, c3)):
+            part = pl.ds(pl.multiple_of(place * ctx_rows, ctx_rows), ctx_rows)
+            moved = jnp.dot(order[part], kk[...], preferred_element_type=jnp.float32)
+            out[:ctx_rows] = moved[:, :width].astype(jnp.bfloat16)
+            out[ctx_rows:] = moved[:, width:].astype(jnp.bfloat16)
+
+
+def halves(z, at, *parts):
+    own, beside, across, beyond = (part[at] for part in parts)
+    inner = middle(z)
+    low = z < 2
+    near = jnp.where(inner, own, beside)
+    far = jnp.where(inner, across, beyond)
+    return (jnp.where(low, near, far), jnp.where(low, far, near))
+
+
+def project_kernel(mine, here, o0, o1, o3, o2, weight, out):
+    a, b = halves(lax.axis_index("seq"), slice(None), o0, o1, o2, o3)
+    mixed = jnp.concatenate([a, b], axis=1)
+    width = mixed.shape[1]
+    me = lax.axis_index("tensor")
+    core = me % 2 if mine else 1 - me % 2
+    chip = me // 2 if here else 1 - me // 2
+    lanes = pl.ds(pl.multiple_of((2 * chip + core) * width, width), width)
+    total = jnp.dot(mixed, weight[:, lanes], preferred_element_type=jnp.float32)
+    out[...] = total.astype(out.dtype)
+
+
+def add_kernel(keep, came, out):
+    out[...] = (keep[...] + came[...].astype(jnp.float32)).astype(jnp.bfloat16)
+
+
+def finish_kernel(last, keep, came, out, out_ctx):
+    total = keep[...] + came[...].astype(jnp.float32) + last[...].astype(jnp.float32)
+    total = total.astype(jnp.bfloat16)
+    out[...] = total[: out.shape[0]]
+    out_ctx[...] = total[out.shape[0] :]
+
+
+def store_kernel(c0, c3, c2, c1, keys, values):
+    z = lax.axis_index("seq")
+    ctx_rows, width = keys.shape
+    half = width // 2
+    for i, out in enumerate((keys, values)):
+        at = slice(i * ctx_rows, (i + 1) * ctx_rows)
+        a, b = halves(z, at, c0, c1, c2, c3)
+        out[:, :half] = a
+        out[:, half:] = b
+
+
+SMALL = pl.BlockSpec(memory_space=pltpu.SMEM)
+AWAY = pl.BlockSpec(memory_space=pltpu.HBM)
+WHOLE = pl.BlockSpec(memory_space=pltpu.VMEM)
+LIMIT = pltpu.CompilerParams(vmem_limit_bytes=32 * 1024 * 1024)
+
+
+def lasts(us):
+    return pl.CostEstimate(flops=int(us * 1.1e9), bytes_accessed=0, transcendentals=0)
+
+
+def shape16(*dims):
+    return jax.ShapeDtypeStruct(dims, jnp.bfloat16)
+
+
+def permute(x, pairs):
+    return lax.ppermute(x, "seq", pairs)
+
+
+BESIDE = ((0, 1), (3, 2))
+ACROSS = ((1, 2), (2, 1))
+BEYOND = ((0, 2), (3, 1))
+SIBLING = ((0, 1), (1, 0), (2, 3), (3, 2))
+OPPOSITE = ((0, 2), (2, 0), (1, 3), (3, 1))
+
+
+def back(pairs):
+    return tuple((b, a) for a, b in pairs)
+
+
+def home(own, beside, across, beyond):
+    return (
+        own,
+        permute(beside, back(BESIDE)),
+        permute(across, ACROSS),
+        permute(beyond, back(BEYOND)),
+    )
+
+
+def fast_device(
+    queries,
+    new_keys,
+    new_values,
+    context_queries,
+    context_keys,
+    context_values,
+    levels,
+    frame_mask,
+    owners,
+    out_weight,
+):
+    new_rows, width = queries.shape
+    ctx_rows = context_keys.shape[0]
+    rows = new_rows + ctx_rows
+    half = width // 2
+    devices = lax.axis_size("seq")
+    ctx_all = ctx_rows * devices
+    hdim = HEAD_DIM
+    heads = half // hdim
+    frames_new = frame_mask.shape[0]
+    factor = math.log2(math.e) / math.sqrt(hdim)
+    near_a, near_b, far_a, far_b = pl.pallas_call(
+        pack_kernel,
+        out_shape=(
+            shape16(2 * rows + ctx_rows, half),
+            shape16(new_rows, half),
+            shape16(2 * rows + ctx_rows, half),
+            shape16(new_rows, half),
+        ),
+        in_specs=[AWAY] * 7,
+        out_specs=[WHOLE] * 4,
+        scratch_shapes=[pltpu.SMEM(levels.shape, jnp.int32)]
+        + [pltpu.VMEM((ctx_rows, width), jnp.bfloat16)] * 3
+        + [pltpu.SemaphoreType.DMA((10,))],
+        name="pack",
+    )(levels, queries, new_keys, new_values, context_queries, context_keys, context_values)
+    beside_a = permute(near_a, BESIDE)
+    across_a = permute(far_a, ACROSS)
+    beyond_a = permute(far_a, BEYOND)
+    near_b, far_b = lax.optimization_barrier((near_b, far_b, beside_a))[:2]
+    beside_b = permute(near_b, BESIDE)
+    across_b = permute(far_b, ACROSS)
+    beyond_b = permute(far_b, BEYOND)
+    order, alive, biases = pl.pallas_call(
+        plan_kernel,
+        out_shape=(
+            shape16(ctx_all, ctx_all),
+            jax.ShapeDtypeStruct((ctx_all, hdim), jnp.float32),
+            jax.ShapeDtypeStruct((8, ctx_all), jnp.float32),
+        ),
+        in_specs=[WHOLE, SMALL, SMALL],
+        compiler_params=LIMIT,
+        name="plan", cost_estimate=lasts(1.6),
+    )(owners.reshape(1, -1), levels, frame_mask)
+    keys, values, n0, held = pl.pallas_call(
+        functools.partial(first_kernel, factor, new_rows, frames_new),
+        out_shape=[
+            shape16(rows * devices, half),
+            shape16(heads, rows * devices, 2 * hdim),
+            shape16(new_rows, half),
+            shape16(ctx_all, half),
+        ],
+        compiler_params=LIMIT,
+        name="attend_first",
+        cost_estimate=lasts(4.4),
+    )(near_a, beside_a, across_a, beyond_a, near_b, order, alive, biases)
+    results = pl.pallas_call(
+        functools.partial(second_kernel, factor, frames_new),
+        out_shape=[shape16(rows, half)] * 4,
+        compiler_params=LIMIT,
+        name="attend_second",
+        cost_estimate=lasts(3.0),
+    )(beside_b, across_b, beyond_b, keys, values, biases, n0, held)
+    mixed = home(*results)
+    near_a = lax.optimization_barrier((near_a, results[0]))[0]
+    caches = pl.pallas_call(
+        functools.partial(cache_kernel, new_rows),
+        out_shape=[shape16(2 * ctx_rows, half)] * 4,
+        scratch_shapes=[pltpu.VMEM((ctx_all, width), jnp.bfloat16)],
+        compiler_params=LIMIT,
+        name="caches",
+        cost_estimate=lasts(0.8),
+    )(near_a, beside_a, across_a, beyond_a, order)
+
+    def project(mine, here, dtype):
+        return pl.pallas_call(
+            functools.partial(project_kernel, mine, here),
+            out_shape=jax.ShapeDtypeStruct((rows, width), dtype),
+            in_specs=[WHOLE] * 5,
+            compiler_params=LIMIT,
+            name=("keep" if mine else "give") + ("_here" if here else "_there"),
+            cost_estimate=lasts(0.6),
+        )(mixed[0], mixed[1], mixed[3], mixed[2], out_weight)
+
+    came_there = lax.ppermute(project(False, False, jnp.bfloat16), "tensor", SIBLING)
+    keep_there = project(True, False, jnp.float32)
+    other = pl.pallas_call(
+        add_kernel,
+        out_shape=shape16(rows, width),
+        compiler_params=LIMIT,
+        name="add",
+        cost_estimate=lasts(0.1),
+    )(keep_there, came_there)
+    last = lax.ppermute(other, "tensor", OPPOSITE)
+    caches = lax.optimization_barrier((*caches, other))[:4]
+    beyond = permute(caches[3], back(BEYOND))
+    across = permute(caches[2], ACROSS)
+    beside = permute(caches[1], back(BESIDE))
+    stored = (caches[0], beyond, across, beside)
+    mixed = lax.optimization_barrier((*mixed, other))[:4]
+    came = lax.ppermute(project(False, True, jnp.bfloat16), "tensor", SIBLING)
+    keep = project(True, True, jnp.float32)
+    block_out, context_out = pl.pallas_call(
+        finish_kernel,
+        out_shape=(shape16(new_rows, width), shape16(ctx_rows, width)),
+        compiler_params=LIMIT,
+        name="finish",
+        cost_estimate=lasts(0.9),
+    )(last, keep, came)
+    cache_keys, cache_values = pl.pallas_call(
+        store_kernel,
+        out_shape=(shape16(ctx_rows, width), shape16(ctx_rows, width)),
+        compiler_params=LIMIT,
+        name="store", cost_estimate=lasts(0.8),
+    )(*stored)
+    return (block_out, context_out, cache_keys, cache_values)
+
+
 def solution(mesh):
-    in_specs = (
-        P(("session", "seq"), "tensor"),
-        P(("session", "seq"), "tensor"),
-        P(("session", "seq"), "tensor"),
-        P(("session", "seq"), "tensor"),
-        P(("session", "seq"), "tensor"),
-        P(("session", "seq"), "tensor"),
-        P("session"),
-        P("session", None),
-        P("session"),
-        P("tensor", None),
-    )
-    out_specs = (
-        P(("session", "seq"), "tensor"),
-        P(("session", "seq"), "tensor"),
-        P(("session", "seq"), "tensor"),
-        P(("session", "seq"), "tensor"),
-    )
+    rows = P(("session", "seq"), "tensor")
+    in_specs = (rows,) * 6 + (P("session"), P("session", None), P("session"), P("tensor", None))
+    sizes = mesh.shape
+    step = fast_device if sizes["seq"] == 4 and sizes["tensor"] == 4 else per_device
     return jax.shard_map(
-        per_device, mesh=mesh, in_specs=in_specs, out_specs=out_specs, check_vma=False
-    )
+        step, mesh=mesh, in_specs=in_specs, out_specs=(rows,) * 4, check_vma=False
+    )

time: 171 us -> 82.1 us (0.48)
  blocking collectives: 64.2 us -> 0 us
  local copies, waits for them, and re-layouts: 35.5 us -> 2 us
  waiting for transfers between devices: 13.1 us -> 45.1 us
  matrix products: 18.4 us -> 0 us
  between operations: 14.2 us -> 0.83 us
  starting transfers between devices: 14 us -> 25.3 us
  other arithmetic: 10.7 us -> 0.01 us
  Pallas kernels: 0 us -> 8.47 us
    all_gather x2 -> x0, blocking collectives: 64.2 us -> none  [the longest x1 36.2 us: per_device(): lax.all_gather(flat_k, 'seq', axis=0, tiled=True)]
    ppermute x0 -> x15, waiting for transfers between devices: none -> 45.1 us  [the longest x12 43.9 us: permute(): return lax.ppermute(x, 'seq', pairs)]
    ppermute x0 -> x15, starting transfers between devices: none -> 25.3 us  [the longest x12 23.5 us: permute(): return lax.ppermute(x, 'seq', pairs)]
    dot_general x12 -> x0, matrix products: 18.4 us -> none  [the longest x5 6.8 us: attend(): jnp.einsum('hqk,khd->hqd', weights.astype(jnp.bfloat16), values_h, prefer...]
    all_to_all x3 -> x0, starting transfers between devices: 13.9 us -> none  [the longest x1 6.32 us: per_device(): lax.all_to_all(pack(pooled_q), 'seq', split_axis=0, concat_axis=0, tiled=...]
    scatter x6 -> x0, local copies, waits for them, and re-layouts: 12.5 us -> none  [the longest x3 7.88 us: unpack(): jnp.zeros((blocks_dev, 4, width), arrived.dtype).at[target]]
    all_to_all x3 -> x0, waiting for transfers between devices: 11.7 us -> none  [the longest x1 6.37 us: per_device(): lax.all_to_all(pack(pooled_k), 'seq', split_axis=0, concat_axis=0, tiled=...]
    reshape x19 -> x0, local copies, waits for them, and re-layouts: 10 us -> none  [the longest x3 2.99 us: pool_blocks(): blocks = rows.reshape(-1, 4, rows.shape[-1])]
  transfers between devices with their start and end apart: 6 -> 15, of which waited for: 2 -> 8; matrix products, arithmetic and copies ran while one was open for 20% -> 0% of each run, Pallas kernels for 0% -> 5%
where the time goes in v2:
time: 82.1 us; the launch traced here: 81.8 us
  waiting for transfers between devices  45.1 us (55%)
  starting transfers between devices  25.3 us (31%)
  Pallas kernels  8.47 us (10%)
  local copies, waits for them, and re-layouts  2 us (2%)
  between operations  0.83 us (1%)
    ppermute x12, waiting for transfers between devices, permute(): return lax.ppermute(x, 'seq', pairs)  43.9 us
    ppermute x12, starting transfers between devices, permute(): return lax.ppermute(x, 'seq', pairs)  23.5 us
    pallas_call x1, Pallas kernels, fast_device(): pl.pallas_call(pack_kernel, out_shape=(shape16(2 * rows + ctx_rows, half)...  2.61 us
    pallas_call x4, Pallas kernels, project(): pl.pallas_call(functools.partial(project_kernel, mine, here), out_shape=j...  2.39 us
    unnamed x16, local copies, waits for them, and re-layouts  2 us
    pallas_call x1, Pallas kernels, fast_device(): pl.pallas_call(plan_kernel, out_shape=(shape16(ctx_all, ctx_all), jax.Sha...  1.72 us
  transfers between devices with their start and end apart: 15, of which 8 were waited for; matrix products, arithmetic and copies ran while one was open for 0% of the time, Pallas kernels for 5%

profile of v2, /device:TPU:0, one launch (start us, length us, event | category | flops | bytes accessed | tf_op | source)
XLA Modules:
  0.0 81.8 jit_solution(14557721040078954038)
XLA Ops:
  0.6 2.6 %pack.1 = (bf16[768,384]{1,0:T(8,128)(2,1)}, bf16[192,384]{1,0:T(8,128)(2,1)}, bf16[768,384]{1,0:T(8,128)(2,1)}, bf16[192,384]{1,0:T(8,128)(2,1)}) custom-call(s32[8]{0:T(128)} %levels.3, bf16[192,768]{1,0:T(8,128)(2,1)} %q.1, bf16[192,768]{1,0:T(8,128)(2,1)} %k.1, bf16[192,768]{1,0:T(8,128)(2,1)} %v.1, bf16[128,768]{1,0:T(8,128)(2,1)} %cq.1, ...), custom_call_target="tpu_custom_call" | custom-call | tf_op jit(solution)/shard_map/pack/pallas_call | solution.py:555
  3.3 5.0 %collective-permute-start = (bf16[768,384]{1,0:T(8,128)(2,1)}, bf16[768,384]{1,0:T(8,128)(2,1)S(1)}, u32[]{:S(2)}, u32[]{:S(2)}) collective-permute-start(bf16[768,384]{1,0:T(8,128)(2,1)} %get-tuple-element.61.a0), channel_id=1, source_target_pairs={{0,4},{12,8},{1,5},{13,9},{2,6},{14,10},{3,7},{15,11},{16,20},{28,... | collective-permute-start | bytes 1769480 | tf_op jit(solution)/shard_map/ppermute | solution.py:510
  8.2 2.3 %collective-permute-start.5 = (bf16[768,384]{1,0:T(8,128)(2,1)}, bf16[768,384]{1,0:T(8,128)(2,1)S(1)}, u32[]{:S(2)}, u32[]{:S(2)}) collective-permute-start(bf16[768,384]{1,0:T(8,128)(2,1)} %get-tuple-element.43), channel_id=1, source_target_pairs={{0,8},{12,4},{1,9},{13,5},{2,10},{14,6},{3,11},{15,7},{16,24},{28,... | collective-permute-start | bytes 1769480 | tf_op jit(solution)/shard_map/ppermute | solution.py:510
  10.5 0.7 collective-permute-start.4
  11.2 0.0 copy-start
  11.3 0.6 copy-done
  11.9 0.0 copy-start.3
  11.9 0.7 copy-done.3
  12.6 0.0 copy-start.4
  12.6 0.7 copy-done.4
  13.2 0.0 copy-start.5
  13.2 0.0 copy-start.2
  13.2 0.0 copy-start.1
  13.2 0.0 slice-start
  13.3 1.7 %plan.1 = (bf16[512,512]{1,0:T(8,128)(2,1)S(1)}, f32[512,128]{1,0:T(8,128)S(1)}, f32[8,512]{1,0:T(8,128)S(1)}) custom-call(s32[1,128]{1,0:T(1,128)S(1)} %bitcast.3, s32[8]{0:T(128)S(1)} %copy-done, s32[2,8]{1,0:T(2,128)S(1)} %copy-done.3), custom_call_target="tpu_custom_call" | custom-call | flops 1760000000 | tf_op jit(solution)/shard_map/plan/pallas_call | solution.py:577
  15.0 7.2 %collective-permute-done.a1 = bf16[768,384]{1,0:T(8,128)(2,1)S(1)} collective-permute-done((bf16[768,384]{1,0:T(8,128)(2,1)}, bf16[768,384]{1,0:T(8,128)(2,1)S(1)}, u32[]{:S(2)}, u32[]{:S(2)}) %collective-permute-start) | collective-permute-done | bytes 589856 | tf_op jit(solution)/shard_map/ppermute | solution.py:510
  22.2 0.0 copy-done.5
  22.2 5.3 %collective-permute-start.3 = (bf16[192,384]{1,0:T(8,128)(2,1)S(1)}, bf16[192,384]{1,0:T(8,128)(2,1)S(1)}, u32[]{:S(2)}, u32[]{:S(2)}) collective-permute-start(bf16[192,384]{1,0:T(8,128)(2,1)S(1)} %copy-done.5), channel_id=1, source_target_pairs={{0,8},{12,4},{1,9},{13,5},{2,10},{14,6},{3,11},{15,7},{16,24},{28,... | collective-permute-start | bytes 442376 | tf_op jit(solution)/shard_map/ppermute | solution.py:510
  27.5 0.7 collective-permute-start.2
  28.2 0.0 copy-done.2
  28.2 3.1 %collective-permute-start.1 = (bf16[192,384]{1,0:T(8,128)(2,1)S(1)}, bf16[192,384]{1,0:T(8,128)(2,1)S(1)}, u32[]{:S(2)}, u32[]{:S(2)}) collective-permute-start(bf16[192,384]{1,0:T(8,128)(2,1)S(1)} %copy-done.2), channel_id=1, source_target_pairs={{0,4},{12,8},{1,5},{13,9},{2,6},{14,10},{3,7},{15,11},{16,20},{28,... | collective-permute-start | bytes 442376 | tf_op jit(solution)/shard_map/ppermute | solution.py:510
  31.3 3.6 %collective-permute-done.5.a3 = bf16[768,384]{1,0:T(8,128)(2,1)S(1)} collective-permute-done((bf16[768,384]{1,0:T(8,128)(2,1)}, bf16[768,384]{1,0:T(8,128)(2,1)S(1)}, u32[]{:S(2)}, u32[]{:S(2)}) %collective-permute-start.5) | collective-permute-done | bytes 589856 | tf_op jit(solution)/shard_map/ppermute | solution.py:510
  34.9 0.0 collective-permute-done.4.a2
  34.9 0.0 copy-done.1
  34.9 0.0 slice-start.1
  34.9 5.1 %collective-permute-done.1.b1 = bf16[192,384]{1,0:T(8,128)(2,1)S(1)} collective-permute-done((bf16[192,384]{1,0:T(8,128)(2,1)S(1)}, bf16[192,384]{1,0:T(8,128)(2,1)S(1)}, u32[]{:S(2)}, u32[]{:S(2)}) %collective-permute-start.1) | collective-permute-done | bytes 147488 | tf_op jit(solution)/shard_map/ppermute | solution.py:510
  40.0 0.0 collective-permute-done.3.b3
  40.0 0.0 collective-permute-done.2.b2
  40.0 1.3 %collective-permute-start.6 = (bf16[320,384]{1,0:T(8,128)(2,1)S(1)}, bf16[320,384]{1,0:T(8,128)(2,1)S(1)}, u32[]{:S(2)}, u32[]{:S(2)}) collective-permute-start(bf16[320,384]{1,0:T(8,128)(2,1)S(1)} %get-tuple-element.52), channel_id=1, source_target_pairs={{4,0},{8,12},{5,1},{9,13},{6,2},{10,14},{7,3},{11,15},{20,16},{24,... | collective-permute-start | bytes 737288 | tf_op jit(solution)/shard_map/ppermute | solution.py:510
  41.3 1.3 %collective-permute-start.7 = (bf16[320,384]{1,0:T(8,128)(2,1)S(1)}, bf16[320,384]{1,0:T(8,128)(2,1)S(1)}, u32[]{:S(2)}, u32[]{:S(2)}) collective-permute-start(bf16[320,384]{1,0:T(8,128)(2,1)S(1)} %get-tuple-element.53), channel_id=1, source_target_pairs={{8,0},{4,12},{9,1},{5,13},{10,2},{6,14},{11,3},{7,15},{24,16},{20,... | collective-permute-start | bytes 737288 | tf_op jit(solution)/shard_map/ppermute | solution.py:510
  42.6 0.7 collective-permute-start.8
  43.3 16.9 %collective-permute-done.6.o1 = bf16[320,384]{1,0:T(8,128)(2,1)S(1)} collective-permute-done((bf16[320,384]{1,0:T(8,128)(2,1)S(1)}, bf16[320,384]{1,0:T(8,128)(2,1)S(1)}, u32[]{:S(2)}, u32[]{:S(2)}) %collective-permute-start.6) | collective-permute-done | bytes 245792 | tf_op jit(solution)/shard_map/ppermute | solution.py:510
  60.1 0.3 collective-permute-done.7.o3
  60.5 0.0 collective-permute-done.8.o2
  60.5 0.0 slice-done
  60.5 0.0 slice-done.1
  60.5 0.6 give_there.1
  61.1 0.1 collective-permute-start.9
  61.2 0.6 keep_there.1.keep
  61.8 1.2 %collective-permute-done.9.came = bf16[320,768]{1,0:T(8,128)(2,1)S(1)} collective-permute-done((bf16[320,768]{1,0:T(8,128)(2,1)S(1)}, bf16[320,768]{1,0:T(8,128)(2,1)S(1)}, u32[]{:S(2)}, u32[]{:S(2)}) %collective-permute-start.9) | collective-permute-done | bytes 491552 | tf_op jit(solution)/shard_map/ppermute | solution.py:628
  63.0 0.1 add.1
  63.1 0.6 give_here.1
  63.7 0.2 collective-permute-start.11
  63.9 1.5 %collective-permute-start.10 = (bf16[320,768]{1,0:T(8,128)(2,1)S(1)}, bf16[320,768]{1,0:T(8,128)(2,1)S(1)}, u32[]{:S(2)}, u32[]{:S(2)}) collective-permute-start(bf16[320,768]{1,0:T(8,128)(2,1)S(1)} %add.1), channel_id=1, source_target_pairs={{0,2},{2,0},{1,3},{3,1},{4,6},{6,4},{5,7},{7,5},{8,10},{10,8},{9,1... | collective-permute-start | bytes 1474568 | tf_op jit(solution)/shard_map/ppermute | solution.py:637
  65.5 1.3 %collective-permute-start.12 = (bf16[256,384]{1,0:T(8,128)(2,1)S(1)}, bf16[256,384]{1,0:T(8,128)(2,1)S(1)}, u32[]{:S(2)}, u32[]{:S(2)}) collective-permute-start(bf16[256,384]{1,0:T(8,128)(2,1)S(1)} %get-tuple-element.67), channel_id=1, source_target_pairs={{8,0},{4,12},{9,1},{5,13},{10,2},{6,14},{11,3},{7,15},{24,16},{20,... | collective-permute-start | bytes 589832 | tf_op jit(solution)/shard_map/ppermute | solution.py:510
  66.7 0.7 collective-permute-start.13
  67.4 1.3 %collective-permute-start.14 = (bf16[256,384]{1,0:T(8,128)(2,1)S(1)}, bf16[256,384]{1,0:T(8,128)(2,1)S(1)}, u32[]{:S(2)}, u32[]{:S(2)}) collective-permute-start(bf16[256,384]{1,0:T(8,128)(2,1)S(1)} %get-tuple-element.69), channel_id=1, source_target_pairs={{4,0},{8,12},{5,1},{9,13},{6,2},{10,14},{7,3},{11,15},{20,16},{24,... | collective-permute-start | bytes 589832 | tf_op jit(solution)/shard_map/ppermute | solution.py:510
  68.7 0.6 keep_here.1.keep
  69.3 7.1 %collective-permute-done.12.c3 = bf16[256,384]{1,0:T(8,128)(2,1)S(1)} collective-permute-done((bf16[256,384]{1,0:T(8,128)(2,1)S(1)}, bf16[256,384]{1,0:T(8,128)(2,1)S(1)}, u32[]{:S(2)}, u32[]{:S(2)}) %collective-permute-start.12) | collective-permute-done | bytes 196640 | tf_op jit(solution)/shard_map/ppermute | solution.py:510
  76.4 0.0 collective-permute-done.13.c2
  76.4 3.7 %collective-permute-done.14.c1 = bf16[256,384]{1,0:T(8,128)(2,1)S(1)} collective-permute-done((bf16[256,384]{1,0:T(8,128)(2,1)S(1)}, bf16[256,384]{1,0:T(8,128)(2,1)S(1)}, u32[]{:S(2)}, u32[]{:S(2)}) %collective-permute-start.14) | collective-permute-done | bytes 196640 | tf_op jit(solution)/shard_map/ppermute | solution.py:510
  80.1 0.8 store.1
  80.9 0.0 collective-permute-done.11.came
  80.9 0.0 collective-permute-done.10.last
  80.9 0.9 %finish.1 = (bf16[192,768]{1,0:T(8,128)(2,1)}, bf16[128,768]{1,0:T(8,128)(2,1)}) custom-call(bf16[320,768]{1,0:T(8,128)(2,1)S(1)} %collective-permute-done.10.last, f32[320,768]{1,0:T(8,128)S(1)} %keep_here.1.keep, bf16[320,768]{1,0:T(8,128)(2,1)S(1)} %collective-permute-done.11.came), custom_call_target="tpu_custom_call" | custom-call | flops 990000000 | tf_op jit(solution)/shard_map/finish/pallas_call | solution.py:646
  (4 shorter events, 0.0 us)
Async XLA Ops:
  3.3 19.0 %collective-permute-start = (bf16[768,384]{1,0:T(8,128)(2,1)}, bf16[768,384]{1,0:T(8,128)(2,1)S(1)}, u32[]{:S(2)}, u32[]{:S(2)}) collective-permute-start(bf16[768,384]{1,0:T(8,128)(2,1)} %get-tuple-element.61.a0), channel_id=1, source_target_pairs={{0,4},{12,8},{1,5},{13,9},{2,6},{14,10},{3,7},{15,11},{16,20},{28,... | collective-permute-start | bytes 1769480 | tf_op jit(solution)/shard_map/ppermute | solution.py:510
  8.2 26.7 %collective-permute-start.5 = (bf16[768,384]{1,0:T(8,128)(2,1)}, bf16[768,384]{1,0:T(8,128)(2,1)S(1)}, u32[]{:S(2)}, u32[]{:S(2)}) collective-permute-start(bf16[768,384]{1,0:T(8,128)(2,1)} %get-tuple-element.43), channel_id=1, source_target_pairs={{0,8},{12,4},{1,9},{13,5},{2,10},{14,6},{3,11},{15,7},{16,24},{28,... | collective-permute-start | bytes 1769480 | tf_op jit(solution)/shard_map/ppermute | solution.py:510
  10.5 24.4 %collective-permute-start.4 = (bf16[768,384]{1,0:T(8,128)(2,1)}, bf16[768,384]{1,0:T(8,128)(2,1)S(1)}, u32[]{:S(2)}, u32[]{:S(2)}) collective-permute-start(bf16[768,384]{1,0:T(8,128)(2,1)} %get-tuple-element.43), channel_id=1, source_target_pairs={{4,8},{8,4},{5,9},{9,5},{6,10},{10,6},{7,11},{11,7},{20,24},{24,20... | collective-permute-start | bytes 1769480 | tf_op jit(solution)/shard_map/ppermute | solution.py:510
  11.2 0.7 copy-start
  11.9 0.7 copy-start.3
  12.6 0.7 copy-start.4
  13.2 9.0 %copy-start.5 = (bf16[192,384]{1,0:T(8,128)(2,1)S(1)}, bf16[192,384]{1,0:T(8,128)(2,1)}, u32[]{:S(2)}) copy-start(bf16[192,384]{1,0:T(8,128)(2,1)} %get-tuple-element.42) | copy-start | bytes 442372
  13.2 15.0 %copy-start.2 = (bf16[192,384]{1,0:T(8,128)(2,1)S(1)}, bf16[192,384]{1,0:T(8,128)(2,1)}, u32[]{:S(2)}) copy-start(bf16[192,384]{1,0:T(8,128)(2,1)} %get-tuple-element.41.b0) | copy-start | bytes 442372
  13.2 21.7 %copy-start.1 = (bf16[768,384]{1,0:T(8,128)(2,1)S(1)}, bf16[768,384]{1,0:T(8,128)(2,1)}, u32[]{:S(2)}) copy-start(bf16[768,384]{1,0:T(8,128)(2,1)} %get-tuple-element.61.a0) | copy-start | bytes 1769476
  13.2 47.2 %slice-start = ((s8[4718592]{0:T(1024)(128)(4,1)}), s8[4194304]{0:T(1024)(128)(4,1)S(1)}, s32[]{:S(2)}) async-start(s8[4718592]{0:T(1024)(128)(4,1)} %bitcast.1), calls=%async_computation | async-start | bytes 8388608
  22.2 17.8 %collective-permute-start.3 = (bf16[192,384]{1,0:T(8,128)(2,1)S(1)}, bf16[192,384]{1,0:T(8,128)(2,1)S(1)}, u32[]{:S(2)}, u32[]{:S(2)}) collective-permute-start(bf16[192,384]{1,0:T(8,128)(2,1)S(1)} %copy-done.5), channel_id=1, source_target_pairs={{0,8},{12,4},{1,9},{13,5},{2,10},{14,6},{3,11},{15,7},{16,24},{28,... | collective-permute-start | bytes 442376 | tf_op jit(solution)/shard_map/ppermute | solution.py:510
  27.5 12.5 %collective-permute-start.2 = (bf16[192,384]{1,0:T(8,128)(2,1)S(1)}, bf16[192,384]{1,0:T(8,128)(2,1)S(1)}, u32[]{:S(2)}, u32[]{:S(2)}) collective-permute-start(bf16[192,384]{1,0:T(8,128)(2,1)S(1)} %copy-done.5), channel_id=1, source_target_pairs={{4,8},{8,4},{5,9},{9,5},{6,10},{10,6},{7,11},{11,7},{20,24},{24,20... | collective-permute-start | bytes 442376 | tf_op jit(solution)/shard_map/ppermute | solution.py:510
  28.2 11.8 %collective-permute-start.1 = (bf16[192,384]{1,0:T(8,128)(2,1)S(1)}, bf16[192,384]{1,0:T(8,128)(2,1)S(1)}, u32[]{:S(2)}, u32[]{:S(2)}) collective-permute-start(bf16[192,384]{1,0:T(8,128)(2,1)S(1)} %copy-done.2), channel_id=1, source_target_pairs={{0,4},{12,8},{1,5},{13,9},{2,6},{14,10},{3,7},{15,11},{16,20},{28,... | collective-permute-start | bytes 442376 | tf_op jit(solution)/shard_map/ppermute | solution.py:510
  34.9 25.6 %slice-start.1 = ((s8[4718592]{0:T(1024)(128)(4,1)}), s8[524288]{0:T(1024)(128)(4,1)S(1)}, s32[]{:S(2)}) async-start(s8[4718592]{0:T(1024)(128)(4,1)} %bitcast.1), calls=%async_computation.1 | async-start | bytes 1048576
  40.0 20.2 %collective-permute-start.6 = (bf16[320,384]{1,0:T(8,128)(2,1)S(1)}, bf16[320,384]{1,0:T(8,128)(2,1)S(1)}, u32[]{:S(2)}, u32[]{:S(2)}) collective-permute-start(bf16[320,384]{1,0:T(8,128)(2,1)S(1)} %get-tuple-element.52), channel_id=1, source_target_pairs={{4,0},{8,12},{5,1},{9,13},{6,2},{10,14},{7,3},{11,15},{20,16},{24,... | collective-permute-start | bytes 737288 | tf_op jit(solution)/shard_map/ppermute | solution.py:510
  41.3 19.2 %collective-permute-start.7 = (bf16[320,384]{1,0:T(8,128)(2,1)S(1)}, bf16[320,384]{1,0:T(8,128)(2,1)S(1)}, u32[]{:S(2)}, u32[]{:S(2)}) collective-permute-start(bf16[320,384]{1,0:T(8,128)(2,1)S(1)} %get-tuple-element.53), channel_id=1, source_target_pairs={{8,0},{4,12},{9,1},{5,13},{10,2},{6,14},{11,3},{7,15},{24,16},{20,... | collective-permute-start | bytes 737288 | tf_op jit(solution)/shard_map/ppermute | solution.py:510
  42.6 17.9 %collective-permute-start.8 = (bf16[320,384]{1,0:T(8,128)(2,1)S(1)}, bf16[320,384]{1,0:T(8,128)(2,1)S(1)}, u32[]{:S(2)}, u32[]{:S(2)}) collective-permute-start(bf16[320,384]{1,0:T(8,128)(2,1)S(1)} %get-tuple-element.54), channel_id=1, source_target_pairs={{4,8},{8,4},{5,9},{9,5},{6,10},{10,6},{7,11},{11,7},{20,24},{24,20... | collective-permute-start | bytes 737288 | tf_op jit(solution)/shard_map/ppermute | solution.py:510
  61.1 1.9 %collective-permute-start.9 = (bf16[320,768]{1,0:T(8,128)(2,1)S(1)}, bf16[320,768]{1,0:T(8,128)(2,1)S(1)}, u32[]{:S(2)}, u32[]{:S(2)}) collective-permute-start(bf16[320,768]{1,0:T(8,128)(2,1)S(1)} %give_there.1), channel_id=1, source_target_pairs={{0,1},{1,0},{2,3},{3,2},{4,5},{5,4},{6,7},{7,6},{8,9},{9,8},{10,11... | collective-permute-start | bytes 1474568 | tf_op jit(solution)/shard_map/ppermute | solution.py:628
  63.7 17.1 %collective-permute-start.11 = (bf16[320,768]{1,0:T(8,128)(2,1)S(1)}, bf16[320,768]{1,0:T(8,128)(2,1)S(1)}, u32[]{:S(2)}, u32[]{:S(2)}) collective-permute-start(bf16[320,768]{1,0:T(8,128)(2,1)S(1)} %give_here.1), channel_id=1, source_target_pairs={{0,1},{1,0},{2,3},{3,2},{4,5},{5,4},{6,7},{7,6},{8,9},{9,8},{10,11... | collective-permute-start | bytes 1474568 | tf_op jit(solution)/shard_map/ppermute | solution.py:644
  63.9 17.0 %collective-permute-start.10 = (bf16[320,768]{1,0:T(8,128)(2,1)S(1)}, bf16[320,768]{1,0:T(8,128)(2,1)S(1)}, u32[]{:S(2)}, u32[]{:S(2)}) collective-permute-start(bf16[320,768]{1,0:T(8,128)(2,1)S(1)} %add.1), channel_id=1, source_target_pairs={{0,2},{2,0},{1,3},{3,1},{4,6},{6,4},{5,7},{7,5},{8,10},{10,8},{9,1... | collective-permute-start | bytes 1474568 | tf_op jit(solution)/shard_map/ppermute | solution.py:637
  65.5 11.0 %collective-permute-start.12 = (bf16[256,384]{1,0:T(8,128)(2,1)S(1)}, bf16[256,384]{1,0:T(8,128)(2,1)S(1)}, u32[]{:S(2)}, u32[]{:S(2)}) collective-permute-start(bf16[256,384]{1,0:T(8,128)(2,1)S(1)} %get-tuple-element.67), channel_id=1, source_target_pairs={{8,0},{4,12},{9,1},{5,13},{10,2},{6,14},{11,3},{7,15},{24,16},{20,... | collective-permute-start | bytes 589832 | tf_op jit(solution)/shard_map/ppermute | solution.py:510
  66.7 9.7 %collective-permute-start.13 = (bf16[256,384]{1,0:T(8,128)(2,1)S(1)}, bf16[256,384]{1,0:T(8,128)(2,1)S(1)}, u32[]{:S(2)}, u32[]{:S(2)}) collective-permute-start(bf16[256,384]{1,0:T(8,128)(2,1)S(1)} %get-tuple-element.68), channel_id=1, source_target_pairs={{4,8},{8,4},{5,9},{9,5},{6,10},{10,6},{7,11},{11,7},{20,24},{24,20... | collective-permute-start | bytes 589832 | tf_op jit(solution)/shard_map/ppermute | solution.py:510
  67.4 12.7 %collective-permute-start.14 = (bf16[256,384]{1,0:T(8,128)(2,1)S(1)}, bf16[256,384]{1,0:T(8,128)(2,1)S(1)}, u32[]{:S(2)}, u32[]{:S(2)}) collective-permute-start(bf16[256,384]{1,0:T(8,128)(2,1)S(1)} %get-tuple-element.69), channel_id=1, source_target_pairs={{4,0},{8,12},{5,1},{9,13},{6,2},{10,14},{7,3},{11,15},{20,16},{24,... | collective-permute-start | bytes 589832 | tf_op jit(solution)/shard_map/ppermute | solution.py:510

commit v3 on v2

--- a/solution.py
+++ b/solution.py
@@ -223,42 +223,52 @@
     return coarse
 
 
-def pack_kernel(levels, q, k, v, cq, ck, cv, near_a, near_b, far_a, far_b, lv, sq, sk, sv, sems):
+def pack_kernel(
+    levels, q, k, v, cq, ck, cv, near_a, near_b, far_a, far_b, lv, sk, sv, sq, sems
+):
     z = lax.axis_index("seq")
     devices = lax.axis_size("seq")
     new_rows, width = q.shape
     ctx_rows = cq.shape[0]
     half = width // 2
+    most = near_a.shape[1]
     rows = new_rows + ctx_rows
     frames_ctx = levels.shape[0]
     low = jnp.where(z < devices // 2, 0, half)
-    near_lanes = pl.ds(pl.multiple_of(low, 128), half)
-    far_lanes = pl.ds(pl.multiple_of(half - low, 128), half)
-    pairs = [(levels, lv), (ck, sk), (cv, sv), (cq, sq)]
-    for out_a, out_b, lanes in ((far_a, far_b, far_lanes), (near_a, near_b, near_lanes)):
-        pairs.append((k.at[:, lanes], out_a.at[0:new_rows]))
-        pairs.append((v.at[:, lanes], out_a.at[rows : rows + new_rows]))
-        pairs.append((q.at[:, lanes], out_b))
-    copies = [pltpu.make_async_copy(src, dst, sems.at[i]) for i, (src, dst) in enumerate(pairs)]
-    for copy in copies:
+    places = (
+        (far_a, half - low, most),
+        (near_a, low, most),
+        (far_b, half - low + most, half - most),
+        (near_b, low + most, half - most),
+    )
+    places = [(out, pl.ds(pl.multiple_of(at, 128), size)) for out, at, size in places]
+    started = []
+
+    def start(src, dst):
+        copy = pltpu.make_async_copy(src, dst, sems.at[len(started)])
         copy.start()
+        started.append(copy)
+        return copy
+
+    reads = [start(levels, lv), start(ck, sk), start(cv, sv), start(cq, sq)]
+    for out, lanes in places:
+        for part, fresh in enumerate((k, v, q)):
+            start(fresh.at[:, lanes], out.at[part * rows : part * rows + new_rows])
+    reads[0].wait()
     index = place_index((ctx_rows, 1), 0)
     first = index % 4 == 0
-    copies[0].wait()
     frame = (z * ctx_rows + index) * frames_ctx // (devices * ctx_rows)
     coarse = coarse_of(frame, lv, frames_ctx)
-    for part, (ref, copy) in enumerate(((sk, copies[1]), (sv, copies[2]), (sq, copies[3]))):
-        copy.wait()
-        at = slice(part * rows + new_rows, (part + 1) * rows)
-        if part == 2:
-            at = slice(2 * rows, 2 * rows + ctx_rows)
-        for out, lanes in ((far_a, far_lanes), (near_a, near_lanes)):
-            wide = ref[:, lanes].astype(jnp.float32)
-            pair = wide + pltpu.roll(wide, ctx_rows - 1, 0)
-            quad = pair + pltpu.roll(pair, ctx_rows - 2, 0)
-            mean = jnp.where(first, quad * 0.25, 0.0)
-            out[at] = jnp.where(coarse, mean, wide).astype(jnp.bfloat16)
-    for copy in copies[4:]:
+    for part, src in enumerate((sk, sv, sq)):
+        reads[part + 1].wait()
+        wide = src[...].astype(jnp.float32)
+        pair = wide + pltpu.roll(wide, ctx_rows - 1, 0)
+        quad = pair + pltpu.roll(pair, ctx_rows - 2, 0)
+        mean = jnp.where(first, quad * 0.25, 0.0)
+        src[...] = jnp.where(coarse, mean, wide).astype(jnp.bfloat16)
+        for out, lanes in places:
+            out[part * rows + new_rows : (part + 1) * rows] = src[:, lanes]
+    for copy in started[4:]:
         copy.wait()
 
 
@@ -346,107 +356,112 @@
         held = None if job is None else (*job, scores)
 
 
+def gather_heads(places, sources, ctx_rows, keys, values, qn, qc):
+    rows = sources[0].shape[0] // 3
+    new_rows = rows - ctx_rows
+    fresh = len(sources) * new_rows
+    heads = values.shape[0]
+    hdim = values.shape[2] // 2
+    values[:, :, hdim:] = jnp.ones((heads, values.shape[1], hdim), jnp.bfloat16)
+    for place, src in zip(places, sources):
+        at = pl.ds(pl.multiple_of(place * new_rows, new_rows), new_rows)
+        spot = pl.ds(pl.multiple_of(place * ctx_rows, ctx_rows), ctx_rows)
+        to = pl.ds(pl.multiple_of(fresh + place * ctx_rows, ctx_rows), ctx_rows)
+        keys[at] = src[0:new_rows]
+        keys[to] = src[new_rows:rows]
+        qn[at] = src[2 * rows : 2 * rows + new_rows]
+        qc[spot] = src[2 * rows + new_rows : 3 * rows]
+        for h in range(heads):
+            lanes = slice(h * hdim, (h + 1) * hdim)
+            values[h, at, :hdim] = src[rows : rows + new_rows, lanes]
+            values[h, to, :hdim] = src[rows + new_rows : 2 * rows, lanes]
+
+
+def attend_heads(factor, frames_new, order, alive, biases, keys, values, qn, qc):
+    heads = values.shape[0]
+    hdim = values.shape[2] // 2
+    fresh = qn.shape[0]
+    per = fresh // frames_new
+    qc[...] = jnp.dot(order[...], qc[...], preferred_element_type=jnp.float32).astype(
+        jnp.bfloat16
+    )
+    jobs = []
+    for h in range(heads):
+        lanes = slice(h * hdim, (h + 1) * hdim)
+        for g in range(frames_new):
+            at = slice(g * per, (g + 1) * per)
+
+            def put_new(r, at=at, lanes=lanes):
+                qn[at, lanes] = r.astype(jnp.bfloat16)
+
+            jobs.append(
+                (h, lambda at=at, lanes=lanes: qn[at, lanes], biases[g + 1 : g + 2], put_new)
+            )
+
+        def put_ctx(r, lanes=lanes):
+            qc[:, lanes] = (r * alive[...]).astype(jnp.bfloat16)
+
+        jobs.append((h, lambda lanes=lanes: qc[:, lanes], biases[0:1], put_ctx))
+    run_jobs(jobs, keys, values, fresh, factor)
+
+
 def first_kernel(
-    factor, new_rows, frames_new,
-    a0, a1, a2, a3, b0, order, alive, biases,
-    keys, values, n0, qc,
+    factor, frames_new, a0, a1, a2, a3, order, alive, biases, qn, qc, keys, values
+):
+    z = lax.axis_index("seq")
+
+    @pl.when(middle(z))
+    def _():
+        gather_heads(far_places(z), (a0, a1, a2, a3), qc.shape[0] // 4, keys, values, qn, qc)
+        attend_heads(factor, frames_new, order, alive, biases, keys, values, qn, qc)
+
+
+def second_kernel(
+    factor, frames_new, b0, b3, b2, b1, order, alive, biases, fn, fc,
+    o0, o1, o2, o3, keys, values, qn, qc,
 ):
     z = lax.axis_index("seq")
     ctx_rows = qc.shape[0] // 4
-    rows = new_rows + ctx_rows
-    fresh = 4 * new_rows
-    heads = values.shape[0]
-    hdim = values.shape[2] // 2
+    new_rows = qn.shape[0] // 4
+    most = fn.shape[1]
 
     @pl.when(middle(z))
     def _():
         places = far_places(z)
-        values[:, :, hdim:] = jnp.ones((heads, values.shape[1], hdim), jnp.bfloat16)
-        for i, src in enumerate((a0, a1, a2, a3)):
-            at = slice(i * new_rows, (i + 1) * new_rows)
-            spot = pl.multiple_of(places[i] * ctx_rows, ctx_rows)
-            to = pl.ds(fresh + spot, ctx_rows)
-            keys[at] = src[0:new_rows]
-            keys[to] = src[new_rows:rows]
-            for h in range(heads):
-                lanes = slice(h * hdim, (h + 1) * hdim)
-                values[h, at, :hdim] = src[rows : rows + new_rows, lanes]
-                values[h, to, :hdim] = src[rows + new_rows : 2 * rows, lanes]
-            qc[pl.ds(spot, ctx_rows)] = src[2 * rows : 2 * rows + ctx_rows]
-        qc[...] = jnp.dot(order[...], qc[...], preferred_element_type=jnp.float32).astype(
-            jnp.bfloat16
-        )
-        mine = biases[pl.ds(1 + z * frames_new // 4, 1)]
-        jobs = []
-        for h in range(heads):
-            lanes = slice(h * hdim, (h + 1) * hdim)
-
-            def put_ctx(r, lanes=lanes):
-                qc[:, lanes] = (r * alive[...]).astype(jnp.bfloat16)
-
-            def put_new(r, lanes=lanes):
-                n0[:, lanes] = r.astype(jnp.bfloat16)
-
-            jobs.append((h, lambda lanes=lanes: qc[:, lanes], biases[0:1], put_ctx))
-            jobs.append((h, lambda lanes=lanes: b0[:, lanes], mine, put_new))
-        run_jobs(jobs, keys, values, fresh, factor)
-
-
-def second_kernel(
-    factor, frames_new, b1, b2, b3, keys, values, biases, n0, held, o0, o1, o2, o3
+        gather_heads(places, (b0, b1, b2, b3), ctx_rows, keys, values, qn, qc)
+        attend_heads(factor, frames_new, order, alive, biases, keys, values, qn, qc)
+        for place, out in zip(places, (o0, o1, o2, o3)):
+            at = pl.ds(pl.multiple_of(place * new_rows, new_rows), new_rows)
+            part = pl.ds(pl.multiple_of(place * ctx_rows, ctx_rows), ctx_rows)
+            out[:new_rows, :most] = fn[at]
+            out[:new_rows, most:] = qn[at]
+            out[new_rows:, :most] = fc[part]
+            out[new_rows:, most:] = qc[part]
+
+
+def cache_kernel(
+    a0, a1, a2, a3, b0, b1, b2, b3, order, c0, c1, c2, c3, kk
 ):
     z = lax.axis_index("seq")
-    new_rows = b1.shape[0]
-    ctx_rows = held.shape[0] // 4
-    heads = values.shape[0]
-    hdim = values.shape[2] // 2
+    ctx_rows, half = c0.shape[0] // 2, c0.shape[1]
+    rows = a0.shape[0] // 3
+    new_rows = rows - ctx_rows
+    most = a0.shape[1]
 
     @pl.when(middle(z))
     def _():
         places = far_places(z)
-        near = biases[pl.ds(1 + places[1] * frames_new // 4, 1)]
-        away = biases[pl.ds(1 + places[2] * frames_new // 4, 1)]
-        jobs = []
-        for h in range(heads):
-            lanes = slice(h * hdim, (h + 1) * hdim)
-
-            def put_near(r, lanes=lanes):
-                o1[:new_rows, lanes] = r.astype(jnp.bfloat16)
-
-            def put_away(r, lanes=lanes):
-                o2[:new_rows, lanes] = r[:new_rows].astype(jnp.bfloat16)
-                o3[:new_rows, lanes] = r[new_rows:].astype(jnp.bfloat16)
-
-            def two(lanes=lanes):
-                return jnp.concatenate([b2[:, lanes], b3[:, lanes]], axis=0)
-
-            jobs.append((h, two, away, put_away))
-            jobs.append((h, lambda lanes=lanes: b1[:, lanes], near, put_near))
-        run_jobs(jobs, keys, values, 4 * new_rows, factor)
-        o0[:new_rows] = n0[...]
-        for place, out in zip(places, (o0, o1, o2, o3)):
-            part = pl.ds(pl.multiple_of(place * ctx_rows, ctx_rows), ctx_rows)
-            out[new_rows:] = held[part]
-
-
-def cache_kernel(new_rows, a0, a1, a2, a3, order, c0, c1, c2, c3, kk):
-    z = lax.axis_index("seq")
-    ctx_rows = c0.shape[0] // 2
-    rows = new_rows + ctx_rows
-    width = a0.shape[1]
-
-    @pl.when(middle(z))
-    def _():
-        places = far_places(z)
-        for place, src in zip(places, (a0, a1, a2, a3)):
+        for place, a, b in zip(places, (a0, a1, a2, a3), (b0, b1, b2, b3)):
             to = pl.ds(pl.multiple_of(place * ctx_rows, ctx_rows), ctx_rows)
-            kk[to, :width] = src[new_rows:rows]
-            kk[to, width:] = src[rows + new_rows : 2 * rows]
+            for part in range(2):
+                at = slice(part * rows + new_rows, (part + 1) * rows)
+                kk[to, part * half : part * half + most] = a[at]
+                kk[to, part * half + most : (part + 1) * half] = b[at]
         for place, out in zip(places, (c0, c1, c2, c3)):
             part = pl.ds(pl.multiple_of(place * ctx_rows, ctx_rows), ctx_rows)
             moved = jnp.dot(order[part], kk[...], preferred_element_type=jnp.float32)
-            out[:ctx_rows] = moved[:, :width].astype(jnp.bfloat16)
-            out[ctx_rows:] = moved[:, width:].astype(jnp.bfloat16)
+            out[:ctx_rows] = moved[:, :half].astype(jnp.bfloat16)
+            out[ctx_rows:] = moved[:, half:].astype(jnp.bfloat16)
 
 
 def halves(z, at, *parts):
@@ -474,22 +489,19 @@
     out[...] = (keep[...] + came[...].astype(jnp.float32)).astype(jnp.bfloat16)
 
 
-def finish_kernel(last, keep, came, out, out_ctx):
+def finish_kernel(last, keep, came, c0, c3, c1, c2, out, out_ctx, keys, values):
     total = keep[...] + came[...].astype(jnp.float32) + last[...].astype(jnp.float32)
     total = total.astype(jnp.bfloat16)
     out[...] = total[: out.shape[0]]
     out_ctx[...] = total[out.shape[0] :]
-
-
-def store_kernel(c0, c3, c2, c1, keys, values):
     z = lax.axis_index("seq")
     ctx_rows, width = keys.shape
     half = width // 2
-    for i, out in enumerate((keys, values)):
+    for i, part in enumerate((keys, values)):
         at = slice(i * ctx_rows, (i + 1) * ctx_rows)
         a, b = halves(z, at, c0, c1, c2, c3)
-        out[:, :half] = a
-        out[:, half:] = b
+        part[:, :half] = a
+        part[:, half:] = b
 
 
 SMALL = pl.BlockSpec(memory_space=pltpu.SMEM)
@@ -549,28 +561,27 @@
     devices = lax.axis_size("seq")
     ctx_all = ctx_rows * devices
     hdim = HEAD_DIM
-    heads = half // hdim
     frames_new = frame_mask.shape[0]
     factor = math.log2(math.e) / math.sqrt(hdim)
+    most = max(hdim, half - hdim)
     near_a, near_b, far_a, far_b = pl.pallas_call(
         pack_kernel,
         out_shape=(
-            shape16(2 * rows + ctx_rows, half),
-            shape16(new_rows, half),
-            shape16(2 * rows + ctx_rows, half),
-            shape16(new_rows, half),
+            shape16(3 * rows, most),
+            shape16(3 * rows, half - most),
+            shape16(3 * rows, most),
+            shape16(3 * rows, half - most),
         ),
         in_specs=[AWAY] * 7,
         out_specs=[WHOLE] * 4,
         scratch_shapes=[pltpu.SMEM(levels.shape, jnp.int32)]
         + [pltpu.VMEM((ctx_rows, width), jnp.bfloat16)] * 3
-        + [pltpu.SemaphoreType.DMA((10,))],
+        + [pltpu.SemaphoreType.DMA((16,))],
         name="pack",
     )(levels, queries, new_keys, new_values, context_queries, context_keys, context_values)
     beside_a = permute(near_a, BESIDE)
     across_a = permute(far_a, ACROSS)
     beyond_a = permute(far_a, BEYOND)
-    near_b, far_b = lax.optimization_barrier((near_b, far_b, beside_a))[:2]
     beside_b = permute(near_b, BESIDE)
     across_b = permute(far_b, ACROSS)
     beyond_b = permute(far_b, BEYOND)
@@ -585,35 +596,48 @@
         compiler_params=LIMIT,
         name="plan", cost_estimate=lasts(1.6),
     )(owners.reshape(1, -1), levels, frame_mask)
-    keys, values, n0, held = pl.pallas_call(
-        functools.partial(first_kernel, factor, new_rows, frames_new),
-        out_shape=[
-            shape16(rows * devices, half),
-            shape16(heads, rows * devices, 2 * hdim),
-            shape16(new_rows, half),
-            shape16(ctx_all, half),
-        ],
+    def scratch(lanes):
+        return [
+            pltpu.VMEM((rows * devices, lanes), jnp.bfloat16),
+            pltpu.VMEM((lanes // hdim, rows * devices, 2 * hdim), jnp.bfloat16),
+        ]
+
+    fresh, held = pl.pallas_call(
+        functools.partial(first_kernel, factor, frames_new),
+        out_shape=[shape16(new_rows * devices, most), shape16(ctx_all, most)],
+        scratch_shapes=scratch(most),
         compiler_params=LIMIT,
         name="attend_first",
-        cost_estimate=lasts(4.4),
-    )(near_a, beside_a, across_a, beyond_a, near_b, order, alive, biases)
+        cost_estimate=lasts(4.8),
+    )(near_a, beside_a, across_a, beyond_a, order, alive, biases)
     results = pl.pallas_call(
         functools.partial(second_kernel, factor, frames_new),
         out_shape=[shape16(rows, half)] * 4,
+        scratch_shapes=scratch(half - most)
+        + [
+            pltpu.VMEM((new_rows * devices, half - most), jnp.bfloat16),
+            pltpu.VMEM((ctx_all, half - most), jnp.bfloat16),
+        ],
         compiler_params=LIMIT,
         name="attend_second",
-        cost_estimate=lasts(3.0),
-    )(beside_b, across_b, beyond_b, keys, values, biases, n0, held)
+        cost_estimate=lasts(2.4),
+    )(near_b, beyond_b, across_b, beside_b, order, alive, biases, fresh, held)
     mixed = home(*results)
     near_a = lax.optimization_barrier((near_a, results[0]))[0]
     caches = pl.pallas_call(
-        functools.partial(cache_kernel, new_rows),
+        cache_kernel,
         out_shape=[shape16(2 * ctx_rows, half)] * 4,
         scratch_shapes=[pltpu.VMEM((ctx_all, width), jnp.bfloat16)],
         compiler_params=LIMIT,
         name="caches",
         cost_estimate=lasts(0.8),
-    )(near_a, beside_a, across_a, beyond_a, order)
+    )(near_a, beside_a, across_a, beyond_a, near_b, beside_b, across_b, beyond_b, order)
+
+    own, beside, across, beyond = mixed
+    own, beside, beyond, across = lax.optimization_barrier(
+        (own, beside, beyond, across, caches[0])
+    )[:4]
+    mixed = (own, beside, across, beyond)
 
     def project(mine, here, dtype):
         return pl.pallas_call(
@@ -625,7 +649,8 @@
             cost_estimate=lasts(0.6),
         )(mixed[0], mixed[1], mixed[3], mixed[2], out_weight)
 
-    came_there = lax.ppermute(project(False, False, jnp.bfloat16), "tensor", SIBLING)
+    give_there = project(False, False, jnp.bfloat16)
+    came_there = lax.ppermute(give_there, "tensor", SIBLING)
     keep_there = project(True, False, jnp.float32)
     other = pl.pallas_call(
         add_kernel,
@@ -639,23 +664,22 @@
     beyond = permute(caches[3], back(BEYOND))
     across = permute(caches[2], ACROSS)
     beside = permute(caches[1], back(BESIDE))
-    stored = (caches[0], beyond, across, beside)
-    mixed = lax.optimization_barrier((*mixed, other))[:4]
+    stored = (caches[0], beyond, beside, across)
+    mixed = lax.optimization_barrier((*mixed, keep_there))[:4]
     came = lax.ppermute(project(False, True, jnp.bfloat16), "tensor", SIBLING)
     keep = project(True, True, jnp.float32)
-    block_out, context_out = pl.pallas_call(
+    block_out, context_out, cache_keys, cache_values = pl.pallas_call(
         finish_kernel,
-        out_shape=(shape16(new_rows, width), shape16(ctx_rows, width)),
+        out_shape=(
+            shape16(new_rows, width),
+            shape16(ctx_rows, width),
+            shape16(ctx_rows, width),
+            shape16(ctx_rows, width),
+        ),
         compiler_params=LIMIT,
         name="finish",
-        cost_estimate=lasts(0.9),
-    )(last, keep, came)
-    cache_keys, cache_values = pl.pallas_call(
-        store_kernel,
-        out_shape=(shape16(ctx_rows, width), shape16(ctx_rows, width)),
-        compiler_params=LIMIT,
-        name="store", cost_estimate=lasts(0.8),
-    )(*stored)
+        cost_estimate=lasts(1.0),
+    )(last, keep, came, *stored)
     return (block_out, context_out, cache_keys, cache_values)
 
 

time: 82.1 us -> 78.5 us (0.956)
  waiting for transfers between devices: 45.1 us -> 39.3 us
  starting transfers between devices: 25.3 us -> 27.4 us
    ppermute x12, waiting for transfers between devices: 43.9 us -> 39.2 us  [permute(): return lax.ppermute(x, 'seq', pairs)]
    ppermute x12, starting transfers between devices: 23.5 us -> 25.2 us  [permute(): return lax.ppermute(x, 'seq', pairs)]
    ppermute x1, waiting for transfers between devices: 1.24 us -> 0.08 us  [fast_device(): came_there = lax.ppermute(give_there, 'tensor', SIBLING)]
    pallas_call x4 -> x3, Pallas kernels: 3.42 us -> 3.3 us  [the longest x1 3.1 us: fast_device(): pl.pallas_call(pack_kernel, out_shape=(shape16(3 * rows, most), shape16(3...]
    unnamed x16 -> x14, local copies, waits for them, and re-layouts: 2 us -> 2 us
  transfers between devices with their start and end apart: 15 -> 15, of which waited for: 8 -> 7; matrix products, arithmetic and copies ran while one was open for 0% -> 0% of each run, Pallas kernels for 5% -> 5%
where the time goes in v3:
time: 78.5 us; the launch traced here: 78.1 us
  waiting for transfers between devices  39.3 us (50%)
  starting transfers between devices  27.4 us (35%)
  Pallas kernels  8.52 us (11%)
  local copies, waits for them, and re-layouts  2 us (3%)
  between operations  0.88 us (1%)
    ppermute x12, waiting for transfers between devices, permute(): return lax.ppermute(x, 'seq', pairs)  39.2 us
    ppermute x12, starting transfers between devices, permute(): return lax.ppermute(x, 'seq', pairs)  25.2 us
    pallas_call x1, Pallas kernels, fast_device(): pl.pallas_call(pack_kernel, out_shape=(shape16(3 * rows, most), shape16(3...  3.1 us
    pallas_call x4, Pallas kernels, project(): pl.pallas_call(functools.partial(project_kernel, mine, here), out_shape=j...  2.38 us
    unnamed x14, local copies, waits for them, and re-layouts  2 us
    pallas_call x1, Pallas kernels, fast_device(): pl.pallas_call(plan_kernel, out_shape=(shape16(ctx_all, ctx_all), jax.Sha...  1.72 us
  transfers between devices with their start and end apart: 15, of which 7 were waited for; matrix products, arithmetic and copies ran while one was open for 0% of the time, Pallas kernels for 5%

profile of v3, /device:TPU:0, one launch (start us, length us, event | category | flops | bytes accessed | tf_op | source)
XLA Modules:
  0.0 78.1 jit_solution(3533556011601182235)
XLA Ops:
  0.6 3.1 %pack.1 = (bf16[960,256]{1,0:T(8,128)(2,1)}, bf16[960,128]{1,0:T(8,128)(2,1)}, bf16[960,256]{1,0:T(8,128)(2,1)}, bf16[960,128]{1,0:T(8,128)(2,1)}) custom-call(s32[8]{0:T(128)} %levels.3, bf16[192,768]{1,0:T(8,128)(2,1)} %q.1, bf16[192,768]{1,0:T(8,128)(2,1)} %k.1, bf16[192,768]{1,0:T(8,128)(2,1)} %v.1, bf16[128,768]{1,0:T(8,128)(2,1)} %cq.1, ...), custom_call_target="tpu_custom_call" | custom-call | tf_op jit(solution)/shard_map/pack/pallas_call | solution.py:567
  3.7 0.0 copy-start.1
  3.8 0.0 copy-start
  3.8 6.1 %collective-permute-start.5 = (bf16[960,256]{1,0:T(8,128)(2,1)}, bf16[960,256]{1,0:T(8,128)(2,1)S(1)}, u32[]{:S(2)}, u32[]{:S(2)}) collective-permute-start(bf16[960,256]{1,0:T(8,128)(2,1)} %get-tuple-element.40), channel_id=1, source_target_pairs={{0,8},{12,4},{1,9},{13,5},{2,10},{14,6},{3,11},{15,7},{16,24},{28,... | collective-permute-start | bytes 1474568 | tf_op jit(solution)/shard_map/ppermute | solution.py:522
  9.9 0.7 collective-permute-start.4
  10.6 3.1 %collective-permute-start.3 = (bf16[960,256]{1,0:T(8,128)(2,1)}, bf16[960,256]{1,0:T(8,128)(2,1)S(1)}, u32[]{:S(2)}, u32[]{:S(2)}) collective-permute-start(bf16[960,256]{1,0:T(8,128)(2,1)} %get-tuple-element.47.a0), channel_id=1, source_target_pairs={{0,4},{12,8},{1,5},{13,9},{2,6},{14,10},{3,7},{15,11},{16,20},{28,... | collective-permute-start | bytes 1474568 | tf_op jit(solution)/shard_map/ppermute | solution.py:522
  13.6 0.7 collective-permute-start.1
  14.3 4.0 %collective-permute-start = (bf16[960,128]{1,0:T(8,128)(2,1)}, bf16[960,128]{1,0:T(8,128)(2,1)S(1)}, u32[]{:S(2)}, u32[]{:S(2)}) collective-permute-start(bf16[960,128]{1,0:T(8,128)(2,1)} %get-tuple-element.35), channel_id=1, source_target_pairs={{0,8},{12,4},{1,9},{13,5},{2,10},{14,6},{3,11},{15,7},{16,24},{28,... | collective-permute-start | bytes 737288 | tf_op jit(solution)/shard_map/ppermute | solution.py:522
  18.3 0.0 copy-start.2
  18.3 0.6 copy-done.2
  19.0 0.0 copy-start.3
  19.0 0.7 copy-done.3
  19.6 0.0 copy-start.4
  19.6 0.7 copy-done.4
  20.3 1.7 %plan.1 = (bf16[512,512]{1,0:T(8,128)(2,1)S(1)}, f32[512,128]{1,0:T(8,128)S(1)}, f32[8,512]{1,0:T(8,128)S(1)}) custom-call(s32[1,128]{1,0:T(1,128)S(1)} %bitcast.3, s32[8]{0:T(128)S(1)} %copy-done.2, s32[2,8]{1,0:T(2,128)S(1)} %copy-done.3), custom_call_target="tpu_custom_call" | custom-call | flops 1760000000 | tf_op jit(solution)/shard_map/plan/pallas_call | solution.py:588
  22.0 0.0 collective-permute-done.5.a3
  22.0 0.0 copy-done.1
  22.0 3.9 %collective-permute-start.2 = (bf16[960,128]{1,0:T(8,128)(2,1)S(1)}, bf16[960,128]{1,0:T(8,128)(2,1)S(1)}, u32[]{:S(2)}, u32[]{:S(2)}) collective-permute-start(bf16[960,128]{1,0:T(8,128)(2,1)S(1)} %copy-done.1), channel_id=1, source_target_pairs={{0,4},{12,8},{1,5},{13,9},{2,6},{14,10},{3,7},{15,11},{16,20},{28,... | collective-permute-start | bytes 737288 | tf_op jit(solution)/shard_map/ppermute | solution.py:522
  26.0 0.0 collective-permute-done.4.a2
  26.0 6.3 %collective-permute-done.3.a1 = bf16[960,256]{1,0:T(8,128)(2,1)S(1)} collective-permute-done((bf16[960,256]{1,0:T(8,128)(2,1)}, bf16[960,256]{1,0:T(8,128)(2,1)S(1)}, u32[]{:S(2)}, u32[]{:S(2)}) %collective-permute-start.3) | collective-permute-done | bytes 491552 | tf_op jit(solution)/shard_map/ppermute | solution.py:522
  32.3 0.0 copy-done
  32.3 0.0 collective-permute-done.1.b2
  32.3 5.3 %collective-permute-done.b3 = bf16[960,128]{1,0:T(8,128)(2,1)S(1)} collective-permute-done((bf16[960,128]{1,0:T(8,128)(2,1)}, bf16[960,128]{1,0:T(8,128)(2,1)S(1)}, u32[]{:S(2)}, u32[]{:S(2)}) %collective-permute-start) | collective-permute-done | bytes 245792 | tf_op jit(solution)/shard_map/ppermute | solution.py:522
  37.6 4.0 %collective-permute-done.2.b1 = bf16[960,128]{1,0:T(8,128)(2,1)S(1)} collective-permute-done((bf16[960,128]{1,0:T(8,128)(2,1)S(1)}, bf16[960,128]{1,0:T(8,128)(2,1)S(1)}, u32[]{:S(2)}, u32[]{:S(2)}) %collective-permute-start.2) | collective-permute-done | bytes 245792 | tf_op jit(solution)/shard_map/ppermute | solution.py:522
  41.7 0.0 slice-start
  41.7 0.0 slice-start.1
  41.7 1.5 %collective-permute-start.6 = (bf16[320,384]{1,0:T(8,128)(2,1)S(1)}, bf16[320,384]{1,0:T(8,128)(2,1)S(1)}, u32[]{:S(2)}, u32[]{:S(2)}) collective-permute-start(bf16[320,384]{1,0:T(8,128)(2,1)S(1)} %get-tuple-element.44), channel_id=1, source_target_pairs={{4,0},{8,12},{5,1},{9,13},{6,2},{10,14},{7,3},{11,15},{20,16},{24,... | collective-permute-start | bytes 737288 | tf_op jit(solution)/shard_map/ppermute | solution.py:522
  43.2 1.3 %collective-permute-start.7 = (bf16[320,384]{1,0:T(8,128)(2,1)S(1)}, bf16[320,384]{1,0:T(8,128)(2,1)S(1)}, u32[]{:S(2)}, u32[]{:S(2)}) collective-permute-start(bf16[320,384]{1,0:T(8,128)(2,1)S(1)} %get-tuple-element.45), channel_id=1, source_target_pairs={{8,0},{4,12},{9,1},{5,13},{10,2},{6,14},{11,3},{7,15},{24,16},{20,... | collective-permute-start | bytes 737288 | tf_op jit(solution)/shard_map/ppermute | solution.py:522
  44.5 0.7 collective-permute-start.8
  45.2 0.2 caches.1
  45.4 13.8 %collective-permute-done.6.o1 = bf16[320,384]{1,0:T(8,128)(2,1)S(1)} collective-permute-done((bf16[320,384]{1,0:T(8,128)(2,1)S(1)}, bf16[320,384]{1,0:T(8,128)(2,1)S(1)}, u32[]{:S(2)}, u32[]{:S(2)}) %collective-permute-start.6) | collective-permute-done | bytes 245792 | tf_op jit(solution)/shard_map/ppermute | solution.py:522
  59.2 0.0 collective-permute-done.7.o3
  59.2 0.0 collective-permute-done.8.o2
  59.2 0.0 slice-done
  59.2 0.0 slice-done.1
  59.2 0.6 give_there.1
  59.8 0.1 collective-permute-start.9
  59.9 0.6 keep_there.1.keep
  60.5 0.6 give_here.1
  61.1 0.6 collective-permute-start.11
  61.7 0.1 collective-permute-done.9.came
  61.8 0.1 add.1
  61.9 1.5 %collective-permute-start.10 = (bf16[320,768]{1,0:T(8,128)(2,1)S(1)}, bf16[320,768]{1,0:T(8,128)(2,1)S(1)}, u32[]{:S(2)}, u32[]{:S(2)}) collective-permute-start(bf16[320,768]{1,0:T(8,128)(2,1)S(1)} %add.1), channel_id=1, source_target_pairs={{0,2},{2,0},{1,3},{3,1},{4,6},{6,4},{5,7},{7,5},{8,10},{10,8},{9,1... | collective-permute-start | bytes 1474568 | tf_op jit(solution)/shard_map/ppermute | solution.py:662
  63.4 1.3 %collective-permute-start.12 = (bf16[256,384]{1,0:T(8,128)(2,1)S(1)}, bf16[256,384]{1,0:T(8,128)(2,1)S(1)}, u32[]{:S(2)}, u32[]{:S(2)}) collective-permute-start(bf16[256,384]{1,0:T(8,128)(2,1)S(1)} %get-tuple-element.61), channel_id=1, source_target_pairs={{8,0},{4,12},{9,1},{5,13},{10,2},{6,14},{11,3},{7,15},{24,16},{20,... | collective-permute-start | bytes 589832 | tf_op jit(solution)/shard_map/ppermute | solution.py:522
  64.7 1.3 %collective-permute-start.13 = (bf16[256,384]{1,0:T(8,128)(2,1)S(1)}, bf16[256,384]{1,0:T(8,128)(2,1)S(1)}, u32[]{:S(2)}, u32[]{:S(2)}) collective-permute-start(bf16[256,384]{1,0:T(8,128)(2,1)S(1)} %get-tuple-element.62), channel_id=1, source_target_pairs={{4,0},{8,12},{5,1},{9,13},{6,2},{10,14},{7,3},{11,15},{20,16},{24,... | collective-permute-start | bytes 589832 | tf_op jit(solution)/shard_map/ppermute | solution.py:522
  66.0 0.7 collective-permute-start.14
  66.7 0.6 keep_here.1.keep
  67.3 0.0 collective-permute-done.11.came
  67.3 5.7 %collective-permute-done.12.c3 = bf16[256,384]{1,0:T(8,128)(2,1)S(1)} collective-permute-done((bf16[256,384]{1,0:T(8,128)(2,1)S(1)}, bf16[256,384]{1,0:T(8,128)(2,1)S(1)}, u32[]{:S(2)}, u32[]{:S(2)}) %collective-permute-start.12) | collective-permute-done | bytes 196640 | tf_op jit(solution)/shard_map/ppermute | solution.py:522
  73.0 4.1 %collective-permute-done.13.c1 = bf16[256,384]{1,0:T(8,128)(2,1)S(1)} collective-permute-done((bf16[256,384]{1,0:T(8,128)(2,1)S(1)}, bf16[256,384]{1,0:T(8,128)(2,1)S(1)}, u32[]{:S(2)}, u32[]{:S(2)}) %collective-permute-start.13) | collective-permute-done | bytes 196640 | tf_op jit(solution)/shard_map/ppermute | solution.py:522
  77.1 0.0 collective-permute-done.14.c2
  77.1 0.0 collective-permute-done.10.last
  77.1 1.0 %finish.1 = (bf16[192,768]{1,0:T(8,128)(2,1)}, bf16[128,768]{1,0:T(8,128)(2,1)}, bf16[128,768]{1,0:T(8,128)(2,1)}, bf16[128,768]{1,0:T(8,128)(2,1)}) custom-call(bf16[320,768]{1,0:T(8,128)(2,1)S(1)} %collective-permute-done.10.last, f32[320,768]{1,0:T(8,128)S(1)} %keep_here.1.keep, bf16[320,768]{1,0:T(8,128)(2,1)S(1)} %collective-permute-done.11.came, ...), custom_call_target="tpu_custom_call" | custom-call | flops 1100000000 | tf_op jit(solution)/shard_map/finish/pallas_call | solution.py:671
  (3 shorter events, 0.0 us)
Async XLA Ops:
  3.7 18.3 %copy-start.1 = (bf16[960,128]{1,0:T(8,128)(2,1)S(1)}, bf16[960,128]{1,0:T(8,128)(2,1)}, u32[]{:S(2)}) copy-start(bf16[960,128]{1,0:T(8,128)(2,1)} %get-tuple-element.34.b0) | copy-start | bytes 737284
  3.8 28.6 %copy-start = (bf16[960,256]{1,0:T(8,128)(2,1)S(1)}, bf16[960,256]{1,0:T(8,128)(2,1)}, u32[]{:S(2)}) copy-start(bf16[960,256]{1,0:T(8,128)(2,1)} %get-tuple-element.47.a0) | copy-start | bytes 1474564
  3.8 18.3 %collective-permute-start.5 = (bf16[960,256]{1,0:T(8,128)(2,1)}, bf16[960,256]{1,0:T(8,128)(2,1)S(1)}, u32[]{:S(2)}, u32[]{:S(2)}) collective-permute-start(bf16[960,256]{1,0:T(8,128)(2,1)} %get-tuple-element.40), channel_id=1, source_target_pairs={{0,8},{12,4},{1,9},{13,5},{2,10},{14,6},{3,11},{15,7},{16,24},{28,... | collective-permute-start | bytes 1474568 | tf_op jit(solution)/shard_map/ppermute | solution.py:522
  9.9 16.1 %collective-permute-start.4 = (bf16[960,256]{1,0:T(8,128)(2,1)}, bf16[960,256]{1,0:T(8,128)(2,1)S(1)}, u32[]{:S(2)}, u32[]{:S(2)}) collective-permute-start(bf16[960,256]{1,0:T(8,128)(2,1)} %get-tuple-element.40), channel_id=1, source_target_pairs={{4,8},{8,4},{5,9},{9,5},{6,10},{10,6},{7,11},{11,7},{20,24},{24,20... | collective-permute-start | bytes 1474568 | tf_op jit(solution)/shard_map/ppermute | solution.py:522
  10.6 21.8 %collective-permute-start.3 = (bf16[960,256]{1,0:T(8,128)(2,1)}, bf16[960,256]{1,0:T(8,128)(2,1)S(1)}, u32[]{:S(2)}, u32[]{:S(2)}) collective-permute-start(bf16[960,256]{1,0:T(8,128)(2,1)} %get-tuple-element.47.a0), channel_id=1, source_target_pairs={{0,4},{12,8},{1,5},{13,9},{2,6},{14,10},{3,7},{15,11},{16,20},{28,... | collective-permute-start | bytes 1474568 | tf_op jit(solution)/shard_map/ppermute | solution.py:522
  13.6 18.7 %collective-permute-start.1 = (bf16[960,128]{1,0:T(8,128)(2,1)}, bf16[960,128]{1,0:T(8,128)(2,1)S(1)}, u32[]{:S(2)}, u32[]{:S(2)}) collective-permute-start(bf16[960,128]{1,0:T(8,128)(2,1)} %get-tuple-element.35), channel_id=1, source_target_pairs={{4,8},{8,4},{5,9},{9,5},{6,10},{10,6},{7,11},{11,7},{20,24},{24,20... | collective-permute-start | bytes 737288 | tf_op jit(solution)/shard_map/ppermute | solution.py:522
  14.3 23.3 %collective-permute-start = (bf16[960,128]{1,0:T(8,128)(2,1)}, bf16[960,128]{1,0:T(8,128)(2,1)S(1)}, u32[]{:S(2)}, u32[]{:S(2)}) collective-permute-start(bf16[960,128]{1,0:T(8,128)(2,1)} %get-tuple-element.35), channel_id=1, source_target_pairs={{0,8},{12,4},{1,9},{13,5},{2,10},{14,6},{3,11},{15,7},{16,24},{28,... | collective-permute-start | bytes 737288 | tf_op jit(solution)/shard_map/ppermute | solution.py:522
  18.3 0.7 copy-start.2
  19.0 0.7 copy-start.3
  19.6 0.7 copy-start.4
  22.0 19.6 %collective-permute-start.2 = (bf16[960,128]{1,0:T(8,128)(2,1)S(1)}, bf16[960,128]{1,0:T(8,128)(2,1)S(1)}, u32[]{:S(2)}, u32[]{:S(2)}) collective-permute-start(bf16[960,128]{1,0:T(8,128)(2,1)S(1)} %copy-done.1), channel_id=1, source_target_pairs={{0,4},{12,8},{1,5},{13,9},{2,6},{14,10},{3,7},{15,11},{16,20},{28,... | collective-permute-start | bytes 737288 | tf_op jit(solution)/shard_map/ppermute | solution.py:522
  41.7 17.6 %slice-start = ((s8[4718592]{0:T(1024)(128)(4,1)}), s8[4194304]{0:T(1024)(128)(4,1)S(1)}, s32[]{:S(2)}) async-start(s8[4718592]{0:T(1024)(128)(4,1)} %bitcast.1), calls=%async_computation | async-start | bytes 8388608
  41.7 17.6 %slice-start.1 = ((s8[4718592]{0:T(1024)(128)(4,1)}), s8[524288]{0:T(1024)(128)(4,1)S(1)}, s32[]{:S(2)}) async-start(s8[4718592]{0:T(1024)(128)(4,1)} %bitcast.1), calls=%async_computation.1 | async-start | bytes 1048576
  41.7 17.5 %collective-permute-start.6 = (bf16[320,384]{1,0:T(8,128)(2,1)S(1)}, bf16[320,384]{1,0:T(8,128)(2,1)S(1)}, u32[]{:S(2)}, u32[]{:S(2)}) collective-permute-start(bf16[320,384]{1,0:T(8,128)(2,1)S(1)} %get-tuple-element.44), channel_id=1, source_target_pairs={{4,0},{8,12},{5,1},{9,13},{6,2},{10,14},{7,3},{11,15},{20,16},{24,... | collective-permute-start | bytes 737288 | tf_op jit(solution)/shard_map/ppermute | solution.py:522
  43.2 16.0 %collective-permute-start.7 = (bf16[320,384]{1,0:T(8,128)(2,1)S(1)}, bf16[320,384]{1,0:T(8,128)(2,1)S(1)}, u32[]{:S(2)}, u32[]{:S(2)}) collective-permute-start(bf16[320,384]{1,0:T(8,128)(2,1)S(1)} %get-tuple-element.45), channel_id=1, source_target_pairs={{8,0},{4,12},{9,1},{5,13},{10,2},{6,14},{11,3},{7,15},{24,16},{20,... | collective-permute-start | bytes 737288 | tf_op jit(solution)/shard_map/ppermute | solution.py:522
  44.5 14.7 %collective-permute-start.8 = (bf16[320,384]{1,0:T(8,128)(2,1)S(1)}, bf16[320,384]{1,0:T(8,128)(2,1)S(1)}, u32[]{:S(2)}, u32[]{:S(2)}) collective-permute-start(bf16[320,384]{1,0:T(8,128)(2,1)S(1)} %get-tuple-element.46), channel_id=1, source_target_pairs={{4,8},{8,4},{5,9},{9,5},{6,10},{10,6},{7,11},{11,7},{20,24},{24,20... | collective-permute-start | bytes 737288 | tf_op jit(solution)/shard_map/ppermute | solution.py:522
  59.8 1.9 %collective-permute-start.9 = (bf16[320,768]{1,0:T(8,128)(2,1)S(1)}, bf16[320,768]{1,0:T(8,128)(2,1)S(1)}, u32[]{:S(2)}, u32[]{:S(2)}) collective-permute-start(bf16[320,768]{1,0:T(8,128)(2,1)S(1)} %give_there.1), channel_id=1, source_target_pairs={{0,1},{1,0},{2,3},{3,2},{4,5},{5,4},{6,7},{7,6},{8,9},{9,8},{10,11... | collective-permute-start | bytes 1474568 | tf_op jit(solution)/shard_map/ppermute | solution.py:653
  61.1 6.1 %collective-permute-start.11 = (bf16[320,768]{1,0:T(8,128)(2,1)S(1)}, bf16[320,768]{1,0:T(8,128)(2,1)S(1)}, u32[]{:S(2)}, u32[]{:S(2)}) collective-permute-start(bf16[320,768]{1,0:T(8,128)(2,1)S(1)} %give_here.1), channel_id=1, source_target_pairs={{0,1},{1,0},{2,3},{3,2},{4,5},{5,4},{6,7},{7,6},{8,9},{9,8},{10,11... | collective-permute-start | bytes 1474568 | tf_op jit(solution)/shard_map/ppermute | solution.py:669
  61.9 15.2 %collective-permute-start.10 = (bf16[320,768]{1,0:T(8,128)(2,1)S(1)}, bf16[320,768]{1,0:T(8,128)(2,1)S(1)}, u32[]{:S(2)}, u32[]{:S(2)}) collective-permute-start(bf16[320,768]{1,0:T(8,128)(2,1)S(1)} %add.1), channel_id=1, source_target_pairs={{0,2},{2,0},{1,3},{3,1},{4,6},{6,4},{5,7},{7,5},{8,10},{10,8},{9,1... | collective-permute-start | bytes 1474568 | tf_op jit(solution)/shard_map/ppermute | solution.py:662
  63.4 9.5 %collective-permute-start.12 = (bf16[256,384]{1,0:T(8,128)(2,1)S(1)}, bf16[256,384]{1,0:T(8,128)(2,1)S(1)}, u32[]{:S(2)}, u32[]{:S(2)}) collective-permute-start(bf16[256,384]{1,0:T(8,128)(2,1)S(1)} %get-tuple-element.61), channel_id=1, source_target_pairs={{8,0},{4,12},{9,1},{5,13},{10,2},{6,14},{11,3},{7,15},{24,16},{20,... | collective-permute-start | bytes 589832 | tf_op jit(solution)/shard_map/ppermute | solution.py:522
  64.7 12.4 %collective-permute-start.13 = (bf16[256,384]{1,0:T(8,128)(2,1)S(1)}, bf16[256,384]{1,0:T(8,128)(2,1)S(1)}, u32[]{:S(2)}, u32[]{:S(2)}) collective-permute-start(bf16[256,384]{1,0:T(8,128)(2,1)S(1)} %get-tuple-element.62), channel_id=1, source_target_pairs={{4,0},{8,12},{5,1},{9,13},{6,2},{10,14},{7,3},{11,15},{20,16},{24,... | collective-permute-start | bytes 589832 | tf_op jit(solution)/shard_map/ppermute | solution.py:522
  66.0 11.1 %collective-permute-start.14 = (bf16[256,384]{1,0:T(8,128)(2,1)S(1)}, bf16[256,384]{1,0:T(8,128)(2,1)S(1)}, u32[]{:S(2)}, u32[]{:S(2)}) collective-permute-start(bf16[256,384]{1,0:T(8,128)(2,1)S(1)} %get-tuple-element.63), channel_id=1, source_target_pairs={{4,8},{8,4},{5,9},{9,5},{6,10},{10,6},{7,11},{11,7},{20,24},{24,20... | collective-permute-start | bytes 589832 | tf_op jit(solution)/shard_map/ppermute | solution.py:522

commit v4 on v3

--- a/solution.py
+++ b/solution.py
@@ -405,38 +405,46 @@
     run_jobs(jobs, keys, values, fresh, factor)
 
 
+def hand_out(place, out, lanes, qn, qc):
+    new_rows = qn.shape[0] // 4
+    ctx_rows = qc.shape[0] // 4
+    at = pl.ds(pl.multiple_of(place * new_rows, new_rows), new_rows)
+    part = pl.ds(pl.multiple_of(place * ctx_rows, ctx_rows), ctx_rows)
+    out[:new_rows, lanes] = qn[at]
+    out[new_rows:, lanes] = qc[part]
+
+
 def first_kernel(
-    factor, frames_new, a0, a1, a2, a3, order, alive, biases, qn, qc, keys, values
+    factor, frames_new, a0, a1, a2, a3, order, alive, biases, qn, qc, e1, e3, keys, values
 ):
     z = lax.axis_index("seq")
-
-    @pl.when(middle(z))
-    def _():
-        gather_heads(far_places(z), (a0, a1, a2, a3), qc.shape[0] // 4, keys, values, qn, qc)
-        attend_heads(factor, frames_new, order, alive, biases, keys, values, qn, qc)
-
-
-def second_kernel(
-    factor, frames_new, b0, b3, b2, b1, order, alive, biases, fn, fc,
-    o0, o1, o2, o3, keys, values, qn, qc,
-):
-    z = lax.axis_index("seq")
-    ctx_rows = qc.shape[0] // 4
-    new_rows = qn.shape[0] // 4
-    most = fn.shape[1]
 
     @pl.when(middle(z))
     def _():
         places = far_places(z)
-        gather_heads(places, (b0, b1, b2, b3), ctx_rows, keys, values, qn, qc)
+        gather_heads(places, (a0, a1, a2, a3), qc.shape[0] // 4, keys, values, qn, qc)
         attend_heads(factor, frames_new, order, alive, biases, keys, values, qn, qc)
-        for place, out in zip(places, (o0, o1, o2, o3)):
-            at = pl.ds(pl.multiple_of(place * new_rows, new_rows), new_rows)
-            part = pl.ds(pl.multiple_of(place * ctx_rows, ctx_rows), ctx_rows)
-            out[:new_rows, :most] = fn[at]
-            out[:new_rows, most:] = qn[at]
-            out[new_rows:, :most] = fc[part]
-            out[new_rows:, most:] = qc[part]
+        hand_out(places[1], e1, slice(None), qn, qc)
+        hand_out(places[3], e3, slice(None), qn, qc)
+
+
+def second_kernel(
+    factor, frames_new, b0, b3, b2, b1, order, alive, biases, fn, fc,
+    o0, o2, n1, n3, keys, values, qn, qc,
+):
+    z = lax.axis_index("seq")
+    most = fn.shape[1]
+
+    @pl.when(middle(z))
+    def _():
+        places = far_places(z)
+        gather_heads(places, (b0, b1, b2, b3), qc.shape[0] // 4, keys, values, qn, qc)
+        attend_heads(factor, frames_new, order, alive, biases, keys, values, qn, qc)
+        hand_out(places[1], n1, slice(None), qn, qc)
+        hand_out(places[3], n3, slice(None), qn, qc)
+        for place, out in ((places[0], o0), (places[2], o2)):
+            hand_out(place, out, slice(0, most), fn, fc)
+            hand_out(place, out, slice(most, None), qn, qc)
 
 
 def cache_kernel(
@@ -473,7 +481,9 @@
     return (jnp.where(low, near, far), jnp.where(low, far, near))
 
 
-def project_kernel(mine, here, o0, o1, o3, o2, weight, out):
+def project_kernel(mine, here, e1, e3, o0, n1, n3, o2, weight, out):
+    o1 = jnp.concatenate([e1[...], n1[...]], axis=1)
+    o3 = jnp.concatenate([e3[...], n3[...]], axis=1)
     a, b = halves(lax.axis_index("seq"), slice(None), o0, o1, o2, o3)
     mixed = jnp.concatenate([a, b], axis=1)
     width = mixed.shape[1]
@@ -531,15 +541,6 @@
 
 def back(pairs):
     return tuple((b, a) for a, b in pairs)
-
-
-def home(own, beside, across, beyond):
-    return (
-        own,
-        permute(beside, back(BESIDE)),
-        permute(across, ACROSS),
-        permute(beyond, back(BEYOND)),
-    )
 
 
 def fast_device(
@@ -602,9 +603,14 @@
             pltpu.VMEM((lanes // hdim, rows * devices, 2 * hdim), jnp.bfloat16),
         ]
 
-    fresh, held = pl.pallas_call(
+    fresh, held, early_beside, early_beyond = pl.pallas_call(
         functools.partial(first_kernel, factor, frames_new),
-        out_shape=[shape16(new_rows * devices, most), shape16(ctx_all, most)],
+        out_shape=[
+            shape16(new_rows * devices, most),
+            shape16(ctx_all, most),
+            shape16(rows, most),
+            shape16(rows, most),
+        ],
         scratch_shapes=scratch(most),
         compiler_params=LIMIT,
         name="attend_first",
@@ -612,7 +618,12 @@
     )(near_a, beside_a, across_a, beyond_a, order, alive, biases)
     results = pl.pallas_call(
         functools.partial(second_kernel, factor, frames_new),
-        out_shape=[shape16(rows, half)] * 4,
+        out_shape=[
+            shape16(rows, half),
+            shape16(rows, half),
+            shape16(rows, half - most),
+            shape16(rows, half - most),
+        ],
         scratch_shapes=scratch(half - most)
         + [
             pltpu.VMEM((new_rows * devices, half - most), jnp.bfloat16),
@@ -622,7 +633,18 @@
         name="attend_second",
         cost_estimate=lasts(2.4),
     )(near_b, beyond_b, across_b, beside_b, order, alive, biases, fresh, held)
-    mixed = home(*results)
+    own, across, late_beside, late_beyond = results
+    early_beside = permute(early_beside, back(BESIDE))
+    early_beyond = permute(early_beyond, back(BEYOND))
+    across = lax.optimization_barrier((across, early_beside, early_beyond))[0]
+    mixed = (
+        early_beside,
+        early_beyond,
+        own,
+        permute(late_beside, back(BESIDE)),
+        permute(late_beyond, back(BEYOND)),
+        permute(across, ACROSS),
+    )
     near_a = lax.optimization_barrier((near_a, results[0]))[0]
     caches = pl.pallas_call(
         cache_kernel,
@@ -630,24 +652,20 @@
         scratch_shapes=[pltpu.VMEM((ctx_all, width), jnp.bfloat16)],
         compiler_params=LIMIT,
         name="caches",
-        cost_estimate=lasts(0.8),
+        cost_estimate=lasts(3),
     )(near_a, beside_a, across_a, beyond_a, near_b, beside_b, across_b, beyond_b, order)
 
-    own, beside, across, beyond = mixed
-    own, beside, beyond, across = lax.optimization_barrier(
-        (own, beside, beyond, across, caches[0])
-    )[:4]
-    mixed = (own, beside, across, beyond)
+    mixed = lax.optimization_barrier((*mixed, caches[0]))[:6]
 
     def project(mine, here, dtype):
         return pl.pallas_call(
             functools.partial(project_kernel, mine, here),
             out_shape=jax.ShapeDtypeStruct((rows, width), dtype),
-            in_specs=[WHOLE] * 5,
+            in_specs=[WHOLE] * 7,
             compiler_params=LIMIT,
             name=("keep" if mine else "give") + ("_here" if here else "_there"),
             cost_estimate=lasts(0.6),
-        )(mixed[0], mixed[1], mixed[3], mixed[2], out_weight)
+        )(*mixed, out_weight)
 
     give_there = project(False, False, jnp.bfloat16)
     came_there = lax.ppermute(give_there, "tensor", SIBLING)
@@ -665,7 +683,7 @@
     across = permute(caches[2], ACROSS)
     beside = permute(caches[1], back(BESIDE))
     stored = (caches[0], beyond, beside, across)
-    mixed = lax.optimization_barrier((*mixed, keep_there))[:4]
+    mixed = lax.optimization_barrier((*mixed, keep_there))[:6]
     came = lax.ppermute(project(False, True, jnp.bfloat16), "tensor", SIBLING)
     keep = project(True, True, jnp.float32)
     block_out, context_out, cache_keys, cache_values = pl.pallas_call(

time: 78.5 us -> 76.1 us (0.969)
  waiting for transfers between devices: 39.3 us -> 34.6 us
  starting transfers between devices: 27.4 us -> 29.6 us
    ppermute x12 -> x14, waiting for transfers between devices: 39.2 us -> 34.5 us  [permute(): return lax.ppermute(x, 'seq', pairs)]
    ppermute x12 -> x14, starting transfers between devices: 25.2 us -> 27.5 us  [permute(): return lax.ppermute(x, 'seq', pairs)]
  transfers between devices with their start and end apart: 15 -> 17, of which waited for: 7 -> 9; matrix products, arithmetic and copies ran while one was open for 0% -> 0% of each run, Pallas kernels for 5% -> 5%
where the time goes in v4:
time: 76.1 us; the launch traced here: 75.7 us
  waiting for transfers between devices  34.6 us (45%)
  starting transfers between devices  29.6 us (39%)
  Pallas kernels  8.58 us (11%)
  local copies, waits for them, and re-layouts  2 us (3%)
  between operations  0.88 us (1%)
    ppermute x14, waiting for transfers between devices, permute(): return lax.ppermute(x, 'seq', pairs)  34.5 us
    ppermute x14, starting transfers between devices, permute(): return lax.ppermute(x, 'seq', pairs)  27.5 us
    pallas_call x1, Pallas kernels, fast_device(): pl.pallas_call(pack_kernel, out_shape=(shape16(3 * rows, most), shape16(3...  3.11 us
    pallas_call x4, Pallas kernels, project(): pl.pallas_call(functools.partial(project_kernel, mine, here), out_shape=j...  2.43 us
    unnamed x14, local copies, waits for them, and re-layouts  2 us
    pallas_call x1, Pallas kernels, fast_device(): pl.pallas_call(plan_kernel, out_shape=(shape16(ctx_all, ctx_all), jax.Sha...  1.72 us
    ppermute x1, starting transfers between devices, fast_device(): last = lax.ppermute(other, 'tensor', OPPOSITE)  1.55 us
  transfers between devices with their start and end apart: 17, of which 9 were waited for; matrix products, arithmetic and copies ran while one was open for 0% of the time, Pallas kernels for 5%

profile of v4, /device:TPU:0, one launch (start us, length us, event | category | flops | bytes accessed | tf_op | source)
XLA Modules:
  0.0 75.7 jit_solution(8341375084174009368)
XLA Ops:
  0.6 3.1 %pack.1 = (bf16[960,256]{1,0:T(8,128)(2,1)}, bf16[960,128]{1,0:T(8,128)(2,1)}, bf16[960,256]{1,0:T(8,128)(2,1)}, bf16[960,128]{1,0:T(8,128)(2,1)}) custom-call(s32[8]{0:T(128)} %levels.3, bf16[192,768]{1,0:T(8,128)(2,1)} %q.1, bf16[192,768]{1,0:T(8,128)(2,1)} %k.1, bf16[192,768]{1,0:T(8,128)(2,1)} %v.1, bf16[128,768]{1,0:T(8,128)(2,1)} %cq.1, ...), custom_call_target="tpu_custom_call" | custom-call | tf_op jit(solution)/shard_map/pack/pallas_call | solution.py:568
  3.7 6.0 %collective-permute-start.2 = (bf16[960,256]{1,0:T(8,128)(2,1)}, bf16[960,256]{1,0:T(8,128)(2,1)S(1)}, u32[]{:S(2)}, u32[]{:S(2)}) collective-permute-start(bf16[960,256]{1,0:T(8,128)(2,1)} %get-tuple-element.42), channel_id=1, source_target_pairs={{0,8},{12,4},{1,9},{13,5},{2,10},{14,6},{3,11},{15,7},{16,24},{28,... | collective-permute-start | bytes 1474568 | tf_op jit(solution)/shard_map/ppermute | solution.py:532
  9.7 0.7 collective-permute-start.1
  10.4 3.1 %collective-permute-start = (bf16[960,256]{1,0:T(8,128)(2,1)}, bf16[960,256]{1,0:T(8,128)(2,1)S(1)}, u32[]{:S(2)}, u32[]{:S(2)}) collective-permute-start(bf16[960,256]{1,0:T(8,128)(2,1)} %get-tuple-element.57.a0), channel_id=1, source_target_pairs={{0,4},{12,8},{1,5},{13,9},{2,6},{14,10},{3,7},{15,11},{16,20},{28,... | collective-permute-start | bytes 1474568 | tf_op jit(solution)/shard_map/ppermute | solution.py:532
  13.5 0.7 collective-permute-start.6
  14.2 4.0 %collective-permute-start.5 = (bf16[960,128]{1,0:T(8,128)(2,1)}, bf16[960,128]{1,0:T(8,128)(2,1)S(1)}, u32[]{:S(2)}, u32[]{:S(2)}) collective-permute-start(bf16[960,128]{1,0:T(8,128)(2,1)} %get-tuple-element.49), channel_id=1, source_target_pairs={{0,8},{12,4},{1,9},{13,5},{2,10},{14,6},{3,11},{15,7},{16,24},{28,... | collective-permute-start | bytes 737288 | tf_op jit(solution)/shard_map/ppermute | solution.py:532
  18.2 0.0 copy-start
  18.2 0.6 copy-done
  18.8 0.0 copy-start.3
  18.8 0.7 copy-done.3
  19.5 0.0 copy-start.4
  19.5 0.7 copy-done.4
  20.2 0.0 copy-start.2
  20.2 0.0 copy-start.1
  20.2 1.7 %plan.1 = (bf16[512,512]{1,0:T(8,128)(2,1)S(1)}, f32[512,128]{1,0:T(8,128)S(1)}, f32[8,512]{1,0:T(8,128)S(1)}) custom-call(s32[1,128]{1,0:T(1,128)S(1)} %bitcast.3, s32[8]{0:T(128)S(1)} %copy-done, s32[2,8]{1,0:T(2,128)S(1)} %copy-done.3), custom_call_target="tpu_custom_call" | custom-call | flops 1760000000 | tf_op jit(solution)/shard_map/plan/pallas_call | solution.py:589
  21.9 0.0 collective-permute-done.2.a3
  21.9 0.0 copy-done.2
  21.9 3.9 %collective-permute-start.7 = (bf16[960,128]{1,0:T(8,128)(2,1)S(1)}, bf16[960,128]{1,0:T(8,128)(2,1)S(1)}, u32[]{:S(2)}, u32[]{:S(2)}) collective-permute-start(bf16[960,128]{1,0:T(8,128)(2,1)S(1)} %copy-done.2), channel_id=1, source_target_pairs={{0,4},{12,8},{1,5},{13,9},{2,6},{14,10},{3,7},{15,11},{16,20},{28,... | collective-permute-start | bytes 737288 | tf_op jit(solution)/shard_map/ppermute | solution.py:532
  25.8 0.0 collective-permute-done.1.a2
  25.9 6.3 %collective-permute-done.a1 = bf16[960,256]{1,0:T(8,128)(2,1)S(1)} collective-permute-done((bf16[960,256]{1,0:T(8,128)(2,1)}, bf16[960,256]{1,0:T(8,128)(2,1)S(1)}, u32[]{:S(2)}, u32[]{:S(2)}) %collective-permute-start) | collective-permute-done | bytes 491552 | tf_op jit(solution)/shard_map/ppermute | solution.py:532
  32.2 0.0 copy-done.1
  32.2 1.3 %collective-permute-start.3 = (bf16[320,256]{1,0:T(8,128)(2,1)S(1)}, bf16[320,256]{1,0:T(8,128)(2,1)S(1)}, u32[]{:S(2)}, u32[]{:S(2)}) collective-permute-start(bf16[320,256]{1,0:T(8,128)(2,1)S(1)} %get-tuple-element.46), channel_id=1, source_target_pairs={{4,0},{8,12},{5,1},{9,13},{6,2},{10,14},{7,3},{11,15},{20,16},{24,... | collective-permute-start | bytes 491528 | tf_op jit(solution)/shard_map/ppermute | solution.py:532
  33.5 1.3 %collective-permute-start.4 = (bf16[320,256]{1,0:T(8,128)(2,1)S(1)}, bf16[320,256]{1,0:T(8,128)(2,1)S(1)}, u32[]{:S(2)}, u32[]{:S(2)}) collective-permute-start(bf16[320,256]{1,0:T(8,128)(2,1)S(1)} %get-tuple-element.47), channel_id=1, source_target_pairs={{8,0},{4,12},{9,1},{5,13},{10,2},{6,14},{11,3},{7,15},{24,16},{20,... | collective-permute-start | bytes 491528 | tf_op jit(solution)/shard_map/ppermute | solution.py:532
  34.8 0.0 collective-permute-done.6.b2
  34.8 2.7 %collective-permute-done.5.b3 = bf16[960,128]{1,0:T(8,128)(2,1)S(1)} collective-permute-done((bf16[960,128]{1,0:T(8,128)(2,1)}, bf16[960,128]{1,0:T(8,128)(2,1)S(1)}, u32[]{:S(2)}, u32[]{:S(2)}) %collective-permute-start.5) | collective-permute-done | bytes 245792 | tf_op jit(solution)/shard_map/ppermute | solution.py:532
  37.5 4.0 %collective-permute-done.7.b1 = bf16[960,128]{1,0:T(8,128)(2,1)S(1)} collective-permute-done((bf16[960,128]{1,0:T(8,128)(2,1)S(1)}, bf16[960,128]{1,0:T(8,128)(2,1)S(1)}, u32[]{:S(2)}, u32[]{:S(2)}) %collective-permute-start.7) | collective-permute-done | bytes 245792 | tf_op jit(solution)/shard_map/ppermute | solution.py:532
  41.5 1.3 %collective-permute-start.8 = (bf16[320,128]{1,0:T(8,128)(2,1)S(1)}, bf16[320,128]{1,0:T(8,128)(2,1)S(1)}, u32[]{:S(2)}, u32[]{:S(2)}) collective-permute-start(bf16[320,128]{1,0:T(8,128)(2,1)S(1)} %get-tuple-element.53), channel_id=1, source_target_pairs={{4,0},{8,12},{5,1},{9,13},{6,2},{10,14},{7,3},{11,15},{20,16},{24,... | collective-permute-start | bytes 245768 | tf_op jit(solution)/shard_map/ppermute | solution.py:532
  42.8 1.3 %collective-permute-start.9 = (bf16[320,128]{1,0:T(8,128)(2,1)S(1)}, bf16[320,128]{1,0:T(8,128)(2,1)S(1)}, u32[]{:S(2)}, u32[]{:S(2)}) collective-permute-start(bf16[320,128]{1,0:T(8,128)(2,1)S(1)} %get-tuple-element.54), channel_id=1, source_target_pairs={{8,0},{4,12},{9,1},{5,13},{10,2},{6,14},{11,3},{7,15},{24,16},{20,... | collective-permute-start | bytes 245768 | tf_op jit(solution)/shard_map/ppermute | solution.py:532
  44.1 3.9 %collective-permute-done.3.e1 = bf16[320,256]{1,0:T(8,128)(2,1)S(1)} collective-permute-done((bf16[320,256]{1,0:T(8,128)(2,1)S(1)}, bf16[320,256]{1,0:T(8,128)(2,1)S(1)}, u32[]{:S(2)}, u32[]{:S(2)}) %collective-permute-start.3) | collective-permute-done | bytes 163872 | tf_op jit(solution)/shard_map/ppermute | solution.py:532
  48.0 0.0 collective-permute-done.4.e3
  48.0 0.0 slice-start
  48.0 0.0 slice-start.1
  48.0 0.8 %collective-permute-start.10 = (bf16[320,384]{1,0:T(8,128)(2,1)S(1)}, bf16[320,384]{1,0:T(8,128)(2,1)S(1)}, u32[]{:S(2)}, u32[]{:S(2)}) collective-permute-start(bf16[320,384]{1,0:T(8,128)(2,1)S(1)} %get-tuple-element.56), channel_id=1, source_target_pairs={{4,8},{8,4},{5,9},{9,5},{6,10},{10,6},{7,11},{11,7},{20,24},{24,20... | collective-permute-start | bytes 737288 | tf_op jit(solution)/shard_map/ppermute | solution.py:532
  48.8 0.2 caches.1
  49.0 1.3 %collective-permute-done.8.n1 = bf16[320,128]{1,0:T(8,128)(2,1)S(1)} collective-permute-done((bf16[320,128]{1,0:T(8,128)(2,1)S(1)}, bf16[320,128]{1,0:T(8,128)(2,1)S(1)}, u32[]{:S(2)}, u32[]{:S(2)}) %collective-permute-start.8) | collective-permute-done | bytes 81952 | tf_op jit(solution)/shard_map/ppermute | solution.py:532
  50.2 2.3 %collective-permute-done.9.n3 = bf16[320,128]{1,0:T(8,128)(2,1)S(1)} collective-permute-done((bf16[320,128]{1,0:T(8,128)(2,1)S(1)}, bf16[320,128]{1,0:T(8,128)(2,1)S(1)}, u32[]{:S(2)}, u32[]{:S(2)}) %collective-permute-start.9) | collective-permute-done | bytes 81952 | tf_op jit(solution)/shard_map/ppermute | solution.py:532
  52.5 0.0 collective-permute-done.10.o2
  52.6 0.0 slice-done
  52.6 0.0 slice-done.1
  52.6 0.6 give_there.1
  53.2 0.1 collective-permute-start.11
  53.3 0.6 keep_there.1.keep
  53.9 0.6 give_here.1
  54.5 0.5 collective-permute-start.13
  55.0 0.1 collective-permute-done.11.came
  55.1 0.1 add.1
  55.2 1.6 %collective-permute-start.12 = (bf16[320,768]{1,0:T(8,128)(2,1)S(1)}, bf16[320,768]{1,0:T(8,128)(2,1)S(1)}, u32[]{:S(2)}, u32[]{:S(2)}) collective-permute-start(bf16[320,768]{1,0:T(8,128)(2,1)S(1)} %add.1), channel_id=1, source_target_pairs={{0,2},{2,0},{1,3},{3,1},{4,6},{6,4},{5,7},{7,5},{8,10},{10,8},{9,1... | collective-permute-start | bytes 1474568 | tf_op jit(solution)/shard_map/ppermute | solution.py:680
  56.8 1.3 %collective-permute-start.14 = (bf16[256,384]{1,0:T(8,128)(2,1)S(1)}, bf16[256,384]{1,0:T(8,128)(2,1)S(1)}, u32[]{:S(2)}, u32[]{:S(2)}) collective-permute-start(bf16[256,384]{1,0:T(8,128)(2,1)S(1)} %get-tuple-element.75), channel_id=1, source_target_pairs={{8,0},{4,12},{9,1},{5,13},{10,2},{6,14},{11,3},{7,15},{24,16},{20,... | collective-permute-start | bytes 589832 | tf_op jit(solution)/shard_map/ppermute | solution.py:532
  58.0 1.3 %collective-permute-start.15 = (bf16[256,384]{1,0:T(8,128)(2,1)S(1)}, bf16[256,384]{1,0:T(8,128)(2,1)S(1)}, u32[]{:S(2)}, u32[]{:S(2)}) collective-permute-start(bf16[256,384]{1,0:T(8,128)(2,1)S(1)} %get-tuple-element.76), channel_id=1, source_target_pairs={{4,0},{8,12},{5,1},{9,13},{6,2},{10,14},{7,3},{11,15},{20,16},{24,... | collective-permute-start | bytes 589832 | tf_op jit(solution)/shard_map/ppermute | solution.py:532
  59.3 0.7 collective-permute-start.16
  60.0 0.6 keep_here.1.keep
  60.6 0.0 collective-permute-done.13.came
  60.6 10.6 %collective-permute-done.14.c3 = bf16[256,384]{1,0:T(8,128)(2,1)S(1)} collective-permute-done((bf16[256,384]{1,0:T(8,128)(2,1)S(1)}, bf16[256,384]{1,0:T(8,128)(2,1)S(1)}, u32[]{:S(2)}, u32[]{:S(2)}) %collective-permute-start.14) | collective-permute-done | bytes 196640 | tf_op jit(solution)/shard_map/ppermute | solution.py:532
  71.2 3.4 %collective-permute-done.15.c1 = bf16[256,384]{1,0:T(8,128)(2,1)S(1)} collective-permute-done((bf16[256,384]{1,0:T(8,128)(2,1)S(1)}, bf16[256,384]{1,0:T(8,128)(2,1)S(1)}, u32[]{:S(2)}, u32[]{:S(2)}) %collective-permute-start.15) | collective-permute-done | bytes 196640 | tf_op jit(solution)/shard_map/ppermute | solution.py:532
  74.6 0.0 collective-permute-done.16.c2
  74.6 0.0 collective-permute-done.12.last
  74.6 1.0 %finish.1 = (bf16[192,768]{1,0:T(8,128)(2,1)}, bf16[128,768]{1,0:T(8,128)(2,1)}, bf16[128,768]{1,0:T(8,128)(2,1)}, bf16[128,768]{1,0:T(8,128)(2,1)}) custom-call(bf16[320,768]{1,0:T(8,128)(2,1)S(1)} %collective-permute-done.12.last, f32[320,768]{1,0:T(8,128)S(1)} %keep_here.1.keep, bf16[320,768]{1,0:T(8,128)(2,1)S(1)} %collective-permute-done.13.came, ...), custom_call_target="tpu_custom_call" | custom-call | flops 1100000000 | tf_op jit(solution)/shard_map/finish/pallas_call | solution.py:689
  (3 shorter events, 0.0 us)
Async XLA Ops:
  3.7 18.1 %collective-permute-start.2 = (bf16[960,256]{1,0:T(8,128)(2,1)}, bf16[960,256]{1,0:T(8,128)(2,1)S(1)}, u32[]{:S(2)}, u32[]{:S(2)}) collective-permute-start(bf16[960,256]{1,0:T(8,128)(2,1)} %get-tuple-element.42), channel_id=1, source_target_pairs={{0,8},{12,4},{1,9},{13,5},{2,10},{14,6},{3,11},{15,7},{16,24},{28,... | collective-permute-start | bytes 1474568 | tf_op jit(solution)/shard_map/ppermute | solution.py:532
  9.7 16.1 %collective-permute-start.1 = (bf16[960,256]{1,0:T(8,128)(2,1)}, bf16[960,256]{1,0:T(8,128)(2,1)S(1)}, u32[]{:S(2)}, u32[]{:S(2)}) collective-permute-start(bf16[960,256]{1,0:T(8,128)(2,1)} %get-tuple-element.42), channel_id=1, source_target_pairs={{4,8},{8,4},{5,9},{9,5},{6,10},{10,6},{7,11},{11,7},{20,24},{24,20... | collective-permute-start | bytes 1474568 | tf_op jit(solution)/shard_map/ppermute | solution.py:532
  10.4 21.8 %collective-permute-start = (bf16[960,256]{1,0:T(8,128)(2,1)}, bf16[960,256]{1,0:T(8,128)(2,1)S(1)}, u32[]{:S(2)}, u32[]{:S(2)}) collective-permute-start(bf16[960,256]{1,0:T(8,128)(2,1)} %get-tuple-element.57.a0), channel_id=1, source_target_pairs={{0,4},{12,8},{1,5},{13,9},{2,6},{14,10},{3,7},{15,11},{16,20},{28,... | collective-permute-start | bytes 1474568 | tf_op jit(solution)/shard_map/ppermute | solution.py:532
  13.5 21.3 %collective-permute-start.6 = (bf16[960,128]{1,0:T(8,128)(2,1)}, bf16[960,128]{1,0:T(8,128)(2,1)S(1)}, u32[]{:S(2)}, u32[]{:S(2)}) collective-permute-start(bf16[960,128]{1,0:T(8,128)(2,1)} %get-tuple-element.49), channel_id=1, source_target_pairs={{4,8},{8,4},{5,9},{9,5},{6,10},{10,6},{7,11},{11,7},{20,24},{24,20... | collective-permute-start | bytes 737288 | tf_op jit(solution)/shard_map/ppermute | solution.py:532
  14.2 23.3 %collective-permute-start.5 = (bf16[960,128]{1,0:T(8,128)(2,1)}, bf16[960,128]{1,0:T(8,128)(2,1)S(1)}, u32[]{:S(2)}, u32[]{:S(2)}) collective-permute-start(bf16[960,128]{1,0:T(8,128)(2,1)} %get-tuple-element.49), channel_id=1, source_target_pairs={{0,8},{12,4},{1,9},{13,5},{2,10},{14,6},{3,11},{15,7},{16,24},{28,... | collective-permute-start | bytes 737288 | tf_op jit(solution)/shard_map/ppermute | solution.py:532
  18.2 0.7 copy-start
  18.8 0.7 copy-start.3
  19.5 0.7 copy-start.4
  20.2 1.7 %copy-start.2 = (bf16[960,128]{1,0:T(8,128)(2,1)S(1)}, bf16[960,128]{1,0:T(8,128)(2,1)}, u32[]{:S(2)}) copy-start(bf16[960,128]{1,0:T(8,128)(2,1)} %get-tuple-element.48.b0) | copy-start | bytes 737284
  20.2 12.0 %copy-start.1 = (bf16[960,256]{1,0:T(8,128)(2,1)S(1)}, bf16[960,256]{1,0:T(8,128)(2,1)}, u32[]{:S(2)}) copy-start(bf16[960,256]{1,0:T(8,128)(2,1)} %get-tuple-element.57.a0) | copy-start | bytes 1474564
  21.9 19.6 %collective-permute-start.7 = (bf16[960,128]{1,0:T(8,128)(2,1)S(1)}, bf16[960,128]{1,0:T(8,128)(2,1)S(1)}, u32[]{:S(2)}, u32[]{:S(2)}) collective-permute-start(bf16[960,128]{1,0:T(8,128)(2,1)S(1)} %copy-done.2), channel_id=1, source_target_pairs={{0,4},{12,8},{1,5},{13,9},{2,6},{14,10},{3,7},{15,11},{16,20},{28,... | collective-permute-start | bytes 737288 | tf_op jit(solution)/shard_map/ppermute | solution.py:532
  32.2 15.8 %collective-permute-start.3 = (bf16[320,256]{1,0:T(8,128)(2,1)S(1)}, bf16[320,256]{1,0:T(8,128)(2,1)S(1)}, u32[]{:S(2)}, u32[]{:S(2)}) collective-permute-start(bf16[320,256]{1,0:T(8,128)(2,1)S(1)} %get-tuple-element.46), channel_id=1, source_target_pairs={{4,0},{8,12},{5,1},{9,13},{6,2},{10,14},{7,3},{11,15},{20,16},{24,... | collective-permute-start | bytes 491528 | tf_op jit(solution)/shard_map/ppermute | solution.py:532
  33.5 14.5 %collective-permute-start.4 = (bf16[320,256]{1,0:T(8,128)(2,1)S(1)}, bf16[320,256]{1,0:T(8,128)(2,1)S(1)}, u32[]{:S(2)}, u32[]{:S(2)}) collective-permute-start(bf16[320,256]{1,0:T(8,128)(2,1)S(1)} %get-tuple-element.47), channel_id=1, source_target_pairs={{8,0},{4,12},{9,1},{5,13},{10,2},{6,14},{11,3},{7,15},{24,16},{20,... | collective-permute-start | bytes 491528 | tf_op jit(solution)/shard_map/ppermute | solution.py:532
  41.5 8.7 %collective-permute-start.8 = (bf16[320,128]{1,0:T(8,128)(2,1)S(1)}, bf16[320,128]{1,0:T(8,128)(2,1)S(1)}, u32[]{:S(2)}, u32[]{:S(2)}) collective-permute-start(bf16[320,128]{1,0:T(8,128)(2,1)S(1)} %get-tuple-element.53), channel_id=1, source_target_pairs={{4,0},{8,12},{5,1},{9,13},{6,2},{10,14},{7,3},{11,15},{20,16},{24,... | collective-permute-start | bytes 245768 | tf_op jit(solution)/shard_map/ppermute | solution.py:532
  42.8 9.7 %collective-permute-start.9 = (bf16[320,128]{1,0:T(8,128)(2,1)S(1)}, bf16[320,128]{1,0:T(8,128)(2,1)S(1)}, u32[]{:S(2)}, u32[]{:S(2)}) collective-permute-start(bf16[320,128]{1,0:T(8,128)(2,1)S(1)} %get-tuple-element.54), channel_id=1, source_target_pairs={{8,0},{4,12},{9,1},{5,13},{10,2},{6,14},{11,3},{7,15},{24,16},{20,... | collective-permute-start | bytes 245768 | tf_op jit(solution)/shard_map/ppermute | solution.py:532
  48.0 4.6 %slice-start = ((s8[4718592]{0:T(1024)(128)(4,1)}), s8[4194304]{0:T(1024)(128)(4,1)S(1)}, s32[]{:S(2)}) async-start(s8[4718592]{0:T(1024)(128)(4,1)} %bitcast.1), calls=%async_computation | async-start | bytes 8388608
  48.0 4.6 %slice-start.1 = ((s8[4718592]{0:T(1024)(128)(4,1)}), s8[524288]{0:T(1024)(128)(4,1)S(1)}, s32[]{:S(2)}) async-start(s8[4718592]{0:T(1024)(128)(4,1)} %bitcast.1), calls=%async_computation.1 | async-start | bytes 1048576
  48.0 4.6 %collective-permute-start.10 = (bf16[320,384]{1,0:T(8,128)(2,1)S(1)}, bf16[320,384]{1,0:T(8,128)(2,1)S(1)}, u32[]{:S(2)}, u32[]{:S(2)}) collective-permute-start(bf16[320,384]{1,0:T(8,128)(2,1)S(1)} %get-tuple-element.56), channel_id=1, source_target_pairs={{4,8},{8,4},{5,9},{9,5},{6,10},{10,6},{7,11},{11,7},{20,24},{24,20... | collective-permute-start | bytes 737288 | tf_op jit(solution)/shard_map/ppermute | solution.py:532
  53.2 1.9 %collective-permute-start.11 = (bf16[320,768]{1,0:T(8,128)(2,1)S(1)}, bf16[320,768]{1,0:T(8,128)(2,1)S(1)}, u32[]{:S(2)}, u32[]{:S(2)}) collective-permute-start(bf16[320,768]{1,0:T(8,128)(2,1)S(1)} %give_there.1), channel_id=1, source_target_pairs={{0,1},{1,0},{2,3},{3,2},{4,5},{5,4},{6,7},{7,6},{8,9},{9,8},{10,11... | collective-permute-start | bytes 1474568 | tf_op jit(solution)/shard_map/ppermute | solution.py:671
  54.5 6.1 %collective-permute-start.13 = (bf16[320,768]{1,0:T(8,128)(2,1)S(1)}, bf16[320,768]{1,0:T(8,128)(2,1)S(1)}, u32[]{:S(2)}, u32[]{:S(2)}) collective-permute-start(bf16[320,768]{1,0:T(8,128)(2,1)S(1)} %give_here.1), channel_id=1, source_target_pairs={{0,1},{1,0},{2,3},{3,2},{4,5},{5,4},{6,7},{7,6},{8,9},{9,8},{10,11... | collective-permute-start | bytes 1474568 | tf_op jit(solution)/shard_map/ppermute | solution.py:687
  55.2 19.4 %collective-permute-start.12 = (bf16[320,768]{1,0:T(8,128)(2,1)S(1)}, bf16[320,768]{1,0:T(8,128)(2,1)S(1)}, u32[]{:S(2)}, u32[]{:S(2)}) collective-permute-start(bf16[320,768]{1,0:T(8,128)(2,1)S(1)} %add.1), channel_id=1, source_target_pairs={{0,2},{2,0},{1,3},{3,1},{4,6},{6,4},{5,7},{7,5},{8,10},{10,8},{9,1... | collective-permute-start | bytes 1474568 | tf_op jit(solution)/shard_map/ppermute | solution.py:680
  56.8 14.5 %collective-permute-start.14 = (bf16[256,384]{1,0:T(8,128)(2,1)S(1)}, bf16[256,384]{1,0:T(8,128)(2,1)S(1)}, u32[]{:S(2)}, u32[]{:S(2)}) collective-permute-start(bf16[256,384]{1,0:T(8,128)(2,1)S(1)} %get-tuple-element.75), channel_id=1, source_target_pairs={{8,0},{4,12},{9,1},{5,13},{10,2},{6,14},{11,3},{7,15},{24,16},{20,... | collective-permute-start | bytes 589832 | tf_op jit(solution)/shard_map/ppermute | solution.py:532
  58.0 16.6 %collective-permute-start.15 = (bf16[256,384]{1,0:T(8,128)(2,1)S(1)}, bf16[256,384]{1,0:T(8,128)(2,1)S(1)}, u32[]{:S(2)}, u32[]{:S(2)}) collective-permute-start(bf16[256,384]{1,0:T(8,128)(2,1)S(1)} %get-tuple-element.76), channel_id=1, source_target_pairs={{4,0},{8,12},{5,1},{9,13},{6,2},{10,14},{7,3},{11,15},{20,16},{24,... | collective-permute-start | bytes 589832 | tf_op jit(solution)/shard_map/ppermute | solution.py:532
  59.3 15.3 %collective-permute-start.16 = (bf16[256,384]{1,0:T(8,128)(2,1)S(1)}, bf16[256,384]{1,0:T(8,128)(2,1)S(1)}, u32[]{:S(2)}, u32[]{:S(2)}) collective-permute-start(bf16[256,384]{1,0:T(8,128)(2,1)S(1)} %get-tuple-element.77), channel_id=1, source_target_pairs={{4,8},{8,4},{5,9},{9,5},{6,10},{10,6},{7,11},{11,7},{20,24},{24,20... | collective-permute-start | bytes 589832 | tf_op jit(solution)/shard_map/ppermute | solution.py:532

commit v5 on v4

--- a/solution.py
+++ b/solution.py
@@ -415,7 +415,7 @@
 
 
 def first_kernel(
-    factor, frames_new, a0, a1, a2, a3, order, alive, biases, qn, qc, e1, e3, keys, values
+    factor, frames_new, a0, a1, a2, a3, order, alive, biases, qn, qc, cn, e3, keys, values
 ):
     z = lax.axis_index("seq")
 
@@ -424,13 +424,24 @@
         places = far_places(z)
         gather_heads(places, (a0, a1, a2, a3), qc.shape[0] // 4, keys, values, qn, qc)
         attend_heads(factor, frames_new, order, alive, biases, keys, values, qn, qc)
-        hand_out(places[1], e1, slice(None), qn, qc)
         hand_out(places[3], e3, slice(None), qn, qc)
+        ctx_rows = cn.shape[0] // 2
+        fresh = qn.shape[0]
+        hdim = values.shape[2] // 2
+        spot = pl.ds(pl.multiple_of(places[1] * ctx_rows, ctx_rows), ctx_rows)
+        move = order[spot]
+        cn[:ctx_rows] = jnp.dot(
+            move, keys[fresh:], preferred_element_type=jnp.float32
+        ).astype(jnp.bfloat16)
+        for h in range(values.shape[0]):
+            cn[ctx_rows:, h * hdim : (h + 1) * hdim] = jnp.dot(
+                move, values[h, fresh:, :hdim], preferred_element_type=jnp.float32
+            ).astype(jnp.bfloat16)
 
 
 def second_kernel(
     factor, frames_new, b0, b3, b2, b1, order, alive, biases, fn, fc,
-    o0, o2, n1, n3, keys, values, qn, qc,
+    o0, o1, o2, n3, keys, values, qn, qc,
 ):
     z = lax.axis_index("seq")
     most = fn.shape[1]
@@ -440,9 +451,8 @@
         places = far_places(z)
         gather_heads(places, (b0, b1, b2, b3), qc.shape[0] // 4, keys, values, qn, qc)
         attend_heads(factor, frames_new, order, alive, biases, keys, values, qn, qc)
-        hand_out(places[1], n1, slice(None), qn, qc)
         hand_out(places[3], n3, slice(None), qn, qc)
-        for place, out in ((places[0], o0), (places[2], o2)):
+        for place, out in zip(places, (o0, o1, o2)):
             hand_out(place, out, slice(0, most), fn, fc)
             hand_out(place, out, slice(most, None), qn, qc)
 
@@ -465,7 +475,15 @@
                 at = slice(part * rows + new_rows, (part + 1) * rows)
                 kk[to, part * half : part * half + most] = a[at]
                 kk[to, part * half + most : (part + 1) * half] = b[at]
-        for place, out in zip(places, (c0, c1, c2, c3)):
+        spot = pl.ds(pl.multiple_of(places[1] * ctx_rows, ctx_rows), ctx_rows)
+        for part in range(2):
+            moved = jnp.dot(
+                order[spot],
+                kk[:, part * half + most : (part + 1) * half],
+                preferred_element_type=jnp.float32,
+            )
+            c1[part * ctx_rows : (part + 1) * ctx_rows] = moved.astype(jnp.bfloat16)
+        for place, out in ((places[0], c0), (places[2], c2), (places[3], c3)):
             part = pl.ds(pl.multiple_of(place * ctx_rows, ctx_rows), ctx_rows)
             moved = jnp.dot(order[part], kk[...], preferred_element_type=jnp.float32)
             out[:ctx_rows] = moved[:, :half].astype(jnp.bfloat16)
@@ -481,8 +499,7 @@
     return (jnp.where(low, near, far), jnp.where(low, far, near))
 
 
-def project_kernel(mine, here, e1, e3, o0, n1, n3, o2, weight, out):
-    o1 = jnp.concatenate([e1[...], n1[...]], axis=1)
+def project_kernel(mine, here, e3, o0, o1, n3, o2, weight, out):
     o3 = jnp.concatenate([e3[...], n3[...]], axis=1)
     a, b = halves(lax.axis_index("seq"), slice(None), o0, o1, o2, o3)
     mixed = jnp.concatenate([a, b], axis=1)
@@ -499,7 +516,7 @@
     out[...] = (keep[...] + came[...].astype(jnp.float32)).astype(jnp.bfloat16)
 
 
-def finish_kernel(last, keep, came, c0, c3, c1, c2, out, out_ctx, keys, values):
+def finish_kernel(last, keep, came, cn, c0, c3, cl, c2, out, out_ctx, keys, values):
     total = keep[...] + came[...].astype(jnp.float32) + last[...].astype(jnp.float32)
     total = total.astype(jnp.bfloat16)
     out[...] = total[: out.shape[0]]
@@ -507,6 +524,7 @@
     z = lax.axis_index("seq")
     ctx_rows, width = keys.shape
     half = width // 2
+    c1 = jnp.concatenate([cn[...], cl[...]], axis=1)
     for i, part in enumerate((keys, values)):
         at = slice(i * ctx_rows, (i + 1) * ctx_rows)
         a, b = halves(z, at, c0, c1, c2, c3)
@@ -603,12 +621,12 @@
             pltpu.VMEM((lanes // hdim, rows * devices, 2 * hdim), jnp.bfloat16),
         ]
 
-    fresh, held, early_beside, early_beyond = pl.pallas_call(
+    fresh, held, early_cache, early_beyond = pl.pallas_call(
         functools.partial(first_kernel, factor, frames_new),
         out_shape=[
             shape16(new_rows * devices, most),
             shape16(ctx_all, most),
-            shape16(rows, most),
+            shape16(2 * ctx_rows, most),
             shape16(rows, most),
         ],
         scratch_shapes=scratch(most),
@@ -621,7 +639,7 @@
         out_shape=[
             shape16(rows, half),
             shape16(rows, half),
-            shape16(rows, half - most),
+            shape16(rows, half),
             shape16(rows, half - most),
         ],
         scratch_shapes=scratch(half - most)
@@ -633,35 +651,39 @@
         name="attend_second",
         cost_estimate=lasts(2.4),
     )(near_b, beyond_b, across_b, beside_b, order, alive, biases, fresh, held)
-    own, across, late_beside, late_beyond = results
-    early_beside = permute(early_beside, back(BESIDE))
+    own, beside, across, late_beyond = results
+    early_cache = permute(early_cache, back(BESIDE))
     early_beyond = permute(early_beyond, back(BEYOND))
-    across = lax.optimization_barrier((across, early_beside, early_beyond))[0]
+    across = lax.optimization_barrier((across, early_cache, early_beyond))[0]
     mixed = (
-        early_beside,
         early_beyond,
         own,
-        permute(late_beside, back(BESIDE)),
+        permute(beside, back(BESIDE)),
         permute(late_beyond, back(BEYOND)),
         permute(across, ACROSS),
     )
     near_a = lax.optimization_barrier((near_a, results[0]))[0]
     caches = pl.pallas_call(
         cache_kernel,
-        out_shape=[shape16(2 * ctx_rows, half)] * 4,
+        out_shape=[
+            shape16(2 * ctx_rows, half),
+            shape16(2 * ctx_rows, half - most),
+            shape16(2 * ctx_rows, half),
+            shape16(2 * ctx_rows, half),
+        ],
         scratch_shapes=[pltpu.VMEM((ctx_all, width), jnp.bfloat16)],
         compiler_params=LIMIT,
         name="caches",
         cost_estimate=lasts(3),
     )(near_a, beside_a, across_a, beyond_a, near_b, beside_b, across_b, beyond_b, order)
 
-    mixed = lax.optimization_barrier((*mixed, caches[0]))[:6]
+    mixed = lax.optimization_barrier((*mixed, caches[0]))[:5]
 
     def project(mine, here, dtype):
         return pl.pallas_call(
             functools.partial(project_kernel, mine, here),
             out_shape=jax.ShapeDtypeStruct((rows, width), dtype),
-            in_specs=[WHOLE] * 7,
+            in_specs=[WHOLE] * 6,
             compiler_params=LIMIT,
             name=("keep" if mine else "give") + ("_here" if here else "_there"),
             cost_estimate=lasts(0.6),
@@ -682,8 +704,8 @@
     beyond = permute(caches[3], back(BEYOND))
     across = permute(caches[2], ACROSS)
     beside = permute(caches[1], back(BESIDE))
-    stored = (caches[0], beyond, beside, across)
-    mixed = lax.optimization_barrier((*mixed, keep_there))[:6]
+    stored = (early_cache, caches[0], beyond, beside, across)
+    mixed = lax.optimization_barrier((*mixed, keep_there))[:5]
     came = lax.ppermute(project(False, True, jnp.bfloat16), "tensor", SIBLING)
     keep = project(True, True, jnp.float32)
     block_out, context_out, cache_keys, cache_values = pl.pallas_call(

time: 76.1 us -> 73.9 us (0.971)
  waiting for transfers between devices: 34.6 us -> 32.4 us
    ppermute x14, waiting for transfers between devices: 34.5 us -> 31.7 us  [permute(): return lax.ppermute(x, 'seq', pairs)]
where the time goes in v5:
time: 73.9 us; the launch traced here: 73.5 us
  waiting for transfers between devices  32.4 us (44%)
  starting transfers between devices  29.7 us (40%)
  Pallas kernels  8.52 us (12%)
  local copies, waits for them, and re-layouts  2 us (3%)
  between operations  0.87 us (1%)
    ppermute x14, waiting for transfers between devices, permute(): return lax.ppermute(x, 'seq', pairs)  31.7 us
    ppermute x14, starting transfers between devices, permute(): return lax.ppermute(x, 'seq', pairs)  27.5 us
    pallas_call x1, Pallas kernels, fast_device(): pl.pallas_call(pack_kernel, out_shape=(shape16(3 * rows, most), shape16(3...  3.11 us
    pallas_call x4, Pallas kernels, project(): pl.pallas_call(functools.partial(project_kernel, mine, here), out_shape=j...  2.42 us
    unnamed x14, local copies, waits for them, and re-layouts  2 us
    pallas_call x1, Pallas kernels, fast_device(): pl.pallas_call(plan_kernel, out_shape=(shape16(ctx_all, ctx_all), jax.Sha...  1.72 us
    ppermute x1, starting transfers between devices, fast_device(): last = lax.ppermute(other, 'tensor', OPPOSITE)  1.56 us
  transfers between devices with their start and end apart: 17, of which 9 were waited for; matrix products, arithmetic and copies ran while one was open for 0% of the time, Pallas kernels for 5%

profile of v5, /device:TPU:0, one launch (start us, length us, event | category | flops | bytes accessed | tf_op | source)
XLA Modules:
  0.0 73.5 jit_solution(18165257657870263219)
XLA Ops:
  0.6 3.1 %pack.1 = (bf16[960,256]{1,0:T(8,128)(2,1)}, bf16[960,128]{1,0:T(8,128)(2,1)}, bf16[960,256]{1,0:T(8,128)(2,1)}, bf16[960,128]{1,0:T(8,128)(2,1)}) custom-call(s32[8]{0:T(128)} %levels.3, bf16[192,768]{1,0:T(8,128)(2,1)} %q.1, bf16[192,768]{1,0:T(8,128)(2,1)} %k.1, bf16[192,768]{1,0:T(8,128)(2,1)} %v.1, bf16[128,768]{1,0:T(8,128)(2,1)} %cq.1, ...), custom_call_target="tpu_custom_call" | custom-call | tf_op jit(solution)/shard_map/pack/pallas_call | solution.py:586
  3.7 6.0 %collective-permute-start.2 = (bf16[960,256]{1,0:T(8,128)(2,1)}, bf16[960,256]{1,0:T(8,128)(2,1)S(1)}, u32[]{:S(2)}, u32[]{:S(2)}) collective-permute-start(bf16[960,256]{1,0:T(8,128)(2,1)} %get-tuple-element.40), channel_id=1, source_target_pairs={{0,8},{12,4},{1,9},{13,5},{2,10},{14,6},{3,11},{15,7},{16,24},{28,... | collective-permute-start | bytes 1474568 | tf_op jit(solution)/shard_map/ppermute | solution.py:550
  9.7 0.7 collective-permute-start.1
  10.4 3.1 %collective-permute-start = (bf16[960,256]{1,0:T(8,128)(2,1)}, bf16[960,256]{1,0:T(8,128)(2,1)S(1)}, u32[]{:S(2)}, u32[]{:S(2)}) collective-permute-start(bf16[960,256]{1,0:T(8,128)(2,1)} %get-tuple-element.55.a0), channel_id=1, source_target_pairs={{0,4},{12,8},{1,5},{13,9},{2,6},{14,10},{3,7},{15,11},{16,20},{28,... | collective-permute-start | bytes 1474568 | tf_op jit(solution)/shard_map/ppermute | solution.py:550
  13.5 0.7 collective-permute-start.5
  14.2 4.0 %collective-permute-start.4 = (bf16[960,128]{1,0:T(8,128)(2,1)}, bf16[960,128]{1,0:T(8,128)(2,1)S(1)}, u32[]{:S(2)}, u32[]{:S(2)}) collective-permute-start(bf16[960,128]{1,0:T(8,128)(2,1)} %get-tuple-element.46), channel_id=1, source_target_pairs={{0,8},{12,4},{1,9},{13,5},{2,10},{14,6},{3,11},{15,7},{16,24},{28,... | collective-permute-start | bytes 737288 | tf_op jit(solution)/shard_map/ppermute | solution.py:550
  18.2 0.0 copy-start
  18.2 0.6 copy-done
  18.8 0.0 copy-start.3
  18.8 0.7 copy-done.3
  19.5 0.0 copy-start.4
  19.5 0.7 copy-done.4
  20.2 0.0 copy-start.2
  20.2 0.0 copy-start.1
  20.2 1.7 %plan.1 = (bf16[512,512]{1,0:T(8,128)(2,1)S(1)}, f32[512,128]{1,0:T(8,128)S(1)}, f32[8,512]{1,0:T(8,128)S(1)}) custom-call(s32[1,128]{1,0:T(1,128)S(1)} %bitcast.3, s32[8]{0:T(128)S(1)} %copy-done, s32[2,8]{1,0:T(2,128)S(1)} %copy-done.3), custom_call_target="tpu_custom_call" | custom-call | flops 1760000000 | tf_op jit(solution)/shard_map/plan/pallas_call | solution.py:607
  21.9 0.0 collective-permute-done.2.a3
  21.9 0.0 copy-done.2
  21.9 3.9 %collective-permute-start.6 = (bf16[960,128]{1,0:T(8,128)(2,1)S(1)}, bf16[960,128]{1,0:T(8,128)(2,1)S(1)}, u32[]{:S(2)}, u32[]{:S(2)}) collective-permute-start(bf16[960,128]{1,0:T(8,128)(2,1)S(1)} %copy-done.2), channel_id=1, source_target_pairs={{0,4},{12,8},{1,5},{13,9},{2,6},{14,10},{3,7},{15,11},{16,20},{28,... | collective-permute-start | bytes 737288 | tf_op jit(solution)/shard_map/ppermute | solution.py:550
  25.8 0.0 collective-permute-done.1.a2
  25.9 6.3 %collective-permute-done.a1 = bf16[960,256]{1,0:T(8,128)(2,1)S(1)} collective-permute-done((bf16[960,256]{1,0:T(8,128)(2,1)}, bf16[960,256]{1,0:T(8,128)(2,1)S(1)}, u32[]{:S(2)}, u32[]{:S(2)}) %collective-permute-start) | collective-permute-done | bytes 491552 | tf_op jit(solution)/shard_map/ppermute | solution.py:550
  32.2 0.0 copy-done.1
  32.2 1.3 %collective-permute-start.9 = (bf16[256,256]{1,0:T(8,128)(2,1)S(1)}, bf16[256,256]{1,0:T(8,128)(2,1)S(1)}, u32[]{:S(2)}, u32[]{:S(2)}) collective-permute-start(bf16[256,256]{1,0:T(8,128)(2,1)S(1)} %get-tuple-element.53), channel_id=1, source_target_pairs={{4,0},{8,12},{5,1},{9,13},{6,2},{10,14},{7,3},{11,15},{20,16},{24,... | collective-permute-start | bytes 393224 | tf_op jit(solution)/shard_map/ppermute | solution.py:550
  33.5 1.3 %collective-permute-start.3 = (bf16[320,256]{1,0:T(8,128)(2,1)S(1)}, bf16[320,256]{1,0:T(8,128)(2,1)S(1)}, u32[]{:S(2)}, u32[]{:S(2)}) collective-permute-start(bf16[320,256]{1,0:T(8,128)(2,1)S(1)} %get-tuple-element.44), channel_id=1, source_target_pairs={{8,0},{4,12},{9,1},{5,13},{10,2},{6,14},{11,3},{7,15},{24,16},{20,... | collective-permute-start | bytes 491528 | tf_op jit(solution)/shard_map/ppermute | solution.py:550
  34.8 0.0 collective-permute-done.5.b2
  34.8 2.7 %collective-permute-done.4.b3 = bf16[960,128]{1,0:T(8,128)(2,1)S(1)} collective-permute-done((bf16[960,128]{1,0:T(8,128)(2,1)}, bf16[960,128]{1,0:T(8,128)(2,1)S(1)}, u32[]{:S(2)}, u32[]{:S(2)}) %collective-permute-start.4) | collective-permute-done | bytes 245792 | tf_op jit(solution)/shard_map/ppermute | solution.py:550
  37.5 4.0 %collective-permute-done.6.b1 = bf16[960,128]{1,0:T(8,128)(2,1)S(1)} collective-permute-done((bf16[960,128]{1,0:T(8,128)(2,1)S(1)}, bf16[960,128]{1,0:T(8,128)(2,1)S(1)}, u32[]{:S(2)}, u32[]{:S(2)}) %collective-permute-start.6) | collective-permute-done | bytes 245792 | tf_op jit(solution)/shard_map/ppermute | solution.py:550
  41.5 1.3 %collective-permute-start.8 = (bf16[320,128]{1,0:T(8,128)(2,1)S(1)}, bf16[320,128]{1,0:T(8,128)(2,1)S(1)}, u32[]{:S(2)}, u32[]{:S(2)}) collective-permute-start(bf16[320,128]{1,0:T(8,128)(2,1)S(1)} %get-tuple-element.51), channel_id=1, source_target_pairs={{8,0},{4,12},{9,1},{5,13},{10,2},{6,14},{11,3},{7,15},{24,16},{20,... | collective-permute-start | bytes 245768 | tf_op jit(solution)/shard_map/ppermute | solution.py:550
  42.8 1.3 %collective-permute-start.7 = (bf16[320,384]{1,0:T(8,128)(2,1)S(1)}, bf16[320,384]{1,0:T(8,128)(2,1)S(1)}, u32[]{:S(2)}, u32[]{:S(2)}) collective-permute-start(bf16[320,384]{1,0:T(8,128)(2,1)S(1)} %get-tuple-element.50), channel_id=1, source_target_pairs={{4,0},{8,12},{5,1},{9,13},{6,2},{10,14},{7,3},{11,15},{20,16},{24,... | collective-permute-start | bytes 737288 | tf_op jit(solution)/shard_map/ppermute | solution.py:550
  44.1 3.2 %collective-permute-done.9.cn = bf16[256,256]{1,0:T(8,128)(2,1)S(1)} collective-permute-done((bf16[256,256]{1,0:T(8,128)(2,1)S(1)}, bf16[256,256]{1,0:T(8,128)(2,1)S(1)}, u32[]{:S(2)}, u32[]{:S(2)}) %collective-permute-start.9) | collective-permute-done | bytes 131104 | tf_op jit(solution)/shard_map/ppermute | solution.py:550
  47.3 0.0 collective-permute-done.3.e3
  47.3 0.0 slice-start
  47.3 0.0 slice-start.1
  47.3 0.8 %collective-permute-start.10 = (bf16[320,384]{1,0:T(8,128)(2,1)S(1)}, bf16[320,384]{1,0:T(8,128)(2,1)S(1)}, u32[]{:S(2)}, u32[]{:S(2)}) collective-permute-start(bf16[320,384]{1,0:T(8,128)(2,1)S(1)} %get-tuple-element.54), channel_id=1, source_target_pairs={{4,8},{8,4},{5,9},{9,5},{6,10},{10,6},{7,11},{11,7},{20,24},{24,20... | collective-permute-start | bytes 737288 | tf_op jit(solution)/shard_map/ppermute | solution.py:550
  48.1 0.2 caches.1
  48.3 3.0 %collective-permute-done.8.n3 = bf16[320,128]{1,0:T(8,128)(2,1)S(1)} collective-permute-done((bf16[320,128]{1,0:T(8,128)(2,1)S(1)}, bf16[320,128]{1,0:T(8,128)(2,1)S(1)}, u32[]{:S(2)}, u32[]{:S(2)}) %collective-permute-start.8) | collective-permute-done | bytes 81952 | tf_op jit(solution)/shard_map/ppermute | solution.py:550
  51.3 5.2 %collective-permute-done.7.o1 = bf16[320,384]{1,0:T(8,128)(2,1)S(1)} collective-permute-done((bf16[320,384]{1,0:T(8,128)(2,1)S(1)}, bf16[320,384]{1,0:T(8,128)(2,1)S(1)}, u32[]{:S(2)}, u32[]{:S(2)}) %collective-permute-start.7) | collective-permute-done | bytes 245792 | tf_op jit(solution)/shard_map/ppermute | solution.py:550
  56.5 0.0 collective-permute-done.10.o2
  56.5 0.0 slice-done
  56.5 0.0 slice-done.1
  56.5 0.6 give_there.1
  57.1 0.1 collective-permute-start.11
  57.2 0.6 keep_there.1.keep
  57.8 0.6 give_here.1
  58.5 0.5 collective-permute-start.13
  59.0 0.1 collective-permute-done.11.came
  59.1 0.1 add.1
  59.1 1.6 %collective-permute-start.12 = (bf16[320,768]{1,0:T(8,128)(2,1)S(1)}, bf16[320,768]{1,0:T(8,128)(2,1)S(1)}, u32[]{:S(2)}, u32[]{:S(2)}) collective-permute-start(bf16[320,768]{1,0:T(8,128)(2,1)S(1)} %add.1), channel_id=1, source_target_pairs={{0,2},{2,0},{1,3},{3,1},{4,6},{6,4},{5,7},{7,5},{8,10},{10,8},{9,1... | collective-permute-start | bytes 1474568 | tf_op jit(solution)/shard_map/ppermute | solution.py:702
  60.7 1.3 %collective-permute-start.14 = (bf16[256,384]{1,0:T(8,128)(2,1)S(1)}, bf16[256,384]{1,0:T(8,128)(2,1)S(1)}, u32[]{:S(2)}, u32[]{:S(2)}) collective-permute-start(bf16[256,384]{1,0:T(8,128)(2,1)S(1)} %get-tuple-element.71), channel_id=1, source_target_pairs={{8,0},{4,12},{9,1},{5,13},{10,2},{6,14},{11,3},{7,15},{24,16},{20,... | collective-permute-start | bytes 589832 | tf_op jit(solution)/shard_map/ppermute | solution.py:550
  62.0 0.7 collective-permute-start.16
  62.7 1.3 %collective-permute-start.15 = (bf16[256,128]{1,0:T(8,128)(2,1)S(1)}, bf16[256,128]{1,0:T(8,128)(2,1)S(1)}, u32[]{:S(2)}, u32[]{:S(2)}) collective-permute-start(bf16[256,128]{1,0:T(8,128)(2,1)S(1)} %get-tuple-element.72), channel_id=1, source_target_pairs={{4,0},{8,12},{5,1},{9,13},{6,2},{10,14},{7,3},{11,15},{20,16},{24,... | collective-permute-start | bytes 196616 | tf_op jit(solution)/shard_map/ppermute | solution.py:550
  64.0 0.6 keep_here.1.keep
  64.6 0.0 collective-permute-done.13.came
  64.6 7.3 %collective-permute-done.15.cl = bf16[256,128]{1,0:T(8,128)(2,1)S(1)} collective-permute-done((bf16[256,128]{1,0:T(8,128)(2,1)S(1)}, bf16[256,128]{1,0:T(8,128)(2,1)S(1)}, u32[]{:S(2)}, u32[]{:S(2)}) %collective-permute-start.15) | collective-permute-done | bytes 65568 | tf_op jit(solution)/shard_map/ppermute | solution.py:550
  71.9 0.0 collective-permute-done.14.c3
  71.9 0.0 collective-permute-done.16.c2
  71.9 0.6 collective-permute-done.12.last
  72.5 1.0 %finish.1 = (bf16[192,768]{1,0:T(8,128)(2,1)}, bf16[128,768]{1,0:T(8,128)(2,1)}, bf16[128,768]{1,0:T(8,128)(2,1)}, bf16[128,768]{1,0:T(8,128)(2,1)}) custom-call(bf16[320,768]{1,0:T(8,128)(2,1)S(1)} %collective-permute-done.12.last, f32[320,768]{1,0:T(8,128)S(1)} %keep_here.1.keep, bf16[320,768]{1,0:T(8,128)(2,1)S(1)} %collective-permute-done.13.came, ...), custom_call_target="tpu_custom_call" | custom-call | flops 1100000000 | tf_op jit(solution)/shard_map/finish/pallas_call | solution.py:711
  (3 shorter events, 0.0 us)
Async XLA Ops:
  3.7 18.1 %collective-permute-start.2 = (bf16[960,256]{1,0:T(8,128)(2,1)}, bf16[960,256]{1,0:T(8,128)(2,1)S(1)}, u32[]{:S(2)}, u32[]{:S(2)}) collective-permute-start(bf16[960,256]{1,0:T(8,128)(2,1)} %get-tuple-element.40), channel_id=1, source_target_pairs={{0,8},{12,4},{1,9},{13,5},{2,10},{14,6},{3,11},{15,7},{16,24},{28,... | collective-permute-start | bytes 1474568 | tf_op jit(solution)/shard_map/ppermute | solution.py:550
  9.7 16.1 %collective-permute-start.1 = (bf16[960,256]{1,0:T(8,128)(2,1)}, bf16[960,256]{1,0:T(8,128)(2,1)S(1)}, u32[]{:S(2)}, u32[]{:S(2)}) collective-permute-start(bf16[960,256]{1,0:T(8,128)(2,1)} %get-tuple-element.40), channel_id=1, source_target_pairs={{4,8},{8,4},{5,9},{9,5},{6,10},{10,6},{7,11},{11,7},{20,24},{24,20... | collective-permute-start | bytes 1474568 | tf_op jit(solution)/shard_map/ppermute | solution.py:550
  10.4 21.8 %collective-permute-start = (bf16[960,256]{1,0:T(8,128)(2,1)}, bf16[960,256]{1,0:T(8,128)(2,1)S(1)}, u32[]{:S(2)}, u32[]{:S(2)}) collective-permute-start(bf16[960,256]{1,0:T(8,128)(2,1)} %get-tuple-element.55.a0), channel_id=1, source_target_pairs={{0,4},{12,8},{1,5},{13,9},{2,6},{14,10},{3,7},{15,11},{16,20},{28,... | collective-permute-start | bytes 1474568 | tf_op jit(solution)/shard_map/ppermute | solution.py:550
  13.5 21.3 %collective-permute-start.5 = (bf16[960,128]{1,0:T(8,128)(2,1)}, bf16[960,128]{1,0:T(8,128)(2,1)S(1)}, u32[]{:S(2)}, u32[]{:S(2)}) collective-permute-start(bf16[960,128]{1,0:T(8,128)(2,1)} %get-tuple-element.46), channel_id=1, source_target_pairs={{4,8},{8,4},{5,9},{9,5},{6,10},{10,6},{7,11},{11,7},{20,24},{24,20... | collective-permute-start | bytes 737288 | tf_op jit(solution)/shard_map/ppermute | solution.py:550
  14.2 23.3 %collective-permute-start.4 = (bf16[960,128]{1,0:T(8,128)(2,1)}, bf16[960,128]{1,0:T(8,128)(2,1)S(1)}, u32[]{:S(2)}, u32[]{:S(2)}) collective-permute-start(bf16[960,128]{1,0:T(8,128)(2,1)} %get-tuple-element.46), channel_id=1, source_target_pairs={{0,8},{12,4},{1,9},{13,5},{2,10},{14,6},{3,11},{15,7},{16,24},{28,... | collective-permute-start | bytes 737288 | tf_op jit(solution)/shard_map/ppermute | solution.py:550
  18.2 0.7 copy-start
  18.8 0.7 copy-start.3
  19.5 0.7 copy-start.4
  20.2 1.7 %copy-start.2 = (bf16[960,128]{1,0:T(8,128)(2,1)S(1)}, bf16[960,128]{1,0:T(8,128)(2,1)}, u32[]{:S(2)}) copy-start(bf16[960,128]{1,0:T(8,128)(2,1)} %get-tuple-element.45.b0) | copy-start | bytes 737284
  20.2 12.0 %copy-start.1 = (bf16[960,256]{1,0:T(8,128)(2,1)S(1)}, bf16[960,256]{1,0:T(8,128)(2,1)}, u32[]{:S(2)}) copy-start(bf16[960,256]{1,0:T(8,128)(2,1)} %get-tuple-element.55.a0) | copy-start | bytes 1474564
  21.9 19.6 %collective-permute-start.6 = (bf16[960,128]{1,0:T(8,128)(2,1)S(1)}, bf16[960,128]{1,0:T(8,128)(2,1)S(1)}, u32[]{:S(2)}, u32[]{:S(2)}) collective-permute-start(bf16[960,128]{1,0:T(8,128)(2,1)S(1)} %copy-done.2), channel_id=1, source_target_pairs={{0,4},{12,8},{1,5},{13,9},{2,6},{14,10},{3,7},{15,11},{16,20},{28,... | collective-permute-start | bytes 737288 | tf_op jit(solution)/shard_map/ppermute | solution.py:550
  32.2 15.1 %collective-permute-start.9 = (bf16[256,256]{1,0:T(8,128)(2,1)S(1)}, bf16[256,256]{1,0:T(8,128)(2,1)S(1)}, u32[]{:S(2)}, u32[]{:S(2)}) collective-permute-start(bf16[256,256]{1,0:T(8,128)(2,1)S(1)} %get-tuple-element.53), channel_id=1, source_target_pairs={{4,0},{8,12},{5,1},{9,13},{6,2},{10,14},{7,3},{11,15},{20,16},{24,... | collective-permute-start | bytes 393224 | tf_op jit(solution)/shard_map/ppermute | solution.py:550
  33.5 13.8 %collective-permute-start.3 = (bf16[320,256]{1,0:T(8,128)(2,1)S(1)}, bf16[320,256]{1,0:T(8,128)(2,1)S(1)}, u32[]{:S(2)}, u32[]{:S(2)}) collective-permute-start(bf16[320,256]{1,0:T(8,128)(2,1)S(1)} %get-tuple-element.44), channel_id=1, source_target_pairs={{8,0},{4,12},{9,1},{5,13},{10,2},{6,14},{11,3},{7,15},{24,16},{20,... | collective-permute-start | bytes 491528 | tf_op jit(solution)/shard_map/ppermute | solution.py:550
  41.5 9.8 %collective-permute-start.8 = (bf16[320,128]{1,0:T(8,128)(2,1)S(1)}, bf16[320,128]{1,0:T(8,128)(2,1)S(1)}, u32[]{:S(2)}, u32[]{:S(2)}) collective-permute-start(bf16[320,128]{1,0:T(8,128)(2,1)S(1)} %get-tuple-element.51), channel_id=1, source_target_pairs={{8,0},{4,12},{9,1},{5,13},{10,2},{6,14},{11,3},{7,15},{24,16},{20,... | collective-permute-start | bytes 245768 | tf_op jit(solution)/shard_map/ppermute | solution.py:550
  42.8 13.7 %collective-permute-start.7 = (bf16[320,384]{1,0:T(8,128)(2,1)S(1)}, bf16[320,384]{1,0:T(8,128)(2,1)S(1)}, u32[]{:S(2)}, u32[]{:S(2)}) collective-permute-start(bf16[320,384]{1,0:T(8,128)(2,1)S(1)} %get-tuple-element.50), channel_id=1, source_target_pairs={{4,0},{8,12},{5,1},{9,13},{6,2},{10,14},{7,3},{11,15},{20,16},{24,... | collective-permute-start | bytes 737288 | tf_op jit(solution)/shard_map/ppermute | solution.py:550
  47.3 9.2 %slice-start = ((s8[4718592]{0:T(1024)(128)(4,1)}), s8[4194304]{0:T(1024)(128)(4,1)S(1)}, s32[]{:S(2)}) async-start(s8[4718592]{0:T(1024)(128)(4,1)} %bitcast.1), calls=%async_computation | async-start | bytes 8388608
  47.3 9.2 %slice-start.1 = ((s8[4718592]{0:T(1024)(128)(4,1)}), s8[524288]{0:T(1024)(128)(4,1)S(1)}, s32[]{:S(2)}) async-start(s8[4718592]{0:T(1024)(128)(4,1)} %bitcast.1), calls=%async_computation.1 | async-start | bytes 1048576
  47.3 9.2 %collective-permute-start.10 = (bf16[320,384]{1,0:T(8,128)(2,1)S(1)}, bf16[320,384]{1,0:T(8,128)(2,1)S(1)}, u32[]{:S(2)}, u32[]{:S(2)}) collective-permute-start(bf16[320,384]{1,0:T(8,128)(2,1)S(1)} %get-tuple-element.54), channel_id=1, source_target_pairs={{4,8},{8,4},{5,9},{9,5},{6,10},{10,6},{7,11},{11,7},{20,24},{24,20... | collective-permute-start | bytes 737288 | tf_op jit(solution)/shard_map/ppermute | solution.py:550
  57.1 1.9 %collective-permute-start.11 = (bf16[320,768]{1,0:T(8,128)(2,1)S(1)}, bf16[320,768]{1,0:T(8,128)(2,1)S(1)}, u32[]{:S(2)}, u32[]{:S(2)}) collective-permute-start(bf16[320,768]{1,0:T(8,128)(2,1)S(1)} %give_there.1), channel_id=1, source_target_pairs={{0,1},{1,0},{2,3},{3,2},{4,5},{5,4},{6,7},{7,6},{8,9},{9,8},{10,11... | collective-permute-start | bytes 1474568 | tf_op jit(solution)/shard_map/ppermute | solution.py:693
  58.5 6.1 %collective-permute-start.13 = (bf16[320,768]{1,0:T(8,128)(2,1)S(1)}, bf16[320,768]{1,0:T(8,128)(2,1)S(1)}, u32[]{:S(2)}, u32[]{:S(2)}) collective-permute-start(bf16[320,768]{1,0:T(8,128)(2,1)S(1)} %give_here.1), channel_id=1, source_target_pairs={{0,1},{1,0},{2,3},{3,2},{4,5},{5,4},{6,7},{7,6},{8,9},{9,8},{10,11... | collective-permute-start | bytes 1474568 | tf_op jit(solution)/shard_map/ppermute | solution.py:709
  59.1 13.3 %collective-permute-start.12 = (bf16[320,768]{1,0:T(8,128)(2,1)S(1)}, bf16[320,768]{1,0:T(8,128)(2,1)S(1)}, u32[]{:S(2)}, u32[]{:S(2)}) collective-permute-start(bf16[320,768]{1,0:T(8,128)(2,1)S(1)} %add.1), channel_id=1, source_target_pairs={{0,2},{2,0},{1,3},{3,1},{4,6},{6,4},{5,7},{7,5},{8,10},{10,8},{9,1... | collective-permute-start | bytes 1474568 | tf_op jit(solution)/shard_map/ppermute | solution.py:702
  60.7 11.2 %collective-permute-start.14 = (bf16[256,384]{1,0:T(8,128)(2,1)S(1)}, bf16[256,384]{1,0:T(8,128)(2,1)S(1)}, u32[]{:S(2)}, u32[]{:S(2)}) collective-permute-start(bf16[256,384]{1,0:T(8,128)(2,1)S(1)} %get-tuple-element.71), channel_id=1, source_target_pairs={{8,0},{4,12},{9,1},{5,13},{10,2},{6,14},{11,3},{7,15},{24,16},{20,... | collective-permute-start | bytes 589832 | tf_op jit(solution)/shard_map/ppermute | solution.py:550
  62.0 9.9 %collective-permute-start.16 = (bf16[256,384]{1,0:T(8,128)(2,1)S(1)}, bf16[256,384]{1,0:T(8,128)(2,1)S(1)}, u32[]{:S(2)}, u32[]{:S(2)}) collective-permute-start(bf16[256,384]{1,0:T(8,128)(2,1)S(1)} %get-tuple-element.73), channel_id=1, source_target_pairs={{4,8},{8,4},{5,9},{9,5},{6,10},{10,6},{7,11},{11,7},{20,24},{24,20... | collective-permute-start | bytes 589832 | tf_op jit(solution)/shard_map/ppermute | solution.py:550
  62.7 9.2 %collective-permute-start.15 = (bf16[256,128]{1,0:T(8,128)(2,1)S(1)}, bf16[256,128]{1,0:T(8,128)(2,1)S(1)}, u32[]{:S(2)}, u32[]{:S(2)}) collective-permute-start(bf16[256,128]{1,0:T(8,128)(2,1)S(1)} %get-tuple-element.72), channel_id=1, source_target_pairs={{4,0},{8,12},{5,1},{9,13},{6,2},{10,14},{7,3},{11,15},{20,16},{24,... | collective-permute-start | bytes 196616 | tf_op jit(solution)/shard_map/ppermute | solution.py:550

commit v6 on v5

--- a/solution.py
+++ b/solution.py
@@ -224,7 +224,8 @@
 
 
 def pack_kernel(
-    levels, q, k, v, cq, ck, cv, near_a, near_b, far_a, far_b, lv, sk, sv, sq, sems
+    levels, q, k, v, cq, ck, cv, near_a, near_b, far_a, far_b,
+    lv, nk, nv, nq, sk, sv, sq, tk, tv, tq, sems,
 ):
     z = lax.axis_index("seq")
     devices = lax.axis_size("seq")
@@ -250,25 +251,29 @@
         started.append(copy)
         return copy
 
+    def send(src, base):
+        for out, lanes in places:
+            start(src.at[:, lanes], out.at[base : base + src.shape[0]])
+
     reads = [start(levels, lv), start(ck, sk), start(cv, sv), start(cq, sq)]
-    for out, lanes in places:
-        for part, fresh in enumerate((k, v, q)):
-            start(fresh.at[:, lanes], out.at[part * rows : part * rows + new_rows])
+    reads += [start(k, nk), start(v, nv), start(q, nq)]
     reads[0].wait()
     index = place_index((ctx_rows, 1), 0)
     first = index % 4 == 0
     frame = (z * ctx_rows + index) * frames_ctx // (devices * ctx_rows)
     coarse = coarse_of(frame, lv, frames_ctx)
-    for part, src in enumerate((sk, sv, sq)):
+    for part, (src, dst) in enumerate(((sk, tk), (sv, tv), (sq, tq))):
         reads[part + 1].wait()
         wide = src[...].astype(jnp.float32)
         pair = wide + pltpu.roll(wide, ctx_rows - 1, 0)
         quad = pair + pltpu.roll(pair, ctx_rows - 2, 0)
         mean = jnp.where(first, quad * 0.25, 0.0)
-        src[...] = jnp.where(coarse, mean, wide).astype(jnp.bfloat16)
-        for out, lanes in places:
-            out[part * rows + new_rows : (part + 1) * rows] = src[:, lanes]
-    for copy in started[4:]:
+        dst[...] = jnp.where(coarse, mean, wide).astype(jnp.bfloat16)
+        send(dst, part * rows + new_rows)
+    for part, src in enumerate((nk, nv, nq)):
+        reads[part + 4].wait()
+        send(src, part * rows)
+    for copy in started[7:]:
         copy.wait()
 
 
@@ -516,7 +521,7 @@
     out[...] = (keep[...] + came[...].astype(jnp.float32)).astype(jnp.bfloat16)
 
 
-def finish_kernel(last, keep, came, cn, c0, c3, cl, c2, out, out_ctx, keys, values):
+def finish_kernel(last, keep, came, cn, c0, cl, c3, c2, out, out_ctx, keys, values):
     total = keep[...] + came[...].astype(jnp.float32) + last[...].astype(jnp.float32)
     total = total.astype(jnp.bfloat16)
     out[...] = total[: out.shape[0]]
@@ -592,10 +597,11 @@
             shape16(3 * rows, half - most),
         ),
         in_specs=[AWAY] * 7,
-        out_specs=[WHOLE] * 4,
+        out_specs=[AWAY] * 4,
         scratch_shapes=[pltpu.SMEM(levels.shape, jnp.int32)]
-        + [pltpu.VMEM((ctx_rows, width), jnp.bfloat16)] * 3
-        + [pltpu.SemaphoreType.DMA((16,))],
+        + [pltpu.VMEM((new_rows, width), jnp.bfloat16)] * 3
+        + [pltpu.VMEM((ctx_rows, width), jnp.bfloat16)] * 6
+        + [pltpu.SemaphoreType.DMA((31,))],
         name="pack",
     )(levels, queries, new_keys, new_values, context_queries, context_keys, context_values)
     beside_a = permute(near_a, BESIDE)
@@ -704,7 +710,7 @@
     beyond = permute(caches[3], back(BEYOND))
     across = permute(caches[2], ACROSS)
     beside = permute(caches[1], back(BESIDE))
-    stored = (early_cache, caches[0], beyond, beside, across)
+    stored = (early_cache, caches[0], beside, beyond, across)
     mixed = lax.optimization_barrier((*mixed, keep_there))[:5]
     came = lax.ppermute(project(False, True, jnp.bfloat16), "tensor", SIBLING)
     keep = project(True, True, jnp.float32)

time: 73.9 us -> 73.4 us (level)
  no operation moved by 1% of the time
where the time goes in v6:
time: 73.4 us; the launch traced here: 73 us
  waiting for transfers between devices  32.4 us (44%)
  starting transfers between devices  29.7 us (40%)
  Pallas kernels  8.07 us (11%)
  local copies, waits for them, and re-layouts  2 us (3%)
  between operations  0.87 us (1%)
    ppermute x14, waiting for transfers between devices, permute(): return lax.ppermute(x, 'seq', pairs)  31.7 us
    ppermute x14, starting transfers between devices, permute(): return lax.ppermute(x, 'seq', pairs)  27.5 us
    pallas_call x1, Pallas kernels, fast_device(): pl.pallas_call(pack_kernel, out_shape=(shape16(3 * rows, most), shape16(3...  2.67 us
    pallas_call x4, Pallas kernels, project(): pl.pallas_call(functools.partial(project_kernel, mine, here), out_shape=j...  2.41 us
    unnamed x14, local copies, waits for them, and re-layouts  2 us
    pallas_call x1, Pallas kernels, fast_device(): pl.pallas_call(plan_kernel, out_shape=(shape16(ctx_all, ctx_all), jax.Sha...  1.72 us
    ppermute x1, starting transfers between devices, fast_device(): last = lax.ppermute(other, 'tensor', OPPOSITE)  1.57 us
  transfers between devices with their start and end apart: 17, of which 9 were waited for; matrix products, arithmetic and copies ran while one was open for 0% of the time, Pallas kernels for 5%

profile of v6, /device:TPU:0, one launch (start us, length us, event | category | flops | bytes accessed | tf_op | source)
XLA Modules:
  0.0 73.0 jit_solution(11715414745783058910)
XLA Ops:
  0.6 2.7 %pack.1 = (bf16[960,256]{1,0:T(8,128)(2,1)}, bf16[960,128]{1,0:T(8,128)(2,1)}, bf16[960,256]{1,0:T(8,128)(2,1)}, bf16[960,128]{1,0:T(8,128)(2,1)}) custom-call(s32[8]{0:T(128)} %levels.3, bf16[192,768]{1,0:T(8,128)(2,1)} %q.1, bf16[192,768]{1,0:T(8,128)(2,1)} %k.1, bf16[192,768]{1,0:T(8,128)(2,1)} %v.1, bf16[128,768]{1,0:T(8,128)(2,1)} %cq.1, ...), custom_call_target="tpu_custom_call" | custom-call | tf_op jit(solution)/shard_map/pack/pallas_call | solution.py:591
  3.3 6.0 %collective-permute-start.2 = (bf16[960,256]{1,0:T(8,128)(2,1)}, bf16[960,256]{1,0:T(8,128)(2,1)S(1)}, u32[]{:S(2)}, u32[]{:S(2)}) collective-permute-start(bf16[960,256]{1,0:T(8,128)(2,1)} %get-tuple-element.40), channel_id=1, source_target_pairs={{0,8},{12,4},{1,9},{13,5},{2,10},{14,6},{3,11},{15,7},{16,24},{28,... | collective-permute-start | bytes 1474568 | tf_op jit(solution)/shard_map/ppermute | solution.py:555
  9.3 0.7 collective-permute-start.1
  10.0 3.1 %collective-permute-start = (bf16[960,256]{1,0:T(8,128)(2,1)}, bf16[960,256]{1,0:T(8,128)(2,1)S(1)}, u32[]{:S(2)}, u32[]{:S(2)}) collective-permute-start(bf16[960,256]{1,0:T(8,128)(2,1)} %get-tuple-element.55.a0), channel_id=1, source_target_pairs={{0,4},{12,8},{1,5},{13,9},{2,6},{14,10},{3,7},{15,11},{16,20},{28,... | collective-permute-start | bytes 1474568 | tf_op jit(solution)/shard_map/ppermute | solution.py:555
  13.1 0.7 collective-permute-start.5
  13.8 4.0 %collective-permute-start.4 = (bf16[960,128]{1,0:T(8,128)(2,1)}, bf16[960,128]{1,0:T(8,128)(2,1)S(1)}, u32[]{:S(2)}, u32[]{:S(2)}) collective-permute-start(bf16[960,128]{1,0:T(8,128)(2,1)} %get-tuple-element.46), channel_id=1, source_target_pairs={{0,8},{12,4},{1,9},{13,5},{2,10},{14,6},{3,11},{15,7},{16,24},{28,... | collective-permute-start | bytes 737288 | tf_op jit(solution)/shard_map/ppermute | solution.py:555
  17.7 0.0 copy-start
  17.7 0.6 copy-done
  18.4 0.0 copy-start.3
  18.4 0.7 copy-done.3
  19.1 0.0 copy-start.4
  19.1 0.7 copy-done.4
  19.7 0.0 copy-start.2
  19.7 0.0 copy-start.1
  19.7 1.7 %plan.1 = (bf16[512,512]{1,0:T(8,128)(2,1)S(1)}, f32[512,128]{1,0:T(8,128)S(1)}, f32[8,512]{1,0:T(8,128)S(1)}) custom-call(s32[1,128]{1,0:T(1,128)S(1)} %bitcast.3, s32[8]{0:T(128)S(1)} %copy-done, s32[2,8]{1,0:T(2,128)S(1)} %copy-done.3), custom_call_target="tpu_custom_call" | custom-call | flops 1760000000 | tf_op jit(solution)/shard_map/plan/pallas_call | solution.py:613
  21.5 0.0 collective-permute-done.2.a3
  21.5 0.0 copy-done.2
  21.5 3.9 %collective-permute-start.6 = (bf16[960,128]{1,0:T(8,128)(2,1)S(1)}, bf16[960,128]{1,0:T(8,128)(2,1)S(1)}, u32[]{:S(2)}, u32[]{:S(2)}) collective-permute-start(bf16[960,128]{1,0:T(8,128)(2,1)S(1)} %copy-done.2), channel_id=1, source_target_pairs={{0,4},{12,8},{1,5},{13,9},{2,6},{14,10},{3,7},{15,11},{16,20},{28,... | collective-permute-start | bytes 737288 | tf_op jit(solution)/shard_map/ppermute | solution.py:555
  25.4 0.0 collective-permute-done.1.a2
  25.4 6.3 %collective-permute-done.a1 = bf16[960,256]{1,0:T(8,128)(2,1)S(1)} collective-permute-done((bf16[960,256]{1,0:T(8,128)(2,1)}, bf16[960,256]{1,0:T(8,128)(2,1)S(1)}, u32[]{:S(2)}, u32[]{:S(2)}) %collective-permute-start) | collective-permute-done | bytes 491552 | tf_op jit(solution)/shard_map/ppermute | solution.py:555
  31.8 0.0 copy-done.1
  31.8 1.3 %collective-permute-start.9 = (bf16[256,256]{1,0:T(8,128)(2,1)S(1)}, bf16[256,256]{1,0:T(8,128)(2,1)S(1)}, u32[]{:S(2)}, u32[]{:S(2)}) collective-permute-start(bf16[256,256]{1,0:T(8,128)(2,1)S(1)} %get-tuple-element.53), channel_id=1, source_target_pairs={{4,0},{8,12},{5,1},{9,13},{6,2},{10,14},{7,3},{11,15},{20,16},{24,... | collective-permute-start | bytes 393224 | tf_op jit(solution)/shard_map/ppermute | solution.py:555
  33.1 1.3 %collective-permute-start.3 = (bf16[320,256]{1,0:T(8,128)(2,1)S(1)}, bf16[320,256]{1,0:T(8,128)(2,1)S(1)}, u32[]{:S(2)}, u32[]{:S(2)}) collective-permute-start(bf16[320,256]{1,0:T(8,128)(2,1)S(1)} %get-tuple-element.44), channel_id=1, source_target_pairs={{8,0},{4,12},{9,1},{5,13},{10,2},{6,14},{11,3},{7,15},{24,16},{20,... | collective-permute-start | bytes 491528 | tf_op jit(solution)/shard_map/ppermute | solution.py:555
  34.4 0.0 collective-permute-done.5.b2
  34.4 2.7 %collective-permute-done.4.b3 = bf16[960,128]{1,0:T(8,128)(2,1)S(1)} collective-permute-done((bf16[960,128]{1,0:T(8,128)(2,1)}, bf16[960,128]{1,0:T(8,128)(2,1)S(1)}, u32[]{:S(2)}, u32[]{:S(2)}) %collective-permute-start.4) | collective-permute-done | bytes 245792 | tf_op jit(solution)/shard_map/ppermute | solution.py:555
  37.1 4.0 %collective-permute-done.6.b1 = bf16[960,128]{1,0:T(8,128)(2,1)S(1)} collective-permute-done((bf16[960,128]{1,0:T(8,128)(2,1)S(1)}, bf16[960,128]{1,0:T(8,128)(2,1)S(1)}, u32[]{:S(2)}, u32[]{:S(2)}) %collective-permute-start.6) | collective-permute-done | bytes 245792 | tf_op jit(solution)/shard_map/ppermute | solution.py:555
  41.1 1.3 %collective-permute-start.8 = (bf16[320,128]{1,0:T(8,128)(2,1)S(1)}, bf16[320,128]{1,0:T(8,128)(2,1)S(1)}, u32[]{:S(2)}, u32[]{:S(2)}) collective-permute-start(bf16[320,128]{1,0:T(8,128)(2,1)S(1)} %get-tuple-element.51), channel_id=1, source_target_pairs={{8,0},{4,12},{9,1},{5,13},{10,2},{6,14},{11,3},{7,15},{24,16},{20,... | collective-permute-start | bytes 245768 | tf_op jit(solution)/shard_map/ppermute | solution.py:555
  42.4 1.3 %collective-permute-start.7 = (bf16[320,384]{1,0:T(8,128)(2,1)S(1)}, bf16[320,384]{1,0:T(8,128)(2,1)S(1)}, u32[]{:S(2)}, u32[]{:S(2)}) collective-permute-start(bf16[320,384]{1,0:T(8,128)(2,1)S(1)} %get-tuple-element.50), channel_id=1, source_target_pairs={{4,0},{8,12},{5,1},{9,13},{6,2},{10,14},{7,3},{11,15},{20,16},{24,... | collective-permute-start | bytes 737288 | tf_op jit(solution)/shard_map/ppermute | solution.py:555
  43.7 3.2 %collective-permute-done.9.cn = bf16[256,256]{1,0:T(8,128)(2,1)S(1)} collective-permute-done((bf16[256,256]{1,0:T(8,128)(2,1)S(1)}, bf16[256,256]{1,0:T(8,128)(2,1)S(1)}, u32[]{:S(2)}, u32[]{:S(2)}) %collective-permute-start.9) | collective-permute-done | bytes 131104 | tf_op jit(solution)/shard_map/ppermute | solution.py:555
  46.9 0.0 collective-permute-done.3.e3
  46.9 0.0 slice-start
  46.9 0.0 slice-start.1
  46.9 0.8 %collective-permute-start.10 = (bf16[320,384]{1,0:T(8,128)(2,1)S(1)}, bf16[320,384]{1,0:T(8,128)(2,1)S(1)}, u32[]{:S(2)}, u32[]{:S(2)}) collective-permute-start(bf16[320,384]{1,0:T(8,128)(2,1)S(1)} %get-tuple-element.54), channel_id=1, source_target_pairs={{4,8},{8,4},{5,9},{9,5},{6,10},{10,6},{7,11},{11,7},{20,24},{24,20... | collective-permute-start | bytes 737288 | tf_op jit(solution)/shard_map/ppermute | solution.py:555
  47.7 0.2 caches.1
  47.9 3.0 %collective-permute-done.8.n3 = bf16[320,128]{1,0:T(8,128)(2,1)S(1)} collective-permute-done((bf16[320,128]{1,0:T(8,128)(2,1)S(1)}, bf16[320,128]{1,0:T(8,128)(2,1)S(1)}, u32[]{:S(2)}, u32[]{:S(2)}) %collective-permute-start.8) | collective-permute-done | bytes 81952 | tf_op jit(solution)/shard_map/ppermute | solution.py:555
  50.9 5.2 %collective-permute-done.7.o1 = bf16[320,384]{1,0:T(8,128)(2,1)S(1)} collective-permute-done((bf16[320,384]{1,0:T(8,128)(2,1)S(1)}, bf16[320,384]{1,0:T(8,128)(2,1)S(1)}, u32[]{:S(2)}, u32[]{:S(2)}) %collective-permute-start.7) | collective-permute-done | bytes 245792 | tf_op jit(solution)/shard_map/ppermute | solution.py:555
  56.1 0.0 collective-permute-done.10.o2
  56.1 0.0 slice-done
  56.1 0.0 slice-done.1
  56.1 0.6 give_there.1
  56.7 0.1 collective-permute-start.11
  56.8 0.6 keep_there.1.keep
  57.4 0.6 give_here.1
  58.1 0.5 collective-permute-start.13
  58.5 0.1 collective-permute-done.11.came
  58.6 0.1 add.1
  58.7 1.6 %collective-permute-start.12 = (bf16[320,768]{1,0:T(8,128)(2,1)S(1)}, bf16[320,768]{1,0:T(8,128)(2,1)S(1)}, u32[]{:S(2)}, u32[]{:S(2)}) collective-permute-start(bf16[320,768]{1,0:T(8,128)(2,1)S(1)} %add.1), channel_id=1, source_target_pairs={{0,2},{2,0},{1,3},{3,1},{4,6},{6,4},{5,7},{7,5},{8,10},{10,8},{9,1... | collective-permute-start | bytes 1474568 | tf_op jit(solution)/shard_map/ppermute | solution.py:708
  60.3 1.3 %collective-permute-start.15 = (bf16[256,384]{1,0:T(8,128)(2,1)S(1)}, bf16[256,384]{1,0:T(8,128)(2,1)S(1)}, u32[]{:S(2)}, u32[]{:S(2)}) collective-permute-start(bf16[256,384]{1,0:T(8,128)(2,1)S(1)} %get-tuple-element.72), channel_id=1, source_target_pairs={{8,0},{4,12},{9,1},{5,13},{10,2},{6,14},{11,3},{7,15},{24,16},{20,... | collective-permute-start | bytes 589832 | tf_op jit(solution)/shard_map/ppermute | solution.py:555
  61.6 0.7 collective-permute-start.16
  62.3 1.3 %collective-permute-start.14 = (bf16[256,128]{1,0:T(8,128)(2,1)S(1)}, bf16[256,128]{1,0:T(8,128)(2,1)S(1)}, u32[]{:S(2)}, u32[]{:S(2)}) collective-permute-start(bf16[256,128]{1,0:T(8,128)(2,1)S(1)} %get-tuple-element.71), channel_id=1, source_target_pairs={{4,0},{8,12},{5,1},{9,13},{6,2},{10,14},{7,3},{11,15},{20,16},{24,... | collective-permute-start | bytes 196616 | tf_op jit(solution)/shard_map/ppermute | solution.py:555
  63.6 0.6 keep_here.1.keep
  64.2 0.0 collective-permute-done.13.came
  64.2 7.3 %collective-permute-done.14.cl = bf16[256,128]{1,0:T(8,128)(2,1)S(1)} collective-permute-done((bf16[256,128]{1,0:T(8,128)(2,1)S(1)}, bf16[256,128]{1,0:T(8,128)(2,1)S(1)}, u32[]{:S(2)}, u32[]{:S(2)}) %collective-permute-start.14) | collective-permute-done | bytes 65568 | tf_op jit(solution)/shard_map/ppermute | solution.py:555
  71.5 0.0 collective-permute-done.15.c3
  71.5 0.0 collective-permute-done.16.c2
  71.5 0.6 collective-permute-done.12.last
  72.0 1.0 %finish.1 = (bf16[192,768]{1,0:T(8,128)(2,1)}, bf16[128,768]{1,0:T(8,128)(2,1)}, bf16[128,768]{1,0:T(8,128)(2,1)}, bf16[128,768]{1,0:T(8,128)(2,1)}) custom-call(bf16[320,768]{1,0:T(8,128)(2,1)S(1)} %collective-permute-done.12.last, f32[320,768]{1,0:T(8,128)S(1)} %keep_here.1.keep, bf16[320,768]{1,0:T(8,128)(2,1)S(1)} %collective-permute-done.13.came, ...), custom_call_target="tpu_custom_call" | custom-call | flops 1100000000 | tf_op jit(solution)/shard_map/finish/pallas_call | solution.py:717
  (3 shorter events, 0.0 us)
Async XLA Ops:
  3.3 18.1 %collective-permute-start.2 = (bf16[960,256]{1,0:T(8,128)(2,1)}, bf16[960,256]{1,0:T(8,128)(2,1)S(1)}, u32[]{:S(2)}, u32[]{:S(2)}) collective-permute-start(bf16[960,256]{1,0:T(8,128)(2,1)} %get-tuple-element.40), channel_id=1, source_target_pairs={{0,8},{12,4},{1,9},{13,5},{2,10},{14,6},{3,11},{15,7},{16,24},{28,... | collective-permute-start | bytes 1474568 | tf_op jit(solution)/shard_map/ppermute | solution.py:555
  9.3 16.1 %collective-permute-start.1 = (bf16[960,256]{1,0:T(8,128)(2,1)}, bf16[960,256]{1,0:T(8,128)(2,1)S(1)}, u32[]{:S(2)}, u32[]{:S(2)}) collective-permute-start(bf16[960,256]{1,0:T(8,128)(2,1)} %get-tuple-element.40), channel_id=1, source_target_pairs={{4,8},{8,4},{5,9},{9,5},{6,10},{10,6},{7,11},{11,7},{20,24},{24,20... | collective-permute-start | bytes 1474568 | tf_op jit(solution)/shard_map/ppermute | solution.py:555
  10.0 21.8 %collective-permute-start = (bf16[960,256]{1,0:T(8,128)(2,1)}, bf16[960,256]{1,0:T(8,128)(2,1)S(1)}, u32[]{:S(2)}, u32[]{:S(2)}) collective-permute-start(bf16[960,256]{1,0:T(8,128)(2,1)} %get-tuple-element.55.a0), channel_id=1, source_target_pairs={{0,4},{12,8},{1,5},{13,9},{2,6},{14,10},{3,7},{15,11},{16,20},{28,... | collective-permute-start | bytes 1474568 | tf_op jit(solution)/shard_map/ppermute | solution.py:555
  13.1 21.3 %collective-permute-start.5 = (bf16[960,128]{1,0:T(8,128)(2,1)}, bf16[960,128]{1,0:T(8,128)(2,1)S(1)}, u32[]{:S(2)}, u32[]{:S(2)}) collective-permute-start(bf16[960,128]{1,0:T(8,128)(2,1)} %get-tuple-element.46), channel_id=1, source_target_pairs={{4,8},{8,4},{5,9},{9,5},{6,10},{10,6},{7,11},{11,7},{20,24},{24,20... | collective-permute-start | bytes 737288 | tf_op jit(solution)/shard_map/ppermute | solution.py:555
  13.8 23.3 %collective-permute-start.4 = (bf16[960,128]{1,0:T(8,128)(2,1)}, bf16[960,128]{1,0:T(8,128)(2,1)S(1)}, u32[]{:S(2)}, u32[]{:S(2)}) collective-permute-start(bf16[960,128]{1,0:T(8,128)(2,1)} %get-tuple-element.46), channel_id=1, source_target_pairs={{0,8},{12,4},{1,9},{13,5},{2,10},{14,6},{3,11},{15,7},{16,24},{28,... | collective-permute-start | bytes 737288 | tf_op jit(solution)/shard_map/ppermute | solution.py:555
  17.7 0.7 copy-start
  18.4 0.7 copy-start.3
  19.1 0.7 copy-start.4
  19.7 1.7 %copy-start.2 = (bf16[960,128]{1,0:T(8,128)(2,1)S(1)}, bf16[960,128]{1,0:T(8,128)(2,1)}, u32[]{:S(2)}) copy-start(bf16[960,128]{1,0:T(8,128)(2,1)} %get-tuple-element.45.b0) | copy-start | bytes 737284
  19.7 12.0 %copy-start.1 = (bf16[960,256]{1,0:T(8,128)(2,1)S(1)}, bf16[960,256]{1,0:T(8,128)(2,1)}, u32[]{:S(2)}) copy-start(bf16[960,256]{1,0:T(8,128)(2,1)} %get-tuple-element.55.a0) | copy-start | bytes 1474564
  21.5 19.6 %collective-permute-start.6 = (bf16[960,128]{1,0:T(8,128)(2,1)S(1)}, bf16[960,128]{1,0:T(8,128)(2,1)S(1)}, u32[]{:S(2)}, u32[]{:S(2)}) collective-permute-start(bf16[960,128]{1,0:T(8,128)(2,1)S(1)} %copy-done.2), channel_id=1, source_target_pairs={{0,4},{12,8},{1,5},{13,9},{2,6},{14,10},{3,7},{15,11},{16,20},{28,... | collective-permute-start | bytes 737288 | tf_op jit(solution)/shard_map/ppermute | solution.py:555
  31.8 15.1 %collective-permute-start.9 = (bf16[256,256]{1,0:T(8,128)(2,1)S(1)}, bf16[256,256]{1,0:T(8,128)(2,1)S(1)}, u32[]{:S(2)}, u32[]{:S(2)}) collective-permute-start(bf16[256,256]{1,0:T(8,128)(2,1)S(1)} %get-tuple-element.53), channel_id=1, source_target_pairs={{4,0},{8,12},{5,1},{9,13},{6,2},{10,14},{7,3},{11,15},{20,16},{24,... | collective-permute-start | bytes 393224 | tf_op jit(solution)/shard_map/ppermute | solution.py:555
  33.1 13.8 %collective-permute-start.3 = (bf16[320,256]{1,0:T(8,128)(2,1)S(1)}, bf16[320,256]{1,0:T(8,128)(2,1)S(1)}, u32[]{:S(2)}, u32[]{:S(2)}) collective-permute-start(bf16[320,256]{1,0:T(8,128)(2,1)S(1)} %get-tuple-element.44), channel_id=1, source_target_pairs={{8,0},{4,12},{9,1},{5,13},{10,2},{6,14},{11,3},{7,15},{24,16},{20,... | collective-permute-start | bytes 491528 | tf_op jit(solution)/shard_map/ppermute | solution.py:555
  41.1 9.8 %collective-permute-start.8 = (bf16[320,128]{1,0:T(8,128)(2,1)S(1)}, bf16[320,128]{1,0:T(8,128)(2,1)S(1)}, u32[]{:S(2)}, u32[]{:S(2)}) collective-permute-start(bf16[320,128]{1,0:T(8,128)(2,1)S(1)} %get-tuple-element.51), channel_id=1, source_target_pairs={{8,0},{4,12},{9,1},{5,13},{10,2},{6,14},{11,3},{7,15},{24,16},{20,... | collective-permute-start | bytes 245768 | tf_op jit(solution)/shard_map/ppermute | solution.py:555
  42.4 13.7 %collective-permute-start.7 = (bf16[320,384]{1,0:T(8,128)(2,1)S(1)}, bf16[320,384]{1,0:T(8,128)(2,1)S(1)}, u32[]{:S(2)}, u32[]{:S(2)}) collective-permute-start(bf16[320,384]{1,0:T(8,128)(2,1)S(1)} %get-tuple-element.50), channel_id=1, source_target_pairs={{4,0},{8,12},{5,1},{9,13},{6,2},{10,14},{7,3},{11,15},{20,16},{24,... | collective-permute-start | bytes 737288 | tf_op jit(solution)/shard_map/ppermute | solution.py:555
  46.9 9.2 %slice-start = ((s8[4718592]{0:T(1024)(128)(4,1)}), s8[4194304]{0:T(1024)(128)(4,1)S(1)}, s32[]{:S(2)}) async-start(s8[4718592]{0:T(1024)(128)(4,1)} %bitcast.1), calls=%async_computation | async-start | bytes 8388608
  46.9 9.2 %slice-start.1 = ((s8[4718592]{0:T(1024)(128)(4,1)}), s8[524288]{0:T(1024)(128)(4,1)S(1)}, s32[]{:S(2)}) async-start(s8[4718592]{0:T(1024)(128)(4,1)} %bitcast.1), calls=%async_computation.1 | async-start | bytes 1048576
  46.9 9.2 %collective-permute-start.10 = (bf16[320,384]{1,0:T(8,128)(2,1)S(1)}, bf16[320,384]{1,0:T(8,128)(2,1)S(1)}, u32[]{:S(2)}, u32[]{:S(2)}) collective-permute-start(bf16[320,384]{1,0:T(8,128)(2,1)S(1)} %get-tuple-element.54), channel_id=1, source_target_pairs={{4,8},{8,4},{5,9},{9,5},{6,10},{10,6},{7,11},{11,7},{20,24},{24,20... | collective-permute-start | bytes 737288 | tf_op jit(solution)/shard_map/ppermute | solution.py:555
  56.7 1.9 %collective-permute-start.11 = (bf16[320,768]{1,0:T(8,128)(2,1)S(1)}, bf16[320,768]{1,0:T(8,128)(2,1)S(1)}, u32[]{:S(2)}, u32[]{:S(2)}) collective-permute-start(bf16[320,768]{1,0:T(8,128)(2,1)S(1)} %give_there.1), channel_id=1, source_target_pairs={{0,1},{1,0},{2,3},{3,2},{4,5},{5,4},{6,7},{7,6},{8,9},{9,8},{10,11... | collective-permute-start | bytes 1474568 | tf_op jit(solution)/shard_map/ppermute | solution.py:699
  58.1 6.1 %collective-permute-start.13 = (bf16[320,768]{1,0:T(8,128)(2,1)S(1)}, bf16[320,768]{1,0:T(8,128)(2,1)S(1)}, u32[]{:S(2)}, u32[]{:S(2)}) collective-permute-start(bf16[320,768]{1,0:T(8,128)(2,1)S(1)} %give_here.1), channel_id=1, source_target_pairs={{0,1},{1,0},{2,3},{3,2},{4,5},{5,4},{6,7},{7,6},{8,9},{9,8},{10,11... | collective-permute-start | bytes 1474568 | tf_op jit(solution)/shard_map/ppermute | solution.py:715
  58.7 13.3 %collective-permute-start.12 = (bf16[320,768]{1,0:T(8,128)(2,1)S(1)}, bf16[320,768]{1,0:T(8,128)(2,1)S(1)}, u32[]{:S(2)}, u32[]{:S(2)}) collective-permute-start(bf16[320,768]{1,0:T(8,128)(2,1)S(1)} %add.1), channel_id=1, source_target_pairs={{0,2},{2,0},{1,3},{3,1},{4,6},{6,4},{5,7},{7,5},{8,10},{10,8},{9,1... | collective-permute-start | bytes 1474568 | tf_op jit(solution)/shard_map/ppermute | solution.py:708
  60.3 11.2 %collective-permute-start.15 = (bf16[256,384]{1,0:T(8,128)(2,1)S(1)}, bf16[256,384]{1,0:T(8,128)(2,1)S(1)}, u32[]{:S(2)}, u32[]{:S(2)}) collective-permute-start(bf16[256,384]{1,0:T(8,128)(2,1)S(1)} %get-tuple-element.72), channel_id=1, source_target_pairs={{8,0},{4,12},{9,1},{5,13},{10,2},{6,14},{11,3},{7,15},{24,16},{20,... | collective-permute-start | bytes 589832 | tf_op jit(solution)/shard_map/ppermute | solution.py:555
  61.6 9.9 %collective-permute-start.16 = (bf16[256,384]{1,0:T(8,128)(2,1)S(1)}, bf16[256,384]{1,0:T(8,128)(2,1)S(1)}, u32[]{:S(2)}, u32[]{:S(2)}) collective-permute-start(bf16[256,384]{1,0:T(8,128)(2,1)S(1)} %get-tuple-element.73), channel_id=1, source_target_pairs={{4,8},{8,4},{5,9},{9,5},{6,10},{10,6},{7,11},{11,7},{20,24},{24,20... | collective-permute-start | bytes 589832 | tf_op jit(solution)/shard_map/ppermute | solution.py:555
  62.3 9.2 %collective-permute-start.14 = (bf16[256,128]{1,0:T(8,128)(2,1)S(1)}, bf16[256,128]{1,0:T(8,128)(2,1)S(1)}, u32[]{:S(2)}, u32[]{:S(2)}) collective-permute-start(bf16[256,128]{1,0:T(8,128)(2,1)S(1)} %get-tuple-element.71), channel_id=1, source_target_pairs={{4,0},{8,12},{5,1},{9,13},{6,2},{10,14},{7,3},{11,15},{20,16},{24,... | collective-permute-start | bytes 196616 | tf_op jit(solution)/shard_map/ppermute | solution.py:555

commit v7 on v6

--- a/solution.py
+++ b/solution.py
@@ -224,57 +224,60 @@
 
 
 def pack_kernel(
-    levels, q, k, v, cq, ck, cv, near_a, near_b, far_a, far_b,
+    inner, levels, q, k, v, cq, ck, cv, near_a, near_b, far_a, far_b,
     lv, nk, nv, nq, sk, sv, sq, tk, tv, tq, sems,
 ):
     z = lax.axis_index("seq")
-    devices = lax.axis_size("seq")
-    new_rows, width = q.shape
-    ctx_rows = cq.shape[0]
-    half = width // 2
-    most = near_a.shape[1]
-    rows = new_rows + ctx_rows
-    frames_ctx = levels.shape[0]
-    low = jnp.where(z < devices // 2, 0, half)
-    places = (
-        (far_a, half - low, most),
-        (near_a, low, most),
-        (far_b, half - low + most, half - most),
-        (near_b, low + most, half - most),
-    )
-    places = [(out, pl.ds(pl.multiple_of(at, 128), size)) for out, at, size in places]
-    started = []
-
-    def start(src, dst):
-        copy = pltpu.make_async_copy(src, dst, sems.at[len(started)])
-        copy.start()
-        started.append(copy)
-        return copy
-
-    def send(src, base):
-        for out, lanes in places:
-            start(src.at[:, lanes], out.at[base : base + src.shape[0]])
-
-    reads = [start(levels, lv), start(ck, sk), start(cv, sv), start(cq, sq)]
-    reads += [start(k, nk), start(v, nv), start(q, nq)]
-    reads[0].wait()
-    index = place_index((ctx_rows, 1), 0)
-    first = index % 4 == 0
-    frame = (z * ctx_rows + index) * frames_ctx // (devices * ctx_rows)
-    coarse = coarse_of(frame, lv, frames_ctx)
-    for part, (src, dst) in enumerate(((sk, tk), (sv, tv), (sq, tq))):
-        reads[part + 1].wait()
-        wide = src[...].astype(jnp.float32)
-        pair = wide + pltpu.roll(wide, ctx_rows - 1, 0)
-        quad = pair + pltpu.roll(pair, ctx_rows - 2, 0)
-        mean = jnp.where(first, quad * 0.25, 0.0)
-        dst[...] = jnp.where(coarse, mean, wide).astype(jnp.bfloat16)
-        send(dst, part * rows + new_rows)
-    for part, src in enumerate((nk, nv, nq)):
-        reads[part + 4].wait()
-        send(src, part * rows)
-    for copy in started[7:]:
-        copy.wait()
+
+    @pl.when(middle(z) if inner else jnp.logical_not(middle(z)))
+    def _():
+        devices = lax.axis_size("seq")
+        new_rows, width = q.shape
+        ctx_rows = cq.shape[0]
+        half = width // 2
+        most = near_a.shape[1]
+        rows = new_rows + ctx_rows
+        frames_ctx = levels.shape[0]
+        low = jnp.where(z < devices // 2, 0, half)
+        places = (
+            (far_a, half - low, most),
+            (near_a, low, most),
+            (far_b, half - low + most, half - most),
+            (near_b, low + most, half - most),
+        )
+        places = [(out, pl.ds(pl.multiple_of(at, 128), size)) for out, at, size in places]
+        started = []
+
+        def start(src, dst):
+            copy = pltpu.make_async_copy(src, dst, sems.at[len(started)])
+            copy.start()
+            started.append(copy)
+            return copy
+
+        def send(src, base):
+            for out, lanes in places:
+                start(src.at[:, lanes], out.at[base : base + src.shape[0]])
+
+        reads = [start(levels, lv), start(ck, sk), start(cv, sv), start(cq, sq)]
+        reads += [start(k, nk), start(v, nv), start(q, nq)]
+        reads[0].wait()
+        index = place_index((ctx_rows, 1), 0)
+        first = index % 4 == 0
+        frame = (z * ctx_rows + index) * frames_ctx // (devices * ctx_rows)
+        coarse = coarse_of(frame, lv, frames_ctx)
+        for part, (src, dst) in enumerate(((sk, tk), (sv, tv), (sq, tq))):
+            reads[part + 1].wait()
+            wide = src[...].astype(jnp.float32)
+            pair = wide + pltpu.roll(wide, ctx_rows - 1, 0)
+            quad = pair + pltpu.roll(pair, ctx_rows - 2, 0)
+            mean = jnp.where(first, quad * 0.25, 0.0)
+            dst[...] = jnp.where(coarse, mean, wide).astype(jnp.bfloat16)
+            send(dst, part * rows + new_rows)
+        for part, src in enumerate((nk, nv, nq)):
+            reads[part + 4].wait()
+            send(src, part * rows)
+        for copy in started[7:]:
+            copy.wait()
 
 
 def plan_kernel(owners, levels, masks, order, alive, biases):
@@ -420,7 +423,7 @@
 
 
 def first_kernel(
-    factor, frames_new, a0, a1, a2, a3, order, alive, biases, qn, qc, cn, e3, keys, values
+    factor, frames_new, a0, a3, a2, a1, order, alive, biases, qn, qc, cn, e3, keys, values
 ):
     z = lax.axis_index("seq")
 
@@ -588,28 +591,34 @@
     frames_new = frame_mask.shape[0]
     factor = math.log2(math.e) / math.sqrt(hdim)
     most = max(hdim, half - hdim)
-    near_a, near_b, far_a, far_b = pl.pallas_call(
-        pack_kernel,
-        out_shape=(
-            shape16(3 * rows, most),
-            shape16(3 * rows, half - most),
-            shape16(3 * rows, most),
-            shape16(3 * rows, half - most),
-        ),
-        in_specs=[AWAY] * 7,
-        out_specs=[AWAY] * 4,
-        scratch_shapes=[pltpu.SMEM(levels.shape, jnp.int32)]
-        + [pltpu.VMEM((new_rows, width), jnp.bfloat16)] * 3
-        + [pltpu.VMEM((ctx_rows, width), jnp.bfloat16)] * 6
-        + [pltpu.SemaphoreType.DMA((31,))],
-        name="pack",
-    )(levels, queries, new_keys, new_values, context_queries, context_keys, context_values)
-    beside_a = permute(near_a, BESIDE)
+
+    def pack(inner):
+        return pl.pallas_call(
+            functools.partial(pack_kernel, inner),
+            out_shape=(
+                shape16(3 * rows, most),
+                shape16(3 * rows, half - most),
+                shape16(3 * rows, most),
+                shape16(3 * rows, half - most),
+            ),
+            in_specs=[AWAY] * 7,
+            out_specs=[AWAY] * 4,
+            scratch_shapes=[pltpu.SMEM(levels.shape, jnp.int32)]
+            + [pltpu.VMEM((new_rows, width), jnp.bfloat16)] * 3
+            + [pltpu.VMEM((ctx_rows, width), jnp.bfloat16)] * 6
+            + [pltpu.SemaphoreType.DMA((31,))],
+            name="pack_inner" if inner else "pack_outer",
+            cost_estimate=lasts(2.6),
+        )(levels, queries, new_keys, new_values, context_queries, context_keys, context_values)
+
+    end_near_a, end_near_b, end_far_a, end_far_b = pack(False)
+    near_a, near_b, far_a, far_b = pack(True)
+    beside_a = permute(end_near_a, BESIDE)
     across_a = permute(far_a, ACROSS)
-    beyond_a = permute(far_a, BEYOND)
-    beside_b = permute(near_b, BESIDE)
+    beyond_a = permute(end_far_a, BEYOND)
+    beside_b = permute(end_near_b, BESIDE)
     across_b = permute(far_b, ACROSS)
-    beyond_b = permute(far_b, BEYOND)
+    beyond_b = permute(end_far_b, BEYOND)
     order, alive, biases = pl.pallas_call(
         plan_kernel,
         out_shape=(
@@ -639,7 +648,7 @@
         compiler_params=LIMIT,
         name="attend_first",
         cost_estimate=lasts(4.8),
-    )(near_a, beside_a, across_a, beyond_a, order, alive, biases)
+    )(near_a, beyond_a, across_a, beside_a, order, alive, biases)
     results = pl.pallas_call(
         functools.partial(second_kernel, factor, frames_new),
         out_shape=[

time: 73.4 us -> 72.3 us (0.985)
  starting transfers between devices: 29.7 us -> 24.7 us
  waiting for transfers between devices: 32.4 us -> 37.2 us
  local copies, waits for them, and re-layouts: 2 us -> 0.05 us
    ppermute x14, starting transfers between devices: 27.5 us -> 22.5 us  [permute(): return lax.ppermute(x, 'seq', pairs)]
    ppermute x14, waiting for transfers between devices: 31.7 us -> 36.3 us  [permute(): return lax.ppermute(x, 'seq', pairs)]
    unnamed x14 -> x20, local copies, waits for them, and re-layouts: 2 us -> 0.05 us
    pallas_call x1 -> x2, Pallas kernels: 2.67 us -> 3.02 us  [pack(): pl.pallas_call(functools.partial(pack_kernel, inner), out_shape=(shape16(...]
  transfers between devices with their start and end apart: 17 -> 17, of which waited for: 9 -> 10; matrix products, arithmetic and copies ran while one was open for 0% -> 0% of each run, Pallas kernels for 5% -> 6%
where the time goes in v7:
time: 72.3 us; the launch traced here: 71.3 us
  waiting for transfers between devices  37.2 us (51%)
  starting transfers between devices  24.7 us (34%)
  Pallas kernels  8.43 us (12%)
  between operations  0.94 us (1%)
    ppermute x14, waiting for transfers between devices, permute(): return lax.ppermute(x, 'seq', pairs)  36.3 us
    ppermute x14, starting transfers between devices, permute(): return lax.ppermute(x, 'seq', pairs)  22.5 us
    pallas_call x2, Pallas kernels, pack(): pl.pallas_call(functools.partial(pack_kernel, inner), out_shape=(shape16(...  3.02 us
    pallas_call x4, Pallas kernels, project(): pl.pallas_call(functools.partial(project_kernel, mine, here), out_shape=j...  2.41 us
    pallas_call x1, Pallas kernels, fast_device(): pl.pallas_call(plan_kernel, out_shape=(shape16(ctx_all, ctx_all), jax.Sha...  1.72 us
    ppermute x1, starting transfers between devices, fast_device(): last = lax.ppermute(other, 'tensor', OPPOSITE)  1.57 us
  transfers between devices with their start and end apart: 17, of which 10 were waited for; matrix products, arithmetic and copies ran while one was open for 0% of the time, Pallas kernels for 6%

profile of v7, /device:TPU:0, one launch (start us, length us, event | category | flops | bytes accessed | tf_op | source)
XLA Modules:
  0.0 71.3 jit_solution(3354517654354609445)
XLA Ops:
  0.6 2.7 %pack_outer.1 = (bf16[960,256]{1,0:T(8,128)(2,1)}, bf16[960,128]{1,0:T(8,128)(2,1)}, bf16[960,256]{1,0:T(8,128)(2,1)}, bf16[960,128]{1,0:T(8,128)(2,1)}) custom-call(s32[8]{0:T(128)} %levels.5, bf16[192,768]{1,0:T(8,128)(2,1)} %q.3, bf16[192,768]{1,0:T(8,128)(2,1)} %k.3, bf16[192,768]{1,0:T(8,128)(2,1)} %v.3, bf16[128,768]{1,0:T(8,128)(2,1)} %cq.3, ...), custom_call_target="tpu_custom_call" | custom-call | flops 2860000000 | tf_op jit(solution)/shard_map/pack_outer/pallas_call | solution.py:596
  3.4 3.5 %collective-permute-start = (bf16[960,256]{1,0:T(8,128)(2,1)}, bf16[960,256]{1,0:T(8,128)(2,1)S(1)}, u32[]{:S(2)}, u32[]{:S(2)}) collective-permute-start(bf16[960,256]{1,0:T(8,128)(2,1)} %get-tuple-element.44), channel_id=1, source_target_pairs={{0,8},{12,4},{1,9},{13,5},{2,10},{14,6},{3,11},{15,7},{16,24},{28,... | collective-permute-start | bytes 1474568 | tf_op jit(solution)/shard_map/ppermute | solution.py:558
  6.9 0.0 copy-start.6
  6.9 0.0 copy-start.5
  6.9 0.0 copy-start
  6.9 0.0 copy-start.1
  7.0 0.0 copy-start.2
  7.0 1.5 %collective-permute-start.2 = (bf16[960,256]{1,0:T(8,128)(2,1)}, bf16[960,256]{1,0:T(8,128)(2,1)S(1)}, u32[]{:S(2)}, u32[]{:S(2)}) collective-permute-start(bf16[960,256]{1,0:T(8,128)(2,1)} %get-tuple-element.46), channel_id=1, source_target_pairs={{0,4},{12,8},{1,5},{13,9},{2,6},{14,10},{3,7},{15,11},{16,20},{28,... | collective-permute-start | bytes 1474568 | tf_op jit(solution)/shard_map/ppermute | solution.py:558
  8.4 0.3 pack_inner.1
  8.7 0.0 copy-start.7
  8.7 0.0 copy-start.3
  8.8 0.8 %collective-permute-start.1 = (bf16[960,256]{1,0:T(8,128)(2,1)}, bf16[960,256]{1,0:T(8,128)(2,1)S(1)}, u32[]{:S(2)}, u32[]{:S(2)}) collective-permute-start(bf16[960,256]{1,0:T(8,128)(2,1)} %get-tuple-element.45), channel_id=1, source_target_pairs={{4,8},{8,4},{5,9},{9,5},{6,10},{10,6},{7,11},{11,7},{20,24},{24,20... | collective-permute-start | bytes 1474568 | tf_op jit(solution)/shard_map/ppermute | solution.py:558
  9.6 0.0 copy-done.6
  9.6 5.3 %collective-permute-start.4 = (bf16[960,128]{1,0:T(8,128)(2,1)S(1)}, bf16[960,128]{1,0:T(8,128)(2,1)S(1)}, u32[]{:S(2)}, u32[]{:S(2)}) collective-permute-start(bf16[960,128]{1,0:T(8,128)(2,1)S(1)} %copy-done.6), channel_id=1, source_target_pairs={{0,8},{12,4},{1,9},{13,5},{2,10},{14,6},{3,11},{15,7},{16,24},{28,... | collective-permute-start | bytes 737288 | tf_op jit(solution)/shard_map/ppermute | solution.py:558
  14.9 0.0 copy-done.5
  14.9 1.4 %collective-permute-start.6 = (bf16[960,128]{1,0:T(8,128)(2,1)S(1)}, bf16[960,128]{1,0:T(8,128)(2,1)S(1)}, u32[]{:S(2)}, u32[]{:S(2)}) collective-permute-start(bf16[960,128]{1,0:T(8,128)(2,1)S(1)} %copy-done.5), channel_id=1, source_target_pairs={{0,4},{12,8},{1,5},{13,9},{2,6},{14,10},{3,7},{15,11},{16,20},{28,... | collective-permute-start | bytes 737288 | tf_op jit(solution)/shard_map/ppermute | solution.py:558
  16.3 0.0 copy-done
  16.3 0.0 copy-done.1
  16.4 0.0 copy-done.2
  16.4 1.7 %plan.1 = (bf16[512,512]{1,0:T(8,128)(2,1)S(1)}, f32[512,128]{1,0:T(8,128)S(1)}, f32[8,512]{1,0:T(8,128)S(1)}) custom-call(s32[1,128]{1,0:T(1,128)S(1)} %bitcast.3, s32[8]{0:T(128)S(1)} %copy-done.1, s32[2,8]{1,0:T(2,128)S(1)} %copy-done), custom_call_target="tpu_custom_call" | custom-call | flops 1760000000 | tf_op jit(solution)/shard_map/plan/pallas_call | solution.py:622
  18.1 0.8 %collective-permute-done.a3 = bf16[960,256]{1,0:T(8,128)(2,1)S(1)} collective-permute-done((bf16[960,256]{1,0:T(8,128)(2,1)}, bf16[960,256]{1,0:T(8,128)(2,1)S(1)}, u32[]{:S(2)}, u32[]{:S(2)}) %collective-permute-start) | collective-permute-done | bytes 491552 | tf_op jit(solution)/shard_map/ppermute | solution.py:558
  18.9 0.0 copy-done.7
  18.9 0.7 collective-permute-start.5
  19.5 9.9 %collective-permute-done.2.a1 = bf16[960,256]{1,0:T(8,128)(2,1)S(1)} collective-permute-done((bf16[960,256]{1,0:T(8,128)(2,1)}, bf16[960,256]{1,0:T(8,128)(2,1)S(1)}, u32[]{:S(2)}, u32[]{:S(2)}) %collective-permute-start.2) | collective-permute-done | bytes 491552 | tf_op jit(solution)/shard_map/ppermute | solution.py:558
  29.4 0.0 collective-permute-done.1.a2
  29.4 0.0 copy-done.3
  29.4 0.0 copy-start.4
  29.4 1.4 %collective-permute-start.9 = (bf16[256,256]{1,0:T(8,128)(2,1)S(1)}, bf16[256,256]{1,0:T(8,128)(2,1)S(1)}, u32[]{:S(2)}, u32[]{:S(2)}) collective-permute-start(bf16[256,256]{1,0:T(8,128)(2,1)S(1)} %get-tuple-element.61), channel_id=1, source_target_pairs={{4,0},{8,12},{5,1},{9,13},{6,2},{10,14},{7,3},{11,15},{20,16},{24,... | collective-permute-start | bytes 393224 | tf_op jit(solution)/shard_map/ppermute | solution.py:558
  30.8 1.3 %collective-permute-start.3 = (bf16[320,256]{1,0:T(8,128)(2,1)S(1)}, bf16[320,256]{1,0:T(8,128)(2,1)S(1)}, u32[]{:S(2)}, u32[]{:S(2)}) collective-permute-start(bf16[320,256]{1,0:T(8,128)(2,1)S(1)} %get-tuple-element.50), channel_id=1, source_target_pairs={{8,0},{4,12},{9,1},{5,13},{10,2},{6,14},{11,3},{7,15},{24,16},{20,... | collective-permute-start | bytes 491528 | tf_op jit(solution)/shard_map/ppermute | solution.py:558
  32.1 2.5 %collective-permute-done.4.b3 = bf16[960,128]{1,0:T(8,128)(2,1)S(1)} collective-permute-done((bf16[960,128]{1,0:T(8,128)(2,1)S(1)}, bf16[960,128]{1,0:T(8,128)(2,1)S(1)}, u32[]{:S(2)}, u32[]{:S(2)}) %collective-permute-start.4) | collective-permute-done | bytes 245792 | tf_op jit(solution)/shard_map/ppermute | solution.py:558
  34.6 4.1 %collective-permute-done.6.b1 = bf16[960,128]{1,0:T(8,128)(2,1)S(1)} collective-permute-done((bf16[960,128]{1,0:T(8,128)(2,1)S(1)}, bf16[960,128]{1,0:T(8,128)(2,1)S(1)}, u32[]{:S(2)}, u32[]{:S(2)}) %collective-permute-start.6) | collective-permute-done | bytes 245792 | tf_op jit(solution)/shard_map/ppermute | solution.py:558
  38.7 0.0 collective-permute-done.5.b2
  38.7 0.0 copy-done.4
  38.7 1.3 %collective-permute-start.8 = (bf16[320,128]{1,0:T(8,128)(2,1)S(1)}, bf16[320,128]{1,0:T(8,128)(2,1)S(1)}, u32[]{:S(2)}, u32[]{:S(2)}) collective-permute-start(bf16[320,128]{1,0:T(8,128)(2,1)S(1)} %get-tuple-element.59), channel_id=1, source_target_pairs={{8,0},{4,12},{9,1},{5,13},{10,2},{6,14},{11,3},{7,15},{24,16},{20,... | collective-permute-start | bytes 245768 | tf_op jit(solution)/shard_map/ppermute | solution.py:558
  40.0 1.3 %collective-permute-start.7 = (bf16[320,384]{1,0:T(8,128)(2,1)S(1)}, bf16[320,384]{1,0:T(8,128)(2,1)S(1)}, u32[]{:S(2)}, u32[]{:S(2)}) collective-permute-start(bf16[320,384]{1,0:T(8,128)(2,1)S(1)} %get-tuple-element.58), channel_id=1, source_target_pairs={{4,0},{8,12},{5,1},{9,13},{6,2},{10,14},{7,3},{11,15},{20,16},{24,... | collective-permute-start | bytes 737288 | tf_op jit(solution)/shard_map/ppermute | solution.py:558
  41.3 4.6 %collective-permute-done.9.cn = bf16[256,256]{1,0:T(8,128)(2,1)S(1)} collective-permute-done((bf16[256,256]{1,0:T(8,128)(2,1)S(1)}, bf16[256,256]{1,0:T(8,128)(2,1)S(1)}, u32[]{:S(2)}, u32[]{:S(2)}) %collective-permute-start.9) | collective-permute-done | bytes 131104 | tf_op jit(solution)/shard_map/ppermute | solution.py:558
  45.9 0.0 collective-permute-done.3.e3
  45.9 0.0 slice-start
  45.9 0.0 slice-start.1
  45.9 0.8 %collective-permute-start.10 = (bf16[320,384]{1,0:T(8,128)(2,1)S(1)}, bf16[320,384]{1,0:T(8,128)(2,1)S(1)}, u32[]{:S(2)}, u32[]{:S(2)}) collective-permute-start(bf16[320,384]{1,0:T(8,128)(2,1)S(1)} %get-tuple-element.62), channel_id=1, source_target_pairs={{4,8},{8,4},{5,9},{9,5},{6,10},{10,6},{7,11},{11,7},{20,24},{24,20... | collective-permute-start | bytes 737288 | tf_op jit(solution)/shard_map/ppermute | solution.py:558
  46.7 0.2 caches.1
  47.0 2.1 %collective-permute-done.8.n3 = bf16[320,128]{1,0:T(8,128)(2,1)S(1)} collective-permute-done((bf16[320,128]{1,0:T(8,128)(2,1)S(1)}, bf16[320,128]{1,0:T(8,128)(2,1)S(1)}, u32[]{:S(2)}, u32[]{:S(2)}) %collective-permute-start.8) | collective-permute-done | bytes 81952 | tf_op jit(solution)/shard_map/ppermute | solution.py:558
  49.1 5.2 %collective-permute-done.7.o1 = bf16[320,384]{1,0:T(8,128)(2,1)S(1)} collective-permute-done((bf16[320,384]{1,0:T(8,128)(2,1)S(1)}, bf16[320,384]{1,0:T(8,128)(2,1)S(1)}, u32[]{:S(2)}, u32[]{:S(2)}) %collective-permute-start.7) | collective-permute-done | bytes 245792 | tf_op jit(solution)/shard_map/ppermute | solution.py:558
  54.3 0.0 collective-permute-done.10.o2
  54.3 0.0 slice-done
  54.3 0.0 slice-done.1
  54.3 0.6 give_there.1
  54.9 0.1 collective-permute-start.11
  55.0 0.6 keep_there.1.keep
  55.6 0.6 give_here.1
  56.3 0.5 collective-permute-start.13
  56.8 0.1 collective-permute-done.11.came
  56.9 0.1 add.1
  57.0 1.6 %collective-permute-start.12 = (bf16[320,768]{1,0:T(8,128)(2,1)S(1)}, bf16[320,768]{1,0:T(8,128)(2,1)S(1)}, u32[]{:S(2)}, u32[]{:S(2)}) collective-permute-start(bf16[320,768]{1,0:T(8,128)(2,1)S(1)} %add.1), channel_id=1, source_target_pairs={{0,2},{2,0},{1,3},{3,1},{4,6},{6,4},{5,7},{7,5},{8,10},{10,8},{9,1... | collective-permute-start | bytes 1474568 | tf_op jit(solution)/shard_map/ppermute | solution.py:717
  58.5 1.3 %collective-permute-start.15 = (bf16[256,384]{1,0:T(8,128)(2,1)S(1)}, bf16[256,384]{1,0:T(8,128)(2,1)S(1)}, u32[]{:S(2)}, u32[]{:S(2)}) collective-permute-start(bf16[256,384]{1,0:T(8,128)(2,1)S(1)} %get-tuple-element.80), channel_id=1, source_target_pairs={{8,0},{4,12},{9,1},{5,13},{10,2},{6,14},{11,3},{7,15},{24,16},{20,... | collective-permute-start | bytes 589832 | tf_op jit(solution)/shard_map/ppermute | solution.py:558
  59.8 0.7 collective-permute-start.16
  60.5 1.3 %collective-permute-start.14 = (bf16[256,128]{1,0:T(8,128)(2,1)S(1)}, bf16[256,128]{1,0:T(8,128)(2,1)S(1)}, u32[]{:S(2)}, u32[]{:S(2)}) collective-permute-start(bf16[256,128]{1,0:T(8,128)(2,1)S(1)} %get-tuple-element.79), channel_id=1, source_target_pairs={{4,0},{8,12},{5,1},{9,13},{6,2},{10,14},{7,3},{11,15},{20,16},{24,... | collective-permute-start | bytes 196616 | tf_op jit(solution)/shard_map/ppermute | solution.py:558
  61.8 0.6 keep_here.1.keep
  62.4 0.0 collective-permute-done.13.came
  62.4 7.1 %collective-permute-done.14.cl = bf16[256,128]{1,0:T(8,128)(2,1)S(1)} collective-permute-done((bf16[256,128]{1,0:T(8,128)(2,1)S(1)}, bf16[256,128]{1,0:T(8,128)(2,1)S(1)}, u32[]{:S(2)}, u32[]{:S(2)}) %collective-permute-start.14) | collective-permute-done | bytes 65568 | tf_op jit(solution)/shard_map/ppermute | solution.py:558
  69.5 0.0 collective-permute-done.15.c3
  69.5 0.0 collective-permute-done.16.c2
  69.5 0.8 %collective-permute-done.12.last = bf16[320,768]{1,0:T(8,128)(2,1)S(1)} collective-permute-done((bf16[320,768]{1,0:T(8,128)(2,1)S(1)}, bf16[320,768]{1,0:T(8,128)(2,1)S(1)}, u32[]{:S(2)}, u32[]{:S(2)}) %collective-permute-start.12) | collective-permute-done | bytes 491552 | tf_op jit(solution)/shard_map/ppermute | solution.py:717
  70.3 1.0 %finish.1 = (bf16[192,768]{1,0:T(8,128)(2,1)}, bf16[128,768]{1,0:T(8,128)(2,1)}, bf16[128,768]{1,0:T(8,128)(2,1)}, bf16[128,768]{1,0:T(8,128)(2,1)}) custom-call(bf16[320,768]{1,0:T(8,128)(2,1)S(1)} %collective-permute-done.12.last, f32[320,768]{1,0:T(8,128)S(1)} %keep_here.1.keep, bf16[320,768]{1,0:T(8,128)(2,1)S(1)} %collective-permute-done.13.came, ...), custom_call_target="tpu_custom_call" | custom-call | flops 1100000000 | tf_op jit(solution)/shard_map/finish/pallas_call | solution.py:726
  (3 shorter events, 0.0 us)
Async XLA Ops:
  3.4 15.5 %collective-permute-start = (bf16[960,256]{1,0:T(8,128)(2,1)}, bf16[960,256]{1,0:T(8,128)(2,1)S(1)}, u32[]{:S(2)}, u32[]{:S(2)}) collective-permute-start(bf16[960,256]{1,0:T(8,128)(2,1)} %get-tuple-element.44), channel_id=1, source_target_pairs={{0,8},{12,4},{1,9},{13,5},{2,10},{14,6},{3,11},{15,7},{16,24},{28,... | collective-permute-start | bytes 1474568 | tf_op jit(solution)/shard_map/ppermute | solution.py:558
  6.9 2.7 %copy-start.6 = (bf16[960,128]{1,0:T(8,128)(2,1)S(1)}, bf16[960,128]{1,0:T(8,128)(2,1)}, u32[]{:S(2)}) copy-start(bf16[960,128]{1,0:T(8,128)(2,1)} %get-tuple-element.52) | copy-start | bytes 737284
  6.9 8.0 %copy-start.5 = (bf16[960,128]{1,0:T(8,128)(2,1)S(1)}, bf16[960,128]{1,0:T(8,128)(2,1)}, u32[]{:S(2)}) copy-start(bf16[960,128]{1,0:T(8,128)(2,1)} %get-tuple-element.54) | copy-start | bytes 737284
  6.9 9.4 %copy-start = (s32[2,8]{1,0:T(2,128)S(1)}, s32[2,8]{1,0:T(2,128)}, u32[]{:S(2)}) copy-start(s32[2,8]{1,0:T(2,128)} %masks.1) | copy-start | bytes 196
  6.9 9.4 %copy-start.1 = (s32[8]{0:T(128)S(1)}, s32[8]{0:T(128)}, u32[]{:S(2)}) copy-start(s32[8]{0:T(128)} %levels.5) | copy-start | bytes 100
  7.0 9.4 %copy-start.2 = (s32[128]{0:T(128)S(1)}, s32[128]{0:T(128)}, u32[]{:S(2)}) copy-start(s32[128]{0:T(128)} %param.18) | copy-start | bytes 1540
  7.0 22.4 %collective-permute-start.2 = (bf16[960,256]{1,0:T(8,128)(2,1)}, bf16[960,256]{1,0:T(8,128)(2,1)S(1)}, u32[]{:S(2)}, u32[]{:S(2)}) collective-permute-start(bf16[960,256]{1,0:T(8,128)(2,1)} %get-tuple-element.46), channel_id=1, source_target_pairs={{0,4},{12,8},{1,5},{13,9},{2,6},{14,10},{3,7},{15,11},{16,20},{28,... | collective-permute-start | bytes 1474568 | tf_op jit(solution)/shard_map/ppermute | solution.py:558
  8.7 10.1 %copy-start.7 = (bf16[960,128]{1,0:T(8,128)(2,1)S(1)}, bf16[960,128]{1,0:T(8,128)(2,1)}, u32[]{:S(2)}) copy-start(bf16[960,128]{1,0:T(8,128)(2,1)} %get-tuple-element.53) | copy-start | bytes 737284
  8.7 20.6 %copy-start.3 = (bf16[960,256]{1,0:T(8,128)(2,1)S(1)}, bf16[960,256]{1,0:T(8,128)(2,1)}, u32[]{:S(2)}) copy-start(bf16[960,256]{1,0:T(8,128)(2,1)} %get-tuple-element.63.a0) | copy-start | bytes 1474564
  8.8 20.6 %collective-permute-start.1 = (bf16[960,256]{1,0:T(8,128)(2,1)}, bf16[960,256]{1,0:T(8,128)(2,1)S(1)}, u32[]{:S(2)}, u32[]{:S(2)}) collective-permute-start(bf16[960,256]{1,0:T(8,128)(2,1)} %get-tuple-element.45), channel_id=1, source_target_pairs={{4,8},{8,4},{5,9},{9,5},{6,10},{10,6},{7,11},{11,7},{20,24},{24,20... | collective-permute-start | bytes 1474568 | tf_op jit(solution)/shard_map/ppermute | solution.py:558
  9.6 25.0 %collective-permute-start.4 = (bf16[960,128]{1,0:T(8,128)(2,1)S(1)}, bf16[960,128]{1,0:T(8,128)(2,1)S(1)}, u32[]{:S(2)}, u32[]{:S(2)}) collective-permute-start(bf16[960,128]{1,0:T(8,128)(2,1)S(1)} %copy-done.6), channel_id=1, source_target_pairs={{0,8},{12,4},{1,9},{13,5},{2,10},{14,6},{3,11},{15,7},{16,24},{28,... | collective-permute-start | bytes 737288 | tf_op jit(solution)/shard_map/ppermute | solution.py:558
  14.9 23.8 %collective-permute-start.6 = (bf16[960,128]{1,0:T(8,128)(2,1)S(1)}, bf16[960,128]{1,0:T(8,128)(2,1)S(1)}, u32[]{:S(2)}, u32[]{:S(2)}) collective-permute-start(bf16[960,128]{1,0:T(8,128)(2,1)S(1)} %copy-done.5), channel_id=1, source_target_pairs={{0,4},{12,8},{1,5},{13,9},{2,6},{14,10},{3,7},{15,11},{16,20},{28,... | collective-permute-start | bytes 737288 | tf_op jit(solution)/shard_map/ppermute | solution.py:558
  18.9 19.9 %collective-permute-start.5 = (bf16[960,128]{1,0:T(8,128)(2,1)S(1)}, bf16[960,128]{1,0:T(8,128)(2,1)S(1)}, u32[]{:S(2)}, u32[]{:S(2)}) collective-permute-start(bf16[960,128]{1,0:T(8,128)(2,1)S(1)} %copy-done.7), channel_id=1, source_target_pairs={{4,8},{8,4},{5,9},{9,5},{6,10},{10,6},{7,11},{11,7},{20,24},{24,20... | collective-permute-start | bytes 737288 | tf_op jit(solution)/shard_map/ppermute | solution.py:558
  29.4 9.3 %copy-start.4 = (bf16[960,128]{1,0:T(8,128)(2,1)S(1)}, bf16[960,128]{1,0:T(8,128)(2,1)}, u32[]{:S(2)}) copy-start(bf16[960,128]{1,0:T(8,128)(2,1)} %get-tuple-element.51.b0) | copy-start | bytes 737284
  29.4 16.5 %collective-permute-start.9 = (bf16[256,256]{1,0:T(8,128)(2,1)S(1)}, bf16[256,256]{1,0:T(8,128)(2,1)S(1)}, u32[]{:S(2)}, u32[]{:S(2)}) collective-permute-start(bf16[256,256]{1,0:T(8,128)(2,1)S(1)} %get-tuple-element.61), channel_id=1, source_target_pairs={{4,0},{8,12},{5,1},{9,13},{6,2},{10,14},{7,3},{11,15},{20,16},{24,... | collective-permute-start | bytes 393224 | tf_op jit(solution)/shard_map/ppermute | solution.py:558
  30.8 15.1 %collective-permute-start.3 = (bf16[320,256]{1,0:T(8,128)(2,1)S(1)}, bf16[320,256]{1,0:T(8,128)(2,1)S(1)}, u32[]{:S(2)}, u32[]{:S(2)}) collective-permute-start(bf16[320,256]{1,0:T(8,128)(2,1)S(1)} %get-tuple-element.50), channel_id=1, source_target_pairs={{8,0},{4,12},{9,1},{5,13},{10,2},{6,14},{11,3},{7,15},{24,16},{20,... | collective-permute-start | bytes 491528 | tf_op jit(solution)/shard_map/ppermute | solution.py:558
  38.7 10.4 %collective-permute-start.8 = (bf16[320,128]{1,0:T(8,128)(2,1)S(1)}, bf16[320,128]{1,0:T(8,128)(2,1)S(1)}, u32[]{:S(2)}, u32[]{:S(2)}) collective-permute-start(bf16[320,128]{1,0:T(8,128)(2,1)S(1)} %get-tuple-element.59), channel_id=1, source_target_pairs={{8,0},{4,12},{9,1},{5,13},{10,2},{6,14},{11,3},{7,15},{24,16},{20,... | collective-permute-start | bytes 245768 | tf_op jit(solution)/shard_map/ppermute | solution.py:558
  40.0 14.3 %collective-permute-start.7 = (bf16[320,384]{1,0:T(8,128)(2,1)S(1)}, bf16[320,384]{1,0:T(8,128)(2,1)S(1)}, u32[]{:S(2)}, u32[]{:S(2)}) collective-permute-start(bf16[320,384]{1,0:T(8,128)(2,1)S(1)} %get-tuple-element.58), channel_id=1, source_target_pairs={{4,0},{8,12},{5,1},{9,13},{6,2},{10,14},{7,3},{11,15},{20,16},{24,... | collective-permute-start | bytes 737288 | tf_op jit(solution)/shard_map/ppermute | solution.py:558
  45.9 8.4 %slice-start = ((s8[4718592]{0:T(1024)(128)(4,1)}), s8[4194304]{0:T(1024)(128)(4,1)S(1)}, s32[]{:S(2)}) async-start(s8[4718592]{0:T(1024)(128)(4,1)} %bitcast.1), calls=%async_computation | async-start | bytes 8388608
  45.9 8.4 %slice-start.1 = ((s8[4718592]{0:T(1024)(128)(4,1)}), s8[524288]{0:T(1024)(128)(4,1)S(1)}, s32[]{:S(2)}) async-start(s8[4718592]{0:T(1024)(128)(4,1)} %bitcast.1), calls=%async_computation.1 | async-start | bytes 1048576
  45.9 8.4 %collective-permute-start.10 = (bf16[320,384]{1,0:T(8,128)(2,1)S(1)}, bf16[320,384]{1,0:T(8,128)(2,1)S(1)}, u32[]{:S(2)}, u32[]{:S(2)}) collective-permute-start(bf16[320,384]{1,0:T(8,128)(2,1)S(1)} %get-tuple-element.62), channel_id=1, source_target_pairs={{4,8},{8,4},{5,9},{9,5},{6,10},{10,6},{7,11},{11,7},{20,24},{24,20... | collective-permute-start | bytes 737288 | tf_op jit(solution)/shard_map/ppermute | solution.py:558
  54.9 1.9 %collective-permute-start.11 = (bf16[320,768]{1,0:T(8,128)(2,1)S(1)}, bf16[320,768]{1,0:T(8,128)(2,1)S(1)}, u32[]{:S(2)}, u32[]{:S(2)}) collective-permute-start(bf16[320,768]{1,0:T(8,128)(2,1)S(1)} %give_there.1), channel_id=1, source_target_pairs={{0,1},{1,0},{2,3},{3,2},{4,5},{5,4},{6,7},{7,6},{8,9},{9,8},{10,11... | collective-permute-start | bytes 1474568 | tf_op jit(solution)/shard_map/ppermute | solution.py:708
  56.3 6.1 %collective-permute-start.13 = (bf16[320,768]{1,0:T(8,128)(2,1)S(1)}, bf16[320,768]{1,0:T(8,128)(2,1)S(1)}, u32[]{:S(2)}, u32[]{:S(2)}) collective-permute-start(bf16[320,768]{1,0:T(8,128)(2,1)S(1)} %give_here.1), channel_id=1, source_target_pairs={{0,1},{1,0},{2,3},{3,2},{4,5},{5,4},{6,7},{7,6},{8,9},{9,8},{10,11... | collective-permute-start | bytes 1474568 | tf_op jit(solution)/shard_map/ppermute | solution.py:724
  57.0 13.3 %collective-permute-start.12 = (bf16[320,768]{1,0:T(8,128)(2,1)S(1)}, bf16[320,768]{1,0:T(8,128)(2,1)S(1)}, u32[]{:S(2)}, u32[]{:S(2)}) collective-permute-start(bf16[320,768]{1,0:T(8,128)(2,1)S(1)} %add.1), channel_id=1, source_target_pairs={{0,2},{2,0},{1,3},{3,1},{4,6},{6,4},{5,7},{7,5},{8,10},{10,8},{9,1... | collective-permute-start | bytes 1474568 | tf_op jit(solution)/shard_map/ppermute | solution.py:717
  58.5 11.0 %collective-permute-start.15 = (bf16[256,384]{1,0:T(8,128)(2,1)S(1)}, bf16[256,384]{1,0:T(8,128)(2,1)S(1)}, u32[]{:S(2)}, u32[]{:S(2)}) collective-permute-start(bf16[256,384]{1,0:T(8,128)(2,1)S(1)} %get-tuple-element.80), channel_id=1, source_target_pairs={{8,0},{4,12},{9,1},{5,13},{10,2},{6,14},{11,3},{7,15},{24,16},{20,... | collective-permute-start | bytes 589832 | tf_op jit(solution)/shard_map/ppermute | solution.py:558
  59.8 9.7 %collective-permute-start.16 = (bf16[256,384]{1,0:T(8,128)(2,1)S(1)}, bf16[256,384]{1,0:T(8,128)(2,1)S(1)}, u32[]{:S(2)}, u32[]{:S(2)}) collective-permute-start(bf16[256,384]{1,0:T(8,128)(2,1)S(1)} %get-tuple-element.81), channel_id=1, source_target_pairs={{4,8},{8,4},{5,9},{9,5},{6,10},{10,6},{7,11},{11,7},{20,24},{24,20... | collective-permute-start | bytes 589832 | tf_op jit(solution)/shard_map/ppermute | solution.py:558
  60.5 9.0 %collective-permute-start.14 = (bf16[256,128]{1,0:T(8,128)(2,1)S(1)}, bf16[256,128]{1,0:T(8,128)(2,1)S(1)}, u32[]{:S(2)}, u32[]{:S(2)}) collective-permute-start(bf16[256,128]{1,0:T(8,128)(2,1)S(1)} %get-tuple-element.79), channel_id=1, source_target_pairs={{4,0},{8,12},{5,1},{9,13},{6,2},{10,14},{7,3},{11,15},{20,16},{24,... | collective-permute-start | bytes 196616 | tf_op jit(solution)/shard_map/ppermute | solution.py:558
